TPU v7x, 32 devices: a whole 2x2x4 slice. The times are simulated.
32 devices in a mesh: groups: 2 (over x), ep: 16 (over z, y, core).
Axes of the slice: x: 2, y: 2, z: 4, core: 2. Of those that a mesh axis runs over, the one named last changes fastest.
Arguments:
- hidden: bfloat16 [2, 128, 7168], P(None, ('groups', 'ep')), parts along dimension 1, may hold values from -6 to 6
- expert_ids: int32 [2, 128, 2], P(None, ('groups', 'ep')), parts along dimension 1, may hold values from 0 to 3, all different within a row; in each aligned block of 4 rows (0 to 3, 4 to 7, ..., all dimensions but the last counted through in order) at most 4 rows name the same one
- route_weight: float32 [2, 128, 2], P(None, ('groups', 'ep')), parts along dimension 1, may hold values from 0.1 to 1
- w_gate: bfloat16 [16, 7168, 256], P('ep'), may hold values from -0.0625 to 0.0625
- w_up: bfloat16 [16, 7168, 256], P('ep'), may hold values from -0.0625 to 0.0625
- w_down: bfloat16 [16, 256, 7168], P('ep'), may hold values from -0.1875 to 0.1875
Outputs:
- moe_output: bfloat16 [2, 128, 7168], P(None, ('groups', 'ep')), parts along dimension 1
There are 2 independent parts, one for each index of `groups`. A program takes and returns all parts, laid end to end along the dimension named above; an argument that names none is the same for every part. Nothing has to cross between parts.
Inputs may be any that keep to these rules, and one draw needn't show every extreme that they name: `expert_ids`: each row names 2 different experts; in one step, the 4 rows of one device name no expert more than 4 times, and in some devices' rows an expert is named exactly 4 times.
All inputs are finite; a program needn't handle non-finite values.
Results may differ from a plain program's by a relative error of at most 0.0064.
Values may be sent and summed in bfloat16 or wider, within the bound.
No kernel may reach another device: no remote copies, remote signals or barrier semaphores. Data moves between devices by JAX's collectives and lax.ppermute only.
A program may use at most 128 MiB of HBM per device.

v0:
```python
import jax
import jax.numpy as jnp
from jax import lax
from jax.sharding import PartitionSpec as P

FF = 1024


route_scale = 2.5


def expert_slice(rows, gate_w, up_w, down_w):
    gate_pre = jnp.dot(rows, gate_w, preferred_element_type=jnp.float32)
    up_pre = jnp.dot(rows, up_w, preferred_element_type=jnp.float32)
    slice_hidden = (jax.nn.silu(gate_pre) * up_pre).astype(jnp.bfloat16)
    return jnp.dot(slice_hidden, down_w, preferred_element_type=jnp.float32).astype(jnp.bfloat16)


def route_targets(ids, capacity, experts):
    row_count, top_count = ids.shape
    flat_ids = ids.reshape(-1)
    onehot = (flat_ids[:, None] == jnp.arange(experts, dtype=jnp.int32)[None, :]).astype(jnp.int32)
    slot_rank = jnp.sum((jnp.cumsum(onehot, axis=0) - 1) * onehot, axis=1)
    return (flat_ids * capacity + slot_rank).reshape(row_count, top_count)


def pack_rows(rows_now, targets, slot_total):
    positions = jnp.arange(slot_total, dtype=jnp.int32)
    chosen = jnp.any(positions[:, None, None] == targets[None, :, :], axis=-1).astype(jnp.bfloat16)
    return jnp.dot(chosen, rows_now, preferred_element_type=jnp.float32).astype(jnp.bfloat16)


def local(hidden, expert_ids, route_weight, w_gate, w_up, w_down):
    step_count, token_count, features = hidden.shape
    top_count = expert_ids.shape[-1]
    slice_units = w_gate.shape[-1]
    splits = FF // slice_units
    devices = lax.axis_size("ep")
    experts = devices // splits
    capacity = max(2, 2 * token_count * top_count // experts)
    gate_w = w_gate[0]
    up_w = w_up[0]
    down_w = w_down[0]

    def compute(received_rows):
        flat_rows = received_rows.reshape(-1, features)
        partial_value = expert_slice(flat_rows, gate_w, up_w, down_w)
        return partial_value.reshape(received_rows.shape[:-1] + (features,))

    def direct_work(received):
        partial_value = compute(received)
        return lax.all_to_all(partial_value, "ep", split_axis=0, concat_axis=0, tiled=True)

    def travel(rows_out):
        return direct_work(lax.all_to_all(rows_out, "ep", split_axis=0, concat_axis=0, tiled=True))

    prepared = []
    for step_index in range(step_count):
        targets = route_targets(expert_ids[step_index], capacity, experts)
        packed = pack_rows(hidden[step_index], targets, experts * capacity)
        prepared.append(
            (
                targets,
                jnp.broadcast_to(
                    packed.reshape(experts, 1, capacity, features),
                    (experts, splits, capacity, features),
                ).reshape(devices, capacity, features),
            )
        )
    returned = [travel(prepared[step_index][1]) for step_index in range(step_count)]
    results = []
    for step_index in range(step_count):
        summed = jnp.sum(
            returned[step_index].reshape(experts, splits, capacity, features).astype(jnp.float32),
            axis=1,
        )
        expert_rows = summed.astype(jnp.bfloat16).reshape(experts * capacity, features)
        weights = route_weight[step_index]
        picked = (
            jnp.take(expert_rows, prepared[step_index][0].reshape(-1), axis=0)
            .reshape(token_count, top_count, features)
            .astype(jnp.float32)
        )
        mix_weight = route_scale * weights / jnp.sum(weights, axis=-1, keepdims=True)
        results.append(jnp.sum(picked * mix_weight[..., None], axis=1).astype(jnp.bfloat16))
    return jnp.stack(results, 0)


def solution(mesh):
    placed = (
        P(None, ("groups", "ep"), None),
        P(None, ("groups", "ep"), None),
        P(None, ("groups", "ep"), None),
        P("ep", None, None),
        P("ep", None, None),
        P("ep", None, None),
    )
    return jax.shard_map(
        local,
        mesh=mesh,
        in_specs=placed,
        out_specs=P(None, ("groups", "ep"), None),
        check_vma=False,
    )
```

profile of v0, /device:TPU:0, one launch (start us, length us, event | category | flops | bytes accessed | tf_op | source)
XLA Modules:
  0.0 117.2 jit_solution(4847603529439202070)
XLA Ops:
  0.0 0.7 fusion.48
  0.7 0.1 copy.29
  0.8 0.1 eq.61
  0.9 0.2 reduce_window_sum.17
  1.1 0.1 reduce_sum.83
  1.2 0.1 copy.24
  1.3 0.1 fusion.42
  1.4 1.1 convolution_convert_fusion.3
  2.5 0.1 broadcast_in_dim.17
  2.6 1.2 %broadcast_in_dim.18 = bf16[4,4,4,7168]{3,2,1,0:T(4,128)(2,1)} broadcast(bf16[4,4,7168]{2,1,0:T(4,128)(2,1)S(1)} %broadcast_in_dim.17), dimensions={0,2,3} | broadcast | bytes 1146880 | tf_op jit(solution)/shard_map/broadcast_in_dim | solution.py:64
  3.8 7.4 %all-to-all-start = ((bf16[16,4,7168]{2,1,0:T(4,128)(2,1)}), bf16[16,4,7168]{2,1,0:T(4,128)(2,1)S(1)}, u32[]{:S(2)}, u32[]{:S(2)}) async-start(bf16[16,4,7168]{2,1,0:T(4,128)(2,1)} %bitcast.2), calls=%async_computation | async-start | bytes 1835008 | tf_op jit(solution)/shard_map/all_to_all | solution.py:55
  11.2 0.1 copy.30
  11.3 0.1 eq.69
  11.4 0.2 reduce_window_sum.18
  11.6 0.1 reduce_sum.88
  11.7 0.1 copy.27
  11.8 0.1 fusion.43
  11.8 0.3 convolution_convert_fusion.2
  12.1 0.1 broadcast_in_dim.19
  12.2 19.8 %all-to-all-done = bf16[16,4,7168]{2,1,0:T(4,128)(2,1)S(1)} async-done(((bf16[16,4,7168]{2,1,0:T(4,128)(2,1)}), bf16[16,4,7168]{2,1,0:T(4,128)(2,1)S(1)}, u32[]{:S(2)}, u32[]{:S(2)}) %all-to-all-start) | async-done | bytes 917536 | tf_op jit(solution)/shard_map/all_to_all | solution.py:55
  32.0 1.2 %broadcast_in_dim.34 = bf16[4,4,4,7168]{3,2,1,0:T(4,128)(2,1)} broadcast(bf16[4,4,7168]{2,1,0:T(4,128)(2,1)S(1)} %broadcast_in_dim.19), dimensions={0,2,3} | broadcast | bytes 1146880 | tf_op jit(solution)/shard_map/broadcast_in_dim | solution.py:64
  33.2 6.2 %all-to-all-start.2 = ((bf16[16,4,7168]{2,1,0:T(4,128)(2,1)}), bf16[16,4,7168]{2,1,0:T(4,128)(2,1)S(1)}, u32[]{:S(2)}, u32[]{:S(2)}) async-start(bf16[16,4,7168]{2,1,0:T(4,128)(2,1)} %bitcast.11), calls=%async_computation.2 | async-start | bytes 1835008 | tf_op jit(solution)/shard_map/all_to_all | solution.py:55
  39.4 0.2 reshape.112
  39.6 2.8 %fusion.8 = f32[64,256]{1,0:T(8,128)S(1)} fusion(bf16[64,7168]{1,0:T(8,128)(2,1)S(1)} %reshape.112, bf16[1,7168,256]{2,1,0:T(8,128)(2,1)} %param.11), kind=kOutput, calls=%fused_computation.14 | convolution fusion | flops 234881024 | bytes 4653056 | tf_op jit(solution)/shard_map/dot_general | solution.py:13
  42.4 5.5 %convolution_convert_fusion.1 = bf16[64,7168]{1,0:T(8,128)(2,1)S(1)} fusion(bf16[1,256,7168]{2,1,0:T(8,128)(2,1)} %param.13, bf16[64,7168]{1,0:T(8,128)(2,1)S(1)} %reshape.112, bf16[1,7168,256]{2,1,0:T(8,128)(2,1)} %param.12, f32[64,256]{1,0:T(8,128)S(1)} %fusion.8), kind=kOutput, calls=%fused_computation.3 | convolution fusion | flops 470319104 | bytes 9240576 | tf_op jit(solution)/shard_map/dot_general | solution.py:16
  47.9 1.3 %reshape.113 = bf16[16,4,7168]{2,1,0:T(4,128)(2,1)} reshape(bf16[64,7168]{1,0:T(8,128)(2,1)S(1)} %convolution_convert_fusion.1) | data formatting | bytes 1835008 | tf_op jit(solution)/shard_map/reshape | solution.py:48
  49.1 11.1 %all-to-all-done.2 = bf16[16,4,7168]{2,1,0:T(4,128)(2,1)S(1)} async-done(((bf16[16,4,7168]{2,1,0:T(4,128)(2,1)}), bf16[16,4,7168]{2,1,0:T(4,128)(2,1)S(1)}, u32[]{:S(2)}, u32[]{:S(2)}) %all-to-all-start.2) | async-done | bytes 917536 | tf_op jit(solution)/shard_map/all_to_all | solution.py:55
  60.2 6.2 %all-to-all-start.1 = ((bf16[16,4,7168]{2,1,0:T(4,128)(2,1)}), bf16[16,4,7168]{2,1,0:T(4,128)(2,1)}, u32[]{:S(2)}, u32[]{:S(2)}) async-start(bf16[16,4,7168]{2,1,0:T(4,128)(2,1)} %reshape.113), calls=%async_computation.1 | async-start | bytes 1835008 | tf_op jit(solution)/shard_map/all_to_all | solution.py:52
  66.5 0.1 copy.25
  66.6 0.1 copy.28
  66.7 0.2 reshape.117
  66.9 2.8 %fusion.6 = f32[64,256]{1,0:T(8,128)S(1)} fusion(bf16[64,7168]{1,0:T(8,128)(2,1)S(1)} %reshape.117, bf16[1,7168,256]{2,1,0:T(8,128)(2,1)} %param.11), kind=kOutput, calls=%fused_computation.12 | convolution fusion | flops 234881024 | bytes 4653056 | tf_op jit(solution)/shard_map/dot_general | solution.py:13
  69.7 5.5 %convolution_convert_fusion = bf16[64,7168]{1,0:T(8,128)(2,1)S(1)} fusion(bf16[1,256,7168]{2,1,0:T(8,128)(2,1)} %param.13, bf16[64,7168]{1,0:T(8,128)(2,1)S(1)} %reshape.117, bf16[1,7168,256]{2,1,0:T(8,128)(2,1)} %param.12, f32[64,256]{1,0:T(8,128)S(1)} %fusion.6), kind=kOutput, calls=%fused_computation.2 | convolution fusion | flops 470319104 | bytes 9240576 | tf_op jit(solution)/shard_map/dot_general | solution.py:16
  75.1 1.3 %reshape.118 = bf16[16,4,7168]{2,1,0:T(4,128)(2,1)} reshape(bf16[64,7168]{1,0:T(8,128)(2,1)S(1)} %convolution_convert_fusion) | data formatting | bytes 1835008 | tf_op jit(solution)/shard_map/reshape | solution.py:48
  76.4 10.9 %all-to-all-done.1 = bf16[16,4,7168]{2,1,0:T(4,128)(2,1)} async-done(((bf16[16,4,7168]{2,1,0:T(4,128)(2,1)}), bf16[16,4,7168]{2,1,0:T(4,128)(2,1)}, u32[]{:S(2)}, u32[]{:S(2)}) %all-to-all-start.1) | async-done | bytes 917536 | tf_op jit(solution)/shard_map/all_to_all | solution.py:52
  87.3 6.2 %all-to-all-start.3 = ((bf16[16,4,7168]{2,1,0:T(4,128)(2,1)}), bf16[16,4,7168]{2,1,0:T(4,128)(2,1)S(1)}, u32[]{:S(2)}, u32[]{:S(2)}) async-start(bf16[16,4,7168]{2,1,0:T(4,128)(2,1)} %reshape.118), calls=%async_computation.3 | async-start | bytes 1835008 | tf_op jit(solution)/shard_map/all_to_all | solution.py:52
  93.5 1.7 %bitcast_reduce_fusion.1 = bf16[4,4,7168]{2,1,0:T(4,128)(2,1)S(1)} fusion(bf16[16,4,7168]{2,1,0:T(4,128)(2,1)} %all-to-all-done.1), kind=kLoop, calls=%fused_computation.21 | loop fusion | flops 344064 | bytes 1146880 | tf_op jit(solution)/shard_map/reduce_sum | solution.py:73
  95.3 0.6 gather_fusion
  95.9 0.1 select_convert_fusion.1
  96.0 0.1 reshape.121
  96.2 18.2 %all-to-all-done.3 = bf16[16,4,7168]{2,1,0:T(4,128)(2,1)S(1)} async-done(((bf16[16,4,7168]{2,1,0:T(4,128)(2,1)}), bf16[16,4,7168]{2,1,0:T(4,128)(2,1)S(1)}, u32[]{:S(2)}, u32[]{:S(2)}) %all-to-all-start.3) | async-done | bytes 917536 | tf_op jit(solution)/shard_map/all_to_all | solution.py:52
  114.3 0.4 bitcast_reduce_fusion
  114.8 0.6 gather_fusion.1
  115.5 0.1 select_convert_fusion
  115.6 0.1 reshape.122
  115.7 0.4 multiply_reduce_fusion.1
  116.1 0.4 multiply_reduce_fusion
  116.4 0.7 pad_maximum_fusion
  (18 shorter events, 0.3 us)
Async XLA Ops:
  0.0 11.8 %copy-start = (bf16[2,4,7168]{2,1,0:T(4,128)(2,1)S(1)}, bf16[2,4,7168]{2,1,0:T(4,128)(2,1)}, u32[]{:S(2)}) copy-start(bf16[2,4,7168]{2,1,0:T(4,128)(2,1)} %param.8) | copy-start | bytes 344068
  2.5 36.9 %copy-start.1 = (f32[2,4,2]{1,2,0:T(2,128)S(1)}, f32[2,4,2]{1,2,0:T(2,128)}, u32[]{:S(2)}) copy-start(f32[2,4,2]{1,2,0:T(2,128)} %param.10) | copy-start | bytes 196
  3.8 28.2 %all-to-all-start = ((bf16[16,4,7168]{2,1,0:T(4,128)(2,1)}), bf16[16,4,7168]{2,1,0:T(4,128)(2,1)S(1)}, u32[]{:S(2)}, u32[]{:S(2)}) async-start(bf16[16,4,7168]{2,1,0:T(4,128)(2,1)} %bitcast.2), calls=%async_computation | async-start | bytes 1835008 | tf_op jit(solution)/shard_map/all_to_all | solution.py:55
  33.2 27.0 %all-to-all-start.2 = ((bf16[16,4,7168]{2,1,0:T(4,128)(2,1)}), bf16[16,4,7168]{2,1,0:T(4,128)(2,1)S(1)}, u32[]{:S(2)}, u32[]{:S(2)}) async-start(bf16[16,4,7168]{2,1,0:T(4,128)(2,1)} %bitcast.11), calls=%async_computation.2 | async-start | bytes 1835008 | tf_op jit(solution)/shard_map/all_to_all | solution.py:55
  60.2 27.1 %all-to-all-start.1 = ((bf16[16,4,7168]{2,1,0:T(4,128)(2,1)}), bf16[16,4,7168]{2,1,0:T(4,128)(2,1)}, u32[]{:S(2)}, u32[]{:S(2)}) async-start(bf16[16,4,7168]{2,1,0:T(4,128)(2,1)} %reshape.113), calls=%async_computation.1 | async-start | bytes 1835008 | tf_op jit(solution)/shard_map/all_to_all | solution.py:52
  87.3 27.0 %all-to-all-start.3 = ((bf16[16,4,7168]{2,1,0:T(4,128)(2,1)}), bf16[16,4,7168]{2,1,0:T(4,128)(2,1)S(1)}, u32[]{:S(2)}, u32[]{:S(2)}) async-start(bf16[16,4,7168]{2,1,0:T(4,128)(2,1)} %reshape.118), calls=%async_computation.3 | async-start | bytes 1835008 | tf_op jit(solution)/shard_map/all_to_all | solution.py:52
where the time goes:
time: 118 us; the launch traced here: 117 us
  waiting for transfers between devices  59.9 us (51%)
  starting transfers between devices  26 us (22%)
  matrix products  17.8 us (15%)
  local copies, waits for them, and re-layouts  8.81 us (7%)
  other arithmetic  4.48 us (4%)
    all_to_all x2, waiting for transfers between devices, travel(): lax.all_to_all(rows_out, 'ep', split_axis=0, concat_axis=0, tiled=True)  30.9 us
    all_to_all x2, waiting for transfers between devices, direct_work(): lax.all_to_all(partial_value, 'ep', split_axis=0, concat_axis=0, tiled=True)  29.1 us
    all_to_all x2, starting transfers between devices, travel(): lax.all_to_all(rows_out, 'ep', split_axis=0, concat_axis=0, tiled=True)  13.6 us
    all_to_all x2, starting transfers between devices, direct_work(): lax.all_to_all(partial_value, 'ep', split_axis=0, concat_axis=0, tiled=True)  12.4 us
    dot_general x2, matrix products, expert_slice(): jnp.dot(slice_hidden, down_w, preferred_element_type=jnp.float32)  10.9 us
    dot_general x2, matrix products, expert_slice(): gate_pre = jnp.dot(rows, gate_w, preferred_element_type=jnp.float32)  5.5 us
    broadcast_in_dim x4, local copies, waits for them, and re-layouts, local(): jnp.broadcast_to(packed.reshape(experts, 1, capacity, features), (experts...  2.59 us
    reshape x2, local copies, waits for them, and re-layouts, compute(): return partial_value.reshape(received_rows.shape[:-1] + (features,))  2.52 us
  transfers between devices with their start and end apart: 4, of which 4 were waited for; matrix products, arithmetic and copies ran while one was open for 20% of the time, Pallas kernels for 0%

commit v1 on v0

v1 whole, which is shorter than its diff:
```python
import jax
import jax.numpy as jnp
from jax import lax
from jax.sharding import PartitionSpec as P

FF = 1024


route_scale = 2.5


def swap(value, mask, devices):
    return lax.ppermute(value, "ep", [(i, i ^ mask) for i in range(devices)])


def local(hidden, expert_ids, route_weight, w_gate, w_up, w_down):
    step_count, token_count, features = hidden.shape
    slice_units = w_gate.shape[-1]
    splits = FF // slice_units
    devices = lax.axis_size("ep")
    experts = devices // splits
    row_count = step_count * token_count
    own_expert = lax.axis_index("ep") // splits

    own = hidden.reshape(row_count, features)
    blocks = [own] + [swap(own, splits * far, devices) for far in range(1, experts)]
    mask = splits // 2
    while mask:
        blocks = blocks + [swap(block, mask, devices) for block in blocks]
        mask //= 2
    rows = jnp.concatenate(blocks, axis=0)

    gate_pre = jnp.dot(rows, w_gate[0], preferred_element_type=jnp.float32)
    up_pre = jnp.dot(rows, w_up[0], preferred_element_type=jnp.float32)
    slice_hidden = (jax.nn.silu(gate_pre) * up_pre).astype(jnp.bfloat16)
    partial = jnp.dot(slice_hidden, w_down[0], preferred_element_type=jnp.float32)

    mask = 1
    while mask < splits:
        half = partial.shape[0] // 2
        other = swap(partial[half:].astype(jnp.bfloat16), mask, devices)
        partial = partial[:half] + other.astype(jnp.float32)
        mask *= 2
    expert_rows = partial.astype(jnp.bfloat16).reshape(experts, row_count, features)

    weights = route_scale * route_weight / jnp.sum(route_weight, axis=-1, keepdims=True)
    total = jnp.zeros((row_count, features), jnp.float32)
    for far in range(experts):
        back = expert_rows[far] if far == 0 else swap(expert_rows[far], splits * far, devices)
        share = jnp.sum(jnp.where(expert_ids == (own_expert ^ far), weights, 0.0), axis=-1)
        total = total + share.reshape(row_count, 1) * back.astype(jnp.float32)
    return total.astype(jnp.bfloat16).reshape(hidden.shape)


def solution(mesh):
    placed = (
        P(None, ("groups", "ep"), None),
        P(None, ("groups", "ep"), None),
        P(None, ("groups", "ep"), None),
        P("ep", None, None),
        P("ep", None, None),
        P("ep", None, None),
    )
    return jax.shard_map(
        local,
        mesh=mesh,
        in_specs=placed,
        out_specs=P(None, ("groups", "ep"), None),
        check_vma=False,
    )
```

time: 118 us -> 66 us (0.56)
  waiting for transfers between devices: 59.9 us -> 30.9 us
  matrix products: 17.8 us -> 9.79 us
  starting transfers between devices: 26 us -> 19.2 us
  local copies, waits for them, and re-layouts: 8.81 us -> 3.77 us
  other arithmetic: 4.48 us -> 1.97 us
    all_to_all x4 -> x0, waiting for transfers between devices: 59.9 us -> none  [the longest x2 30.9 us: travel(): lax.all_to_all(rows_out, 'ep', split_axis=0, concat_axis=0, tiled=True)]
    ppermute x0 -> x20, waiting for transfers between devices: none -> 30.9 us  [swap(): return lax.ppermute(value, 'ep', [(i, i ^ mask) for i in range(devices)])]
    all_to_all x4 -> x0, starting transfers between devices: 26 us -> none  [the longest x2 13.6 us: travel(): lax.all_to_all(rows_out, 'ep', split_axis=0, concat_axis=0, tiled=True)]
    ppermute x0 -> x20, starting transfers between devices: none -> 19.2 us  [swap(): return lax.ppermute(value, 'ep', [(i, i ^ mask) for i in range(devices)])]
    dot_general x6 -> x2, matrix products: 17.8 us -> 9.79 us  [the longest x1 7.1 us: local(): jnp.dot(slice_hidden, w_down[0], preferred_element_type=jnp.float32)]
    reduce_sum x7 -> x0, other arithmetic: 2.97 us -> none  [the longest x2 2.17 us: local(): jnp.sum(returned[step_index].reshape(experts, splits, capacity, features)...]
    broadcast_in_dim x4 -> x0, local copies, waits for them, and re-layouts: 2.59 us -> none  [local(): jnp.broadcast_to(packed.reshape(experts, 1, capacity, features), (experts...]
    add x2 -> x1, other arithmetic: 0.01 us -> 1.7 us  [local(): partial = partial[:half] + other.astype(jnp.float32)]
  transfers between devices with their start and end apart: 4 -> 20, of which waited for: 4 -> 10; matrix products, arithmetic and copies ran while one was open for 20% -> 1% of each run, Pallas kernels for 0% -> 0%
where the time goes in v1:
time: 66 us; the launch traced here: 65.8 us
  waiting for transfers between devices  30.9 us (47%)
  starting transfers between devices  19.2 us (29%)
  matrix products  9.79 us (15%)
  local copies, waits for them, and re-layouts  3.77 us (6%)
  other arithmetic  1.97 us (3%)
    ppermute x20, waiting for transfers between devices, swap(): return lax.ppermute(value, 'ep', [(i, i ^ mask) for i in range(devices)])  30.9 us
    ppermute x20, starting transfers between devices, swap(): return lax.ppermute(value, 'ep', [(i, i ^ mask) for i in range(devices)])  19.2 us
    dot_general x1, matrix products, local(): jnp.dot(slice_hidden, w_down[0], preferred_element_type=jnp.float32)  7.1 us
    dot_general x1, matrix products, local(): up_pre = jnp.dot(rows, w_up[0], preferred_element_type=jnp.float32)  2.69 us
    add x1, other arithmetic, local(): partial = partial[:half] + other.astype(jnp.float32)  1.7 us
    slice x2, local copies, waits for them, and re-layouts, local(): other = swap(partial[half:].astype(jnp.bfloat16), mask, devices)  1.64 us
  transfers between devices with their start and end apart: 20, of which 10 were waited for; matrix products, arithmetic and copies ran while one was open for 1% of the time, Pallas kernels for 0%

profile of v1, /device:TPU:0, one launch (start us, length us, event | category | flops | bytes accessed | tf_op | source)
XLA Modules:
  0.0 65.8 jit_solution(6364251789228372578)
XLA Ops:
  0.0 0.9 %reshape.24 = bf16[8,7168]{1,0:T(8,128)(2,1)S(1)} reshape(bf16[2,4,7168]{2,1,0:T(4,128)(2,1)} %param.6) | data formatting | bytes 229376 | tf_op jit(solution)/shard_map/reshape | solution.py:25
  0.9 3.1 %collective-permute-start = (bf16[8,7168]{1,0:T(8,128)(2,1)S(1)}, bf16[8,7168]{1,0:T(8,128)(2,1)S(1)}, u32[]{:S(2)}, u32[]{:S(2)}) collective-permute-start(bf16[8,7168]{1,0:T(8,128)(2,1)S(1)} %reshape.24), channel_id=1, source_target_pairs={{0,4},{1,5},{2,6},{3,7},{4,0},{5,1},{6,2},{7,3},{8,12},{9,13},{10,... | collective-permute-start | bytes 344072 | tf_op jit(solution)/shard_map/ppermute | solution.py:13
  4.0 2.6 %collective-permute-start.1 = (bf16[8,7168]{1,0:T(8,128)(2,1)S(1)}, bf16[8,7168]{1,0:T(8,128)(2,1)S(1)}, u32[]{:S(2)}, u32[]{:S(2)}) collective-permute-start(bf16[8,7168]{1,0:T(8,128)(2,1)S(1)} %reshape.24), channel_id=1, source_target_pairs={{0,8},{1,9},{2,10},{3,11},{4,12},{5,13},{6,14},{7,15},{8,0},{9,1},... | collective-permute-start | bytes 344072 | tf_op jit(solution)/shard_map/ppermute | solution.py:13
  6.6 0.0 collective-permute-start.2
  6.6 1.7 %collective-permute-start.3 = (bf16[8,7168]{1,0:T(8,128)(2,1)S(1)}, bf16[8,7168]{1,0:T(8,128)(2,1)S(1)}, u32[]{:S(2)}, u32[]{:S(2)}) collective-permute-start(bf16[8,7168]{1,0:T(8,128)(2,1)S(1)} %reshape.24), channel_id=1, source_target_pairs={{0,2},{1,3},{2,0},{3,1},{4,6},{5,7},{6,4},{7,5},{8,10},{9,11},{10,... | collective-permute-start | bytes 344072 | tf_op jit(solution)/shard_map/ppermute | solution.py:13
  8.4 0.0 collective-permute-start.7
  8.4 0.0 collective-permute-done
  8.4 1.7 %collective-permute-start.4 = (bf16[8,7168]{1,0:T(8,128)(2,1)S(1)}, bf16[8,7168]{1,0:T(8,128)(2,1)S(1)}, u32[]{:S(2)}, u32[]{:S(2)}) collective-permute-start(bf16[8,7168]{1,0:T(8,128)(2,1)S(1)} %collective-permute-done), channel_id=1, source_target_pairs={{0,2},{1,3},{2,0},{3,1},{4,6},{5,7},{6,4},{7,5},{8,10},{9,11},{10,... | collective-permute-start | bytes 344072 | tf_op jit(solution)/shard_map/ppermute | solution.py:13
  10.1 5.6 %collective-permute-done.1 = bf16[8,7168]{1,0:T(8,128)(2,1)S(1)} collective-permute-done((bf16[8,7168]{1,0:T(8,128)(2,1)S(1)}, bf16[8,7168]{1,0:T(8,128)(2,1)S(1)}, u32[]{:S(2)}, u32[]{:S(2)}) %collective-permute-start.1) | collective-permute-done | bytes 114720 | tf_op jit(solution)/shard_map/ppermute | solution.py:13
  15.7 1.5 %collective-permute-start.5 = (bf16[8,7168]{1,0:T(8,128)(2,1)S(1)}, bf16[8,7168]{1,0:T(8,128)(2,1)S(1)}, u32[]{:S(2)}, u32[]{:S(2)}) collective-permute-start(bf16[8,7168]{1,0:T(8,128)(2,1)S(1)} %collective-permute-done.1), channel_id=1, source_target_pairs={{0,2},{1,3},{2,0},{3,1},{4,6},{5,7},{6,4},{7,5},{8,10},{9,11},{10,... | collective-permute-start | bytes 344072 | tf_op jit(solution)/shard_map/ppermute | solution.py:13
  17.2 0.0 collective-permute-done.2
  17.3 0.6 collective-permute-start.6
  17.8 0.0 collective-permute-done.3
  17.9 0.1 collective-permute-start.8
  18.0 0.6 collective-permute-start.9
  18.5 2.0 %collective-permute-done.5 = bf16[8,7168]{1,0:T(8,128)(2,1)S(1)} collective-permute-done((bf16[8,7168]{1,0:T(8,128)(2,1)S(1)}, bf16[8,7168]{1,0:T(8,128)(2,1)S(1)}, u32[]{:S(2)}, u32[]{:S(2)}) %collective-permute-start.5) | collective-permute-done | bytes 114720 | tf_op jit(solution)/shard_map/ppermute | solution.py:13
  20.5 1.6 %collective-permute-done.6 = bf16[8,7168]{1,0:T(8,128)(2,1)S(1)} collective-permute-done((bf16[8,7168]{1,0:T(8,128)(2,1)S(1)}, bf16[8,7168]{1,0:T(8,128)(2,1)S(1)}, u32[]{:S(2)}, u32[]{:S(2)}) %collective-permute-start.6) | collective-permute-done | bytes 114720 | tf_op jit(solution)/shard_map/ppermute | solution.py:13
  22.1 0.0 collective-permute-start.11
  22.1 0.0 collective-permute-done.7
  22.1 0.6 collective-permute-start.12
  22.7 0.0 collective-permute-done.8
  22.7 0.1 collective-permute-start.13
  22.8 0.6 collective-permute-start.14
  23.5 0.2 collective-permute-done.12
  23.7 0.4 collective-permute-done.13
  24.1 0.2 collective-permute-done.14
  24.4 2.7 %fusion.3 = f32[128,256]{1,0:T(8,128)S(1)} fusion(bf16[128,7168]{1,0:T(8,128)(2,1)S(1)} %constant_dynamic-update-slice_fusion, bf16[1,7168,256]{2,1,0:T(8,128)(2,1)} %param.10), kind=kOutput, calls=%fused_computation.3 | convolution fusion | flops 469762048 | bytes 5636096 | tf_op jit(solution)/shard_map/dot_general | solution.py:34
  27.1 7.1 %fusion.1 = f32[128,7168]{1,0:T(8,128)} fusion(bf16[1,256,7168]{2,1,0:T(8,128)(2,1)} %param.11, f32[128,256]{1,0:T(8,128)S(1)} %fusion.3, bf16[128,7168]{1,0:T(8,128)(2,1)S(1)} %constant_dynamic-update-slice_fusion, bf16[1,7168,256]{2,1,0:T(8,128)(2,1)} %param.9), kind=kOutput, calls=%fused_computation.1 | convolution fusion | flops 939720704 | bytes 12976128 | tf_op jit(solution)/shard_map/dot_general | solution.py:36
  34.2 1.6 %slice.53 = bf16[64,7168]{1,0:T(8,128)(2,1)S(1)} slice(f32[128,7168]{1,0:T(8,128)} %fusion.1), slice={[64:128], [0:7168]} | slice | bytes 1835008 | tf_op jit(solution)/shard_map/slice | solution.py:41
  35.8 0.4 collective-permute-start.15
  36.2 2.1 %collective-permute-done.15 = bf16[64,7168]{1,0:T(8,128)(2,1)S(1)} collective-permute-done((bf16[64,7168]{1,0:T(8,128)(2,1)S(1)}, bf16[64,7168]{1,0:T(8,128)(2,1)S(1)}, u32[]{:S(2)}, u32[]{:S(2)}) %collective-permute-start.15) | collective-permute-done | bytes 917536 | tf_op jit(solution)/shard_map/ppermute | solution.py:13
  38.3 1.7 %slice_add_fusion = f32[64,7168]{1,0:T(8,128)S(1)} fusion(f32[128,7168]{1,0:T(8,128)} %fusion.1, bf16[64,7168]{1,0:T(8,128)(2,1)S(1)} %collective-permute-done.15), kind=kLoop, calls=%fused_computation.8 | loop fusion | flops 917504 | bytes 4587520 | tf_op jit(solution)/shard_map/add | solution.py:42
  40.0 0.0 copy-start
  40.0 0.0 copy-start.1
  40.1 1.2 %collective-permute-start.16 = (bf16[32,7168]{1,0:T(8,128)(2,1)S(1)}, bf16[32,7168]{1,0:T(8,128)(2,1)S(1)}, u32[]{:S(2)}, u32[]{:S(2)}) collective-permute-start(bf16[32,7168]{1,0:T(8,128)(2,1)S(1)} %slice.54), channel_id=1, source_target_pairs={{0,2},{1,3},{2,0},{3,1},{4,6},{5,7},{6,4},{7,5},{8,10},{9,11},{10,... | collective-permute-start | bytes 1376264 | tf_op jit(solution)/shard_map/ppermute | solution.py:13
  41.3 11.6 %collective-permute-done.16 = bf16[32,7168]{1,0:T(8,128)(2,1)S(1)} collective-permute-done((bf16[32,7168]{1,0:T(8,128)(2,1)S(1)}, bf16[32,7168]{1,0:T(8,128)(2,1)S(1)}, u32[]{:S(2)}, u32[]{:S(2)}) %collective-permute-start.16) | collective-permute-done | bytes 458784 | tf_op jit(solution)/shard_map/ppermute | solution.py:13
  52.9 0.1 fusion.8
  53.1 0.3 collective-permute-start.17
  53.3 2.8 %collective-permute-start.18 = (bf16[8,7168]{1,0:T(8,128)(2,1)S(1)}, bf16[8,7168]{1,0:T(8,128)(2,1)S(1)}, u32[]{:S(2)}, u32[]{:S(2)}) collective-permute-start(bf16[8,7168]{1,0:T(8,128)(2,1)S(1)} %get-tuple-element.11), channel_id=1, source_target_pairs={{0,8},{1,9},{2,10},{3,11},{4,12},{5,13},{6,14},{7,15},{8,0},{9,1},... | collective-permute-start | bytes 344072 | tf_op jit(solution)/shard_map/ppermute | solution.py:13
  56.2 1.4 %collective-permute-start.19 = (bf16[8,7168]{1,0:T(8,128)(2,1)S(1)}, bf16[8,7168]{1,0:T(8,128)(2,1)S(1)}, u32[]{:S(2)}, u32[]{:S(2)}) collective-permute-start(bf16[8,7168]{1,0:T(8,128)(2,1)S(1)} %get-tuple-element.10), channel_id=1, source_target_pairs={{0,12},{1,13},{2,14},{3,15},{4,8},{5,9},{6,10},{7,11},{8,4},{9,5},... | collective-permute-start | bytes 344072 | tf_op jit(solution)/shard_map/ppermute | solution.py:13
  57.6 0.1 mul.51
  57.6 0.1 mul.56
  57.7 0.1 mul.59
  57.8 0.1 mul.62
  57.9 1.4 %collective-permute-done.17 = bf16[8,7168]{1,0:T(8,128)(2,1)S(1)} collective-permute-done((bf16[8,7168]{1,0:T(8,128)(2,1)S(1)}, bf16[8,7168]{1,0:T(8,128)(2,1)S(1)}, u32[]{:S(2)}, u32[]{:S(2)}) %collective-permute-start.17) | collective-permute-done | bytes 114720 | tf_op jit(solution)/shard_map/ppermute | solution.py:13
  59.3 5.6 %collective-permute-done.18 = bf16[8,7168]{1,0:T(8,128)(2,1)S(1)} collective-permute-done((bf16[8,7168]{1,0:T(8,128)(2,1)S(1)}, bf16[8,7168]{1,0:T(8,128)(2,1)S(1)}, u32[]{:S(2)}, u32[]{:S(2)}) %collective-permute-start.18) | collective-permute-done | bytes 114720 | tf_op jit(solution)/shard_map/ppermute | solution.py:13
  64.9 0.2 add_convert_fusion
  65.1 0.7 %reshape.25 = bf16[2,4,7168]{2,1,0:T(4,128)(2,1)} reshape(bf16[8,7168]{1,0:T(8,128)(2,1)S(1)} %add_convert_fusion) | data formatting | bytes 229376 | tf_op jit(solution)/shard_map/reshape | solution.py:52
  (27 shorter events, 0.3 us)
Async XLA Ops:
  0.9 7.4 %collective-permute-start = (bf16[8,7168]{1,0:T(8,128)(2,1)S(1)}, bf16[8,7168]{1,0:T(8,128)(2,1)S(1)}, u32[]{:S(2)}, u32[]{:S(2)}) collective-permute-start(bf16[8,7168]{1,0:T(8,128)(2,1)S(1)} %reshape.24), channel_id=1, source_target_pairs={{0,4},{1,5},{2,6},{3,7},{4,0},{5,1},{6,2},{7,3},{8,12},{9,13},{10,... | collective-permute-start | bytes 344072 | tf_op jit(solution)/shard_map/ppermute | solution.py:13
  4.0 11.7 %collective-permute-start.1 = (bf16[8,7168]{1,0:T(8,128)(2,1)S(1)}, bf16[8,7168]{1,0:T(8,128)(2,1)S(1)}, u32[]{:S(2)}, u32[]{:S(2)}) collective-permute-start(bf16[8,7168]{1,0:T(8,128)(2,1)S(1)} %reshape.24), channel_id=1, source_target_pairs={{0,8},{1,9},{2,10},{3,11},{4,12},{5,13},{6,14},{7,15},{8,0},{9,1},... | collective-permute-start | bytes 344072 | tf_op jit(solution)/shard_map/ppermute | solution.py:13
  6.6 10.6 %collective-permute-start.2 = (bf16[8,7168]{1,0:T(8,128)(2,1)S(1)}, bf16[8,7168]{1,0:T(8,128)(2,1)S(1)}, u32[]{:S(2)}, u32[]{:S(2)}) collective-permute-start(bf16[8,7168]{1,0:T(8,128)(2,1)S(1)} %reshape.24), channel_id=1, source_target_pairs={{0,12},{1,13},{2,14},{3,15},{4,8},{5,9},{6,10},{7,11},{8,4},{9,5},... | collective-permute-start | bytes 344072 | tf_op jit(solution)/shard_map/ppermute | solution.py:13
  6.6 11.2 %collective-permute-start.3 = (bf16[8,7168]{1,0:T(8,128)(2,1)S(1)}, bf16[8,7168]{1,0:T(8,128)(2,1)S(1)}, u32[]{:S(2)}, u32[]{:S(2)}) collective-permute-start(bf16[8,7168]{1,0:T(8,128)(2,1)S(1)} %reshape.24), channel_id=1, source_target_pairs={{0,2},{1,3},{2,0},{3,1},{4,6},{5,7},{6,4},{7,5},{8,10},{9,11},{10,... | collective-permute-start | bytes 344072 | tf_op jit(solution)/shard_map/ppermute | solution.py:13
  8.4 13.8 %collective-permute-start.7 = (bf16[8,7168]{1,0:T(8,128)(2,1)S(1)}, bf16[8,7168]{1,0:T(8,128)(2,1)S(1)}, u32[]{:S(2)}, u32[]{:S(2)}) collective-permute-start(bf16[8,7168]{1,0:T(8,128)(2,1)S(1)} %reshape.24), channel_id=1, source_target_pairs={{0,1},{1,0},{2,3},{3,2},{4,5},{5,4},{6,7},{7,6},{8,9},{9,8},{10,11... | collective-permute-start | bytes 344072 | tf_op jit(solution)/shard_map/ppermute | solution.py:13
  8.4 9.6 %collective-permute-start.4 = (bf16[8,7168]{1,0:T(8,128)(2,1)S(1)}, bf16[8,7168]{1,0:T(8,128)(2,1)S(1)}, u32[]{:S(2)}, u32[]{:S(2)}) collective-permute-start(bf16[8,7168]{1,0:T(8,128)(2,1)S(1)} %collective-permute-done), channel_id=1, source_target_pairs={{0,2},{1,3},{2,0},{3,1},{4,6},{5,7},{6,4},{7,5},{8,10},{9,11},{10,... | collective-permute-start | bytes 344072 | tf_op jit(solution)/shard_map/ppermute | solution.py:13
  15.7 4.8 %collective-permute-start.5 = (bf16[8,7168]{1,0:T(8,128)(2,1)S(1)}, bf16[8,7168]{1,0:T(8,128)(2,1)S(1)}, u32[]{:S(2)}, u32[]{:S(2)}) collective-permute-start(bf16[8,7168]{1,0:T(8,128)(2,1)S(1)} %collective-permute-done.1), channel_id=1, source_target_pairs={{0,2},{1,3},{2,0},{3,1},{4,6},{5,7},{6,4},{7,5},{8,10},{9,11},{10,... | collective-permute-start | bytes 344072 | tf_op jit(solution)/shard_map/ppermute | solution.py:13
  17.3 4.9 %collective-permute-start.6 = (bf16[8,7168]{1,0:T(8,128)(2,1)S(1)}, bf16[8,7168]{1,0:T(8,128)(2,1)S(1)}, u32[]{:S(2)}, u32[]{:S(2)}) collective-permute-start(bf16[8,7168]{1,0:T(8,128)(2,1)S(1)} %collective-permute-done.2), channel_id=1, source_target_pairs={{0,2},{1,3},{2,0},{3,1},{4,6},{5,7},{6,4},{7,5},{8,10},{9,11},{10,... | collective-permute-start | bytes 344072 | tf_op jit(solution)/shard_map/ppermute | solution.py:13
  17.9 4.9 %collective-permute-start.8 = (bf16[8,7168]{1,0:T(8,128)(2,1)S(1)}, bf16[8,7168]{1,0:T(8,128)(2,1)S(1)}, u32[]{:S(2)}, u32[]{:S(2)}) collective-permute-start(bf16[8,7168]{1,0:T(8,128)(2,1)S(1)} %collective-permute-done), channel_id=1, source_target_pairs={{0,1},{1,0},{2,3},{3,2},{4,5},{5,4},{6,7},{7,6},{8,9},{9,8},{10,11... | collective-permute-start | bytes 344072 | tf_op jit(solution)/shard_map/ppermute | solution.py:13
  18.0 4.9 %collective-permute-start.9 = (bf16[8,7168]{1,0:T(8,128)(2,1)S(1)}, bf16[8,7168]{1,0:T(8,128)(2,1)S(1)}, u32[]{:S(2)}, u32[]{:S(2)}) collective-permute-start(bf16[8,7168]{1,0:T(8,128)(2,1)S(1)} %collective-permute-done.1), channel_id=1, source_target_pairs={{0,1},{1,0},{2,3},{3,2},{4,5},{5,4},{6,7},{7,6},{8,9},{9,8},{10,11... | collective-permute-start | bytes 344072 | tf_op jit(solution)/shard_map/ppermute | solution.py:13
  20.5 2.9 %collective-permute-start.10 = (bf16[8,7168]{1,0:T(8,128)(2,1)S(1)}, bf16[8,7168]{1,0:T(8,128)(2,1)S(1)}, u32[]{:S(2)}, u32[]{:S(2)}) collective-permute-start(bf16[8,7168]{1,0:T(8,128)(2,1)S(1)} %collective-permute-done.2), channel_id=1, source_target_pairs={{0,1},{1,0},{2,3},{3,2},{4,5},{5,4},{6,7},{7,6},{8,9},{9,8},{10,11... | collective-permute-start | bytes 344072 | tf_op jit(solution)/shard_map/ppermute | solution.py:13
  22.1 1.3 %collective-permute-start.11 = (bf16[8,7168]{1,0:T(8,128)(2,1)S(1)}, bf16[8,7168]{1,0:T(8,128)(2,1)S(1)}, u32[]{:S(2)}, u32[]{:S(2)}) collective-permute-start(bf16[8,7168]{1,0:T(8,128)(2,1)S(1)} %collective-permute-done.3), channel_id=1, source_target_pairs={{0,1},{1,0},{2,3},{3,2},{4,5},{5,4},{6,7},{7,6},{8,9},{9,8},{10,11... | collective-permute-start | bytes 344072 | tf_op jit(solution)/shard_map/ppermute | solution.py:13
  22.1 1.5 %collective-permute-start.12 = (bf16[8,7168]{1,0:T(8,128)(2,1)S(1)}, bf16[8,7168]{1,0:T(8,128)(2,1)S(1)}, u32[]{:S(2)}, u32[]{:S(2)}) collective-permute-start(bf16[8,7168]{1,0:T(8,128)(2,1)S(1)} %collective-permute-done.4), channel_id=1, source_target_pairs={{0,1},{1,0},{2,3},{3,2},{4,5},{5,4},{6,7},{7,6},{8,9},{9,8},{10,11... | collective-permute-start | bytes 344072 | tf_op jit(solution)/shard_map/ppermute | solution.py:13
  22.7 1.4 %collective-permute-start.13 = (bf16[8,7168]{1,0:T(8,128)(2,1)S(1)}, bf16[8,7168]{1,0:T(8,128)(2,1)S(1)}, u32[]{:S(2)}, u32[]{:S(2)}) collective-permute-start(bf16[8,7168]{1,0:T(8,128)(2,1)S(1)} %collective-permute-done.5), channel_id=1, source_target_pairs={{0,1},{1,0},{2,3},{3,2},{4,5},{5,4},{6,7},{7,6},{8,9},{9,8},{10,11... | collective-permute-start | bytes 344072 | tf_op jit(solution)/shard_map/ppermute | solution.py:13
  22.8 1.5 %collective-permute-start.14 = (bf16[8,7168]{1,0:T(8,128)(2,1)S(1)}, bf16[8,7168]{1,0:T(8,128)(2,1)S(1)}, u32[]{:S(2)}, u32[]{:S(2)}) collective-permute-start(bf16[8,7168]{1,0:T(8,128)(2,1)S(1)} %collective-permute-done.6), channel_id=1, source_target_pairs={{0,1},{1,0},{2,3},{3,2},{4,5},{5,4},{6,7},{7,6},{8,9},{9,8},{10,11... | collective-permute-start | bytes 344072 | tf_op jit(solution)/shard_map/ppermute | solution.py:13
  35.8 2.5 %collective-permute-start.15 = (bf16[64,7168]{1,0:T(8,128)(2,1)S(1)}, bf16[64,7168]{1,0:T(8,128)(2,1)S(1)}, u32[]{:S(2)}, u32[]{:S(2)}) collective-permute-start(bf16[64,7168]{1,0:T(8,128)(2,1)S(1)} %slice.53), channel_id=1, source_target_pairs={{0,1},{1,0},{2,3},{3,2},{4,5},{5,4},{6,7},{7,6},{8,9},{9,8},{10,11... | collective-permute-start | bytes 2752520 | tf_op jit(solution)/shard_map/ppermute | solution.py:13
  40.0 17.5 %copy-start = (s32[2,4,2]{1,2,0:T(2,128)S(1)}, s32[2,4,2]{1,2,0:T(2,128)}, u32[]{:S(2)}) copy-start(s32[2,4,2]{1,2,0:T(2,128)} %param.7) | copy-start | bytes 196
  40.0 17.5 %copy-start.1 = (f32[2,4,2]{1,2,0:T(2,128)S(1)}, f32[2,4,2]{1,2,0:T(2,128)}, u32[]{:S(2)}) copy-start(f32[2,4,2]{1,2,0:T(2,128)} %param.8) | copy-start | bytes 196
  40.1 12.8 %collective-permute-start.16 = (bf16[32,7168]{1,0:T(8,128)(2,1)S(1)}, bf16[32,7168]{1,0:T(8,128)(2,1)S(1)}, u32[]{:S(2)}, u32[]{:S(2)}) collective-permute-start(bf16[32,7168]{1,0:T(8,128)(2,1)S(1)} %slice.54), channel_id=1, source_target_pairs={{0,2},{1,3},{2,0},{3,1},{4,6},{5,7},{6,4},{7,5},{8,10},{9,11},{10,... | collective-permute-start | bytes 1376264 | tf_op jit(solution)/shard_map/ppermute | solution.py:13
  53.1 6.2 %collective-permute-start.17 = (bf16[8,7168]{1,0:T(8,128)(2,1)S(1)}, bf16[8,7168]{1,0:T(8,128)(2,1)S(1)}, u32[]{:S(2)}, u32[]{:S(2)}) collective-permute-start(bf16[8,7168]{1,0:T(8,128)(2,1)S(1)} %get-tuple-element.9), channel_id=1, source_target_pairs={{0,4},{1,5},{2,6},{3,7},{4,0},{5,1},{6,2},{7,3},{8,12},{9,13},{10,... | collective-permute-start | bytes 344072 | tf_op jit(solution)/shard_map/ppermute | solution.py:13
  53.3 11.6 %collective-permute-start.18 = (bf16[8,7168]{1,0:T(8,128)(2,1)S(1)}, bf16[8,7168]{1,0:T(8,128)(2,1)S(1)}, u32[]{:S(2)}, u32[]{:S(2)}) collective-permute-start(bf16[8,7168]{1,0:T(8,128)(2,1)S(1)} %get-tuple-element.11), channel_id=1, source_target_pairs={{0,8},{1,9},{2,10},{3,11},{4,12},{5,13},{6,14},{7,15},{8,0},{9,1},... | collective-permute-start | bytes 344072 | tf_op jit(solution)/shard_map/ppermute | solution.py:13
  56.2 8.8 %collective-permute-start.19 = (bf16[8,7168]{1,0:T(8,128)(2,1)S(1)}, bf16[8,7168]{1,0:T(8,128)(2,1)S(1)}, u32[]{:S(2)}, u32[]{:S(2)}) collective-permute-start(bf16[8,7168]{1,0:T(8,128)(2,1)S(1)} %get-tuple-element.10), channel_id=1, source_target_pairs={{0,12},{1,13},{2,14},{3,15},{4,8},{5,9},{6,10},{7,11},{8,4},{9,5},... | collective-permute-start | bytes 344072 | tf_op jit(solution)/shard_map/ppermute | solution.py:13

commit v2 on v1

v2 whole, which is shorter than its diff:
```python
import functools

import jax
import jax.numpy as jnp
from jax import lax
from jax.experimental import pallas as pl
from jax.experimental.pallas import tpu as pltpu
from jax.sharding import PartitionSpec as P

FF = 1024


route_scale = 2.5
MIB = 1 << 20
VMEM = pl.BlockSpec(memory_space=pltpu.VMEM)


def swap(value, mask, devices):
    return lax.ppermute(value, "ep", [(i, i ^ mask) for i in range(devices)])


def largest_chunk(total, most):
    return max(c for c in range(128, most + 1, 128) if total % c == 0)


def expert_kernel(count, *refs):
    blocks, (gate_ref, up_ref, down_ref, send_ref, keep_ref, both) = refs[:count], refs[count:]
    features, units = gate_ref.shape[-2:]
    depth = largest_chunk(features, 1024)
    half = send_ref.shape[0]
    both[...] = jnp.zeros_like(both)

    @pl.loop(0, features // depth)
    def _(step):
        at = pl.ds(pl.multiple_of(step * depth, depth), depth)
        rows = jnp.concatenate([block[:, at] for block in blocks], axis=0)
        both[0] += jnp.dot(rows, gate_ref[at, :], preferred_element_type=jnp.float32)
        both[1] += jnp.dot(rows, up_ref[at, :], preferred_element_type=jnp.float32)

    gate_pre = both[0]
    slice_hidden = (gate_pre / (1 + jnp.exp(-gate_pre)) * both[1]).astype(jnp.bfloat16)

    @pl.loop(0, features // depth)
    def _(step):
        at = pl.ds(pl.multiple_of(step * depth, depth), depth)
        out = jnp.dot(slice_hidden, down_ref[:, at], preferred_element_type=jnp.float32)
        keep_ref[:, at] = out[:half]
        send_ref[:, at] = out[half:].astype(jnp.bfloat16)


def expert_slice(blocks, gate_w, up_w, down_w):
    features, units = gate_w.shape
    rows = sum(block.shape[0] for block in blocks)
    half = rows // 2
    return pl.pallas_call(
        functools.partial(expert_kernel, len(blocks)),
        out_shape=(
            jax.ShapeDtypeStruct((half, features), jnp.bfloat16),
            jax.ShapeDtypeStruct((half, features), jnp.float32),
        ),
        in_specs=[VMEM] * (len(blocks) + 3),
        out_specs=(VMEM, VMEM),
        scratch_shapes=[pltpu.VMEM((2, rows, units), jnp.float32)],
        compiler_params=pltpu.CompilerParams(vmem_limit_bytes=28 * MIB),
        cost_estimate=pl.CostEstimate(flops=6 * rows * units * features, bytes_accessed=6 * units * features, transcendentals=0),
        name="expert_slice",
    )(*blocks, gate_w, up_w, down_w)


def pass_kernel(rows_ref, *refs):
    refs[-1][...] = rows_ref[...]


def pass_rows(rows, *beside):
    return pl.pallas_call(
        pass_kernel,
        out_shape=jax.ShapeDtypeStruct(rows.shape, rows.dtype),
        in_specs=[VMEM] + [pl.BlockSpec(memory_space=pl.ANY)] * len(beside),
        out_specs=VMEM,
        compiler_params=pltpu.CompilerParams(vmem_limit_bytes=16 * MIB),
        name="pass_rows",
    )(rows, *[pltpu.with_memory_space_constraint(w, pltpu.HBM) for w in beside])


def add_kernel(size, places, keep_ref, *refs):
    terms, out_ref = refs[:-1], refs[-1]
    total = keep_ref[pl.ds(places[0] * size, size), :]
    for place, term in zip(places[1:], terms):
        total = total + term[pl.ds(place * size, size), :].astype(jnp.float32)
    out_ref[...] = total.astype(out_ref.dtype)


def add_rows(size, places, keep, *terms):
    features = keep.shape[1]
    return pl.pallas_call(
        functools.partial(add_kernel, size, places),
        out_shape=jax.ShapeDtypeStruct((size, features), jnp.bfloat16),
        in_specs=[VMEM] * (1 + len(terms)),
        out_specs=VMEM,
        compiler_params=pltpu.CompilerParams(vmem_limit_bytes=16 * MIB),
        cost_estimate=pl.CostEstimate(flops=size * features, bytes_accessed=8 * size * features, transcendentals=0),
        name="add_rows",
    )(keep, *terms)


def mix_kernel(share_ref, *refs):
    backs, out_ref = refs[:-1], refs[-1]
    steps, tokens, _ = out_ref.shape
    share = share_ref[...]
    total = share[:, 0:1] * backs[0][...].astype(jnp.float32)
    for far in range(1, len(backs)):
        total = total + share[:, far:far + 1] * backs[far][...].astype(jnp.float32)
    for step in range(steps):
        out_ref[step] = total[step * tokens:(step + 1) * tokens].astype(out_ref.dtype)


def mix(share, backs, shape):
    return pl.pallas_call(
        mix_kernel,
        out_shape=jax.ShapeDtypeStruct(shape, jnp.bfloat16),
        in_specs=[VMEM] * (1 + len(backs)),
        out_specs=VMEM,
        compiler_params=pltpu.CompilerParams(vmem_limit_bytes=16 * MIB),
        name="mix",
    )(share, *backs)


def local(hidden, expert_ids, route_weight, w_gate, w_up, w_down):
    step_count, token_count, features = hidden.shape
    slice_units = w_gate.shape[-1]
    splits = FF // slice_units
    devices = lax.axis_size("ep")
    experts = devices // splits
    row_count = step_count * token_count
    own_expert = lax.axis_index("ep") // splits

    own = hidden.reshape(row_count, features)
    blocks = {0: own}
    mask = devices // 2
    while mask:
        for key, block in list(blocks.items()):
            if key == devices // 2 and mask == devices // 4:
                block = pass_rows(block, w_gate, w_up, w_down)
            blocks[key + mask] = swap(block, mask, devices)
        mask //= 2
    order = [e * splits + y + c for c in (0, 1) for y in (0, 2) for e in range(experts)]
    send, keep = expert_slice([blocks[k] for k in order], w_gate[0], w_up[0], w_down[0])

    twin = swap(send, 1, devices)
    across = {}
    for far in reversed(range(experts)):
        across[far] = swap(add_rows(row_count, (experts + far, experts + far), keep, twin), 2, devices)
    backs = {}
    for far in reversed(range(experts)):
        rows = add_rows(row_count, (far, far, 0), keep, twin, across[far])
        backs[far] = swap(rows, splits * far, devices) if far else rows

    weights = route_scale * route_weight / jnp.sum(route_weight, axis=-1, keepdims=True)
    away = own_expert ^ jnp.arange(experts, dtype=jnp.int32)
    share = jnp.sum(jnp.where(expert_ids[..., None] == away, weights[..., None], 0.0), axis=-2)
    return mix(share.reshape(row_count, experts), [backs[far] for far in range(experts)], hidden.shape)


def solution(mesh):
    placed = (
        P(None, ("groups", "ep"), None),
        P(None, ("groups", "ep"), None),
        P(None, ("groups", "ep"), None),
        P("ep", None, None),
        P("ep", None, None),
        P("ep", None, None),
    )
    return jax.shard_map(
        local,
        mesh=mesh,
        in_specs=placed,
        out_specs=P(None, ("groups", "ep"), None),
        check_vma=False,
    )
```

time: 66 us -> 49.1 us (0.74)
  waiting for transfers between devices: 30.9 us -> 19.4 us
  matrix products: 9.79 us -> 0 us
  Pallas kernels: 0 us -> 4.96 us
  starting transfers between devices: 19.2 us -> 23.4 us
  local copies, waits for them, and re-layouts: 3.77 us -> 0.96 us
  other arithmetic: 1.97 us -> 0.1 us
    ppermute x20 -> x23, waiting for transfers between devices: 30.9 us -> 19.4 us  [swap(): return lax.ppermute(value, 'ep', [(i, i ^ mask) for i in range(devices)])]
    dot_general x2 -> x0, matrix products: 9.79 us -> none  [the longest x1 7.1 us: local(): jnp.dot(slice_hidden, w_down[0], preferred_element_type=jnp.float32)]
    pallas_call x0 -> x11, Pallas kernels: none -> 4.96 us  [the longest x1 3.89 us: expert_slice(): pl.pallas_call(functools.partial(expert_kernel, len(blocks)), out_shape=(...]
    ppermute x20 -> x23, starting transfers between devices: 19.2 us -> 23.4 us  [swap(): return lax.ppermute(value, 'ep', [(i, i ^ mask) for i in range(devices)])]
    add x1 -> x0, other arithmetic: 1.7 us -> none  [local(): partial = partial[:half] + other.astype(jnp.float32)]
    slice x3 -> x0, local copies, waits for them, and re-layouts: 1.66 us -> none  [the longest x2 1.64 us: local(): other = swap(partial[half:].astype(jnp.bfloat16), mask, devices)]
    reshape x1 -> x0, local copies, waits for them, and re-layouts: 0.7 us -> none  [local(): return total.astype(jnp.bfloat16).reshape(hidden.shape)]
  transfers between devices with their start and end apart: 20 -> 23, of which waited for: 10 -> 15; matrix products, arithmetic and copies ran while one was open for 1% -> 0% of each run, Pallas kernels for 0% -> 0%
where the time goes in v2:
time: 49.1 us; the launch traced here: 49 us
  starting transfers between devices  23.4 us (48%)
  waiting for transfers between devices  19.4 us (40%)
  Pallas kernels  4.96 us (10%)
  local copies, waits for them, and re-layouts  0.96 us (2%)
    ppermute x23, starting transfers between devices, swap(): return lax.ppermute(value, 'ep', [(i, i ^ mask) for i in range(devices)])  23.4 us
    ppermute x23, waiting for transfers between devices, swap(): return lax.ppermute(value, 'ep', [(i, i ^ mask) for i in range(devices)])  19.4 us
    pallas_call x1, Pallas kernels, expert_slice(): pl.pallas_call(functools.partial(expert_kernel, len(blocks)), out_shape=(...  3.89 us
  transfers between devices with their start and end apart: 23, of which 15 were waited for; matrix products, arithmetic and copies ran while one was open for 0% of the time, Pallas kernels for 0%

profile of v2, /device:TPU:0, one launch (start us, length us, event | category | flops | bytes accessed | tf_op | source)
XLA Modules:
  0.0 49.0 jit_solution(5152960914935465720)
XLA Ops:
  0.0 0.9 %reshape.14.refs_0_ = bf16[8,7168]{1,0:T(8,128)(2,1)S(1)} reshape(bf16[2,4,7168]{2,1,0:T(4,128)(2,1)} %param.6) | data formatting | bytes 229376 | tf_op jit(solution)/shard_map/reshape | solution.py:137
  0.9 0.0 copy-start
  0.9 0.0 copy-start.1
  1.0 0.0 copy-start.2
  1.0 4.1 %collective-permute-start.1 = (bf16[8,7168]{1,0:T(8,128)(2,1)S(1)}, bf16[8,7168]{1,0:T(8,128)(2,1)S(1)}, u32[]{:S(2)}, u32[]{:S(2)}) collective-permute-start(bf16[8,7168]{1,0:T(8,128)(2,1)S(1)} %reshape.14.refs_0_), channel_id=1, source_target_pairs={{0,8},{1,9},{2,10},{3,11},{4,12},{5,13},{6,14},{7,15},{8,0},{9,1},... | collective-permute-start | bytes 344072 | tf_op jit(solution)/shard_map/ppermute | solution.py:19
  5.1 1.6 %collective-permute-start = (bf16[8,7168]{1,0:T(8,128)(2,1)S(1)}, bf16[8,7168]{1,0:T(8,128)(2,1)S(1)}, u32[]{:S(2)}, u32[]{:S(2)}) collective-permute-start(bf16[8,7168]{1,0:T(8,128)(2,1)S(1)} %reshape.14.refs_0_), channel_id=1, source_target_pairs={{0,4},{1,5},{2,6},{3,7},{4,0},{5,1},{6,2},{7,3},{8,12},{9,13},{10,... | collective-permute-start | bytes 344072 | tf_op jit(solution)/shard_map/ppermute | solution.py:19
  6.6 1.5 %collective-permute-start.3 = (bf16[8,7168]{1,0:T(8,128)(2,1)S(1)}, bf16[8,7168]{1,0:T(8,128)(2,1)S(1)}, u32[]{:S(2)}, u32[]{:S(2)}) collective-permute-start(bf16[8,7168]{1,0:T(8,128)(2,1)S(1)} %reshape.14.refs_0_), channel_id=1, source_target_pairs={{0,2},{1,3},{2,0},{3,1},{4,6},{5,7},{6,4},{7,5},{8,10},{9,11},{10,... | collective-permute-start | bytes 344072 | tf_op jit(solution)/shard_map/ppermute | solution.py:19
  8.2 0.0 collective-permute-start.7
  8.2 2.6 %collective-permute-done.1.rows_ref.refs_2_ = bf16[8,7168]{1,0:T(8,128)(2,1)S(1)} collective-permute-done((bf16[8,7168]{1,0:T(8,128)(2,1)S(1)}, bf16[8,7168]{1,0:T(8,128)(2,1)S(1)}, u32[]{:S(2)}, u32[]{:S(2)}) %collective-permute-start.1) | collective-permute-done | bytes 114720 | tf_op jit(solution)/shard_map/ppermute | solution.py:19
  10.8 0.7 %collective-permute-start.2 = (bf16[8,7168]{1,0:T(8,128)(2,1)S(1)}, bf16[8,7168]{1,0:T(8,128)(2,1)S(1)}, u32[]{:S(2)}, u32[]{:S(2)}) collective-permute-start(bf16[8,7168]{1,0:T(8,128)(2,1)S(1)} %pass_rows.1), channel_id=1, source_target_pairs={{0,4},{1,5},{2,6},{3,7},{4,0},{5,1},{6,2},{7,3},{8,12},{9,13},{10,... | collective-permute-start | bytes 344072 | tf_op jit(solution)/shard_map/ppermute | solution.py:19
  11.5 1.5 %collective-permute-start.5 = (bf16[8,7168]{1,0:T(8,128)(2,1)S(1)}, bf16[8,7168]{1,0:T(8,128)(2,1)S(1)}, u32[]{:S(2)}, u32[]{:S(2)}) collective-permute-start(bf16[8,7168]{1,0:T(8,128)(2,1)S(1)} %collective-permute-done.1.rows_ref.refs_2_), channel_id=1, source_target_pairs={{0,2},{1,3},{2,0},{3,1},{4,6},{5,7},{6,4},{7,5},{8,10},{9,11},{10,... | collective-permute-start | bytes 344072 | tf_op jit(solution)/shard_map/ppermute | solution.py:19
  13.0 0.0 collective-permute-done.refs_1_
  13.0 0.5 %collective-permute-start.4 = (bf16[8,7168]{1,0:T(8,128)(2,1)S(1)}, bf16[8,7168]{1,0:T(8,128)(2,1)S(1)}, u32[]{:S(2)}, u32[]{:S(2)}) collective-permute-start(bf16[8,7168]{1,0:T(8,128)(2,1)S(1)} %collective-permute-done.refs_1_), channel_id=1, source_target_pairs={{0,2},{1,3},{2,0},{3,1},{4,6},{5,7},{6,4},{7,5},{8,10},{9,11},{10,... | collective-permute-start | bytes 344072 | tf_op jit(solution)/shard_map/ppermute | solution.py:19
  13.5 0.5 %collective-permute-start.8 = (bf16[8,7168]{1,0:T(8,128)(2,1)S(1)}, bf16[8,7168]{1,0:T(8,128)(2,1)S(1)}, u32[]{:S(2)}, u32[]{:S(2)}) collective-permute-start(bf16[8,7168]{1,0:T(8,128)(2,1)S(1)} %collective-permute-done.refs_1_), channel_id=1, source_target_pairs={{0,1},{1,0},{2,3},{3,2},{4,5},{5,4},{6,7},{7,6},{8,9},{9,8},{10,11... | collective-permute-start | bytes 344072 | tf_op jit(solution)/shard_map/ppermute | solution.py:19
  14.0 1.6 %collective-permute-done.2.refs_3_ = bf16[8,7168]{1,0:T(8,128)(2,1)S(1)} collective-permute-done((bf16[8,7168]{1,0:T(8,128)(2,1)S(1)}, bf16[8,7168]{1,0:T(8,128)(2,1)S(1)}, u32[]{:S(2)}, u32[]{:S(2)}) %collective-permute-start.2) | collective-permute-done | bytes 114720 | tf_op jit(solution)/shard_map/ppermute | solution.py:19
  15.6 1.6 %collective-permute-start.6 = (bf16[8,7168]{1,0:T(8,128)(2,1)S(1)}, bf16[8,7168]{1,0:T(8,128)(2,1)S(1)}, u32[]{:S(2)}, u32[]{:S(2)}) collective-permute-start(bf16[8,7168]{1,0:T(8,128)(2,1)S(1)} %collective-permute-done.2.refs_3_), channel_id=1, source_target_pairs={{0,2},{1,3},{2,0},{3,1},{4,6},{5,7},{6,4},{7,5},{8,10},{9,11},{10,... | collective-permute-start | bytes 344072 | tf_op jit(solution)/shard_map/ppermute | solution.py:19
  17.2 0.3 collective-permute-done.5.refs_6_
  17.5 2.5 %collective-permute-done.4.refs_5_ = bf16[8,7168]{1,0:T(8,128)(2,1)S(1)} collective-permute-done((bf16[8,7168]{1,0:T(8,128)(2,1)S(1)}, bf16[8,7168]{1,0:T(8,128)(2,1)S(1)}, u32[]{:S(2)}, u32[]{:S(2)}) %collective-permute-start.4) | collective-permute-done | bytes 114720 | tf_op jit(solution)/shard_map/ppermute | solution.py:19
  19.9 0.0 collective-permute-start.10
  19.9 0.0 collective-permute-done.9.refs_10_
  19.9 0.5 %collective-permute-start.13 = (bf16[8,7168]{1,0:T(8,128)(2,1)S(1)}, bf16[8,7168]{1,0:T(8,128)(2,1)S(1)}, u32[]{:S(2)}, u32[]{:S(2)}) collective-permute-start(bf16[8,7168]{1,0:T(8,128)(2,1)S(1)} %collective-permute-done.5.refs_6_), channel_id=1, source_target_pairs={{0,1},{1,0},{2,3},{3,2},{4,5},{5,4},{6,7},{7,6},{8,9},{9,8},{10,11... | collective-permute-start | bytes 344072 | tf_op jit(solution)/shard_map/ppermute | solution.py:19
  20.5 0.0 collective-permute-done.8.refs_9_
  20.5 0.1 collective-permute-start.12
  20.5 0.7 %collective-permute-done.6.refs_7_ = bf16[8,7168]{1,0:T(8,128)(2,1)S(1)} collective-permute-done((bf16[8,7168]{1,0:T(8,128)(2,1)S(1)}, bf16[8,7168]{1,0:T(8,128)(2,1)S(1)}, u32[]{:S(2)}, u32[]{:S(2)}) %collective-permute-start.6) | collective-permute-done | bytes 114720 | tf_op jit(solution)/shard_map/ppermute | solution.py:19
  21.2 0.0 collective-permute-start.14
  21.2 0.0 collective-permute-done.11.refs_12_
  21.2 0.1 collective-permute-done.10.refs_11_
  21.3 0.2 collective-permute-done.13.refs_14_
  21.4 0.4 collective-permute-done.12.refs_13_
  21.8 0.7 %collective-permute-done.14.refs_15_ = bf16[8,7168]{1,0:T(8,128)(2,1)S(1)} collective-permute-done((bf16[8,7168]{1,0:T(8,128)(2,1)S(1)}, bf16[8,7168]{1,0:T(8,128)(2,1)S(1)}, u32[]{:S(2)}, u32[]{:S(2)}) %collective-permute-start.14) | collective-permute-done | bytes 114720 | tf_op jit(solution)/shard_map/ppermute | solution.py:19
  22.5 3.9 %expert_slice.1 = (bf16[64,7168]{1,0:T(8,128)(2,1)S(1)}, f32[64,7168]{1,0:T(8,128)S(1)}) custom-call(bf16[8,7168]{1,0:T(8,128)(2,1)S(1)} %reshape.14.refs_0_, bf16[8,7168]{1,0:T(8,128)(2,1)S(1)} %collective-permute-done.refs_1_, bf16[8,7168]{1,0:T(8,128)(2,1)S(1)} %collective-permute-done.1.rows_ref.refs_2_, ...), custom_call_target="tpu_custom_call" | custom-call | flops 1409286144 | bytes 11010048 | tf_op jit(solution)/shard_map/expert_slice/pallas_call | solution.py:55
  26.4 0.2 collective-permute-start.15
  26.6 2.3 %collective-permute-done.15.refs_0_ = bf16[64,7168]{1,0:T(8,128)(2,1)S(1)} collective-permute-done((bf16[64,7168]{1,0:T(8,128)(2,1)S(1)}, bf16[64,7168]{1,0:T(8,128)(2,1)S(1)}, u32[]{:S(2)}, u32[]{:S(2)}) %collective-permute-start.15) | collective-permute-done | bytes 917536 | tf_op jit(solution)/shard_map/ppermute | solution.py:19
  29.0 1.6 %collective-permute-start.21 = (bf16[8,7168]{1,0:T(8,128)(2,1)S(1)}, bf16[8,7168]{1,0:T(8,128)(2,1)S(1)}, u32[]{:S(2)}, u32[]{:S(2)}) collective-permute-start(bf16[8,7168]{1,0:T(8,128)(2,1)S(1)} %add_rows.14), channel_id=1, source_target_pairs={{0,2},{1,3},{2,0},{3,1},{4,6},{5,7},{6,4},{7,5},{8,10},{9,11},{10,... | collective-permute-start | bytes 344072 | tf_op jit(solution)/shard_map/ppermute | solution.py:19
  30.6 0.6 %collective-permute-start.19 = (bf16[8,7168]{1,0:T(8,128)(2,1)S(1)}, bf16[8,7168]{1,0:T(8,128)(2,1)S(1)}, u32[]{:S(2)}, u32[]{:S(2)}) collective-permute-start(bf16[8,7168]{1,0:T(8,128)(2,1)S(1)} %add_rows.12), channel_id=1, source_target_pairs={{0,2},{1,3},{2,0},{3,1},{4,6},{5,7},{6,4},{7,5},{8,10},{9,11},{10,... | collective-permute-start | bytes 344072 | tf_op jit(solution)/shard_map/ppermute | solution.py:19
  31.2 1.6 %collective-permute-start.17 = (bf16[8,7168]{1,0:T(8,128)(2,1)S(1)}, bf16[8,7168]{1,0:T(8,128)(2,1)S(1)}, u32[]{:S(2)}, u32[]{:S(2)}) collective-permute-start(bf16[8,7168]{1,0:T(8,128)(2,1)S(1)} %add_rows.10), channel_id=1, source_target_pairs={{0,2},{1,3},{2,0},{3,1},{4,6},{5,7},{6,4},{7,5},{8,10},{9,11},{10,... | collective-permute-start | bytes 344072 | tf_op jit(solution)/shard_map/ppermute | solution.py:19
  32.8 0.6 %collective-permute-start.16 = (bf16[8,7168]{1,0:T(8,128)(2,1)S(1)}, bf16[8,7168]{1,0:T(8,128)(2,1)S(1)}, u32[]{:S(2)}, u32[]{:S(2)}) collective-permute-start(bf16[8,7168]{1,0:T(8,128)(2,1)S(1)} %add_rows.8), channel_id=1, source_target_pairs={{0,2},{1,3},{2,0},{3,1},{4,6},{5,7},{6,4},{7,5},{8,10},{9,11},{10,... | collective-permute-start | bytes 344072 | tf_op jit(solution)/shard_map/ppermute | solution.py:19
  33.4 1.6 %collective-permute-done.21.refs_1_ = bf16[8,7168]{1,0:T(8,128)(2,1)S(1)} collective-permute-done((bf16[8,7168]{1,0:T(8,128)(2,1)S(1)}, bf16[8,7168]{1,0:T(8,128)(2,1)S(1)}, u32[]{:S(2)}, u32[]{:S(2)}) %collective-permute-start.21) | collective-permute-done | bytes 114720 | tf_op jit(solution)/shard_map/ppermute | solution.py:19
  35.1 0.0 copy-start.3
  35.1 3.2 %collective-permute-start.22 = (bf16[8,7168]{1,0:T(8,128)(2,1)S(1)}, bf16[8,7168]{1,0:T(8,128)(2,1)S(1)}, u32[]{:S(2)}, u32[]{:S(2)}) collective-permute-start(bf16[8,7168]{1,0:T(8,128)(2,1)S(1)} %add_rows.15), channel_id=1, source_target_pairs={{0,12},{1,13},{2,14},{3,15},{4,8},{5,9},{6,10},{7,11},{8,4},{9,5},... | collective-permute-start | bytes 344072 | tf_op jit(solution)/shard_map/ppermute | solution.py:19
  38.4 2.6 %collective-permute-start.20 = (bf16[8,7168]{1,0:T(8,128)(2,1)S(1)}, bf16[8,7168]{1,0:T(8,128)(2,1)S(1)}, u32[]{:S(2)}, u32[]{:S(2)}) collective-permute-start(bf16[8,7168]{1,0:T(8,128)(2,1)S(1)} %add_rows.13), channel_id=1, source_target_pairs={{0,8},{1,9},{2,10},{3,11},{4,12},{5,13},{6,14},{7,15},{8,0},{9,1},... | collective-permute-start | bytes 344072 | tf_op jit(solution)/shard_map/ppermute | solution.py:19
  41.0 0.4 collective-permute-start.18
  41.5 0.1 select_reduce_fusion
  41.5 0.1 collective-permute-done.16.refs_1_
  41.7 1.4 %collective-permute-done.22.refs_3_ = bf16[8,7168]{1,0:T(8,128)(2,1)S(1)} collective-permute-done((bf16[8,7168]{1,0:T(8,128)(2,1)S(1)}, bf16[8,7168]{1,0:T(8,128)(2,1)S(1)}, u32[]{:S(2)}, u32[]{:S(2)}) %collective-permute-start.22) | collective-permute-done | bytes 114720 | tf_op jit(solution)/shard_map/ppermute | solution.py:19
  43.0 4.8 %collective-permute-done.20.refs_2_ = bf16[8,7168]{1,0:T(8,128)(2,1)S(1)} collective-permute-done((bf16[8,7168]{1,0:T(8,128)(2,1)S(1)}, bf16[8,7168]{1,0:T(8,128)(2,1)S(1)}, u32[]{:S(2)}, u32[]{:S(2)}) %collective-permute-start.20) | collective-permute-done | bytes 114720 | tf_op jit(solution)/shard_map/ppermute | solution.py:19
  47.9 0.3 collective-permute-done.18.refs_1_
  48.1 0.8 %mix.1 = bf16[2,4,7168]{2,1,0:T(4,128)(2,1)} custom-call(f32[8,4]{1,0:T(8,128)S(1)} %bitcast.8, bf16[8,7168]{1,0:T(8,128)(2,1)S(1)} %add_rows.9.refs_0_, bf16[8,7168]{1,0:T(8,128)(2,1)S(1)} %collective-permute-done.18.refs_1_, bf16[8,7168]{1,0:T(8,128)(2,1)S(1)} %collective-permute-done.20.refs_2_, bf16[8,7168]{1,0:T(8,128)(2,1)S(1)} %collective-permute-done.22.refs_3_), custom_call_target="tpu_custom_call" | custom-call | tf_op jit(solution)/shard_map/mix/pallas_call | solution.py:118
  (23 shorter events, 0.3 us)
Async XLA Ops:
  0.9 21.6 %copy-start = (bf16[1,7168,256]{2,1,0:T(8,128)(2,1)S(1)}, bf16[1,7168,256]{2,1,0:T(8,128)(2,1)}, u32[]{:S(2)}) copy-start(bf16[1,7168,256]{2,1,0:T(8,128)(2,1)} %refs_0_.1) | copy-start | bytes 11010052
  0.9 21.6 %copy-start.1 = (bf16[1,7168,256]{2,1,0:T(8,128)(2,1)S(1)}, bf16[1,7168,256]{2,1,0:T(8,128)(2,1)}, u32[]{:S(2)}) copy-start(bf16[1,7168,256]{2,1,0:T(8,128)(2,1)} %refs_1_.1) | copy-start | bytes 11010052
  1.0 21.6 %copy-start.2 = (bf16[1,256,7168]{2,1,0:T(8,128)(2,1)S(1)}, bf16[1,256,7168]{2,1,0:T(8,128)(2,1)}, u32[]{:S(2)}) copy-start(bf16[1,256,7168]{2,1,0:T(8,128)(2,1)} %refs_2_.1) | copy-start | bytes 11010052
  1.0 9.8 %collective-permute-start.1 = (bf16[8,7168]{1,0:T(8,128)(2,1)S(1)}, bf16[8,7168]{1,0:T(8,128)(2,1)S(1)}, u32[]{:S(2)}, u32[]{:S(2)}) collective-permute-start(bf16[8,7168]{1,0:T(8,128)(2,1)S(1)} %reshape.14.refs_0_), channel_id=1, source_target_pairs={{0,8},{1,9},{2,10},{3,11},{4,12},{5,13},{6,14},{7,15},{8,0},{9,1},... | collective-permute-start | bytes 344072 | tf_op jit(solution)/shard_map/ppermute | solution.py:19
  5.1 7.9 %collective-permute-start = (bf16[8,7168]{1,0:T(8,128)(2,1)S(1)}, bf16[8,7168]{1,0:T(8,128)(2,1)S(1)}, u32[]{:S(2)}, u32[]{:S(2)}) collective-permute-start(bf16[8,7168]{1,0:T(8,128)(2,1)S(1)} %reshape.14.refs_0_), channel_id=1, source_target_pairs={{0,4},{1,5},{2,6},{3,7},{4,0},{5,1},{6,2},{7,3},{8,12},{9,13},{10,... | collective-permute-start | bytes 344072 | tf_op jit(solution)/shard_map/ppermute | solution.py:19
  6.6 6.9 %collective-permute-start.3 = (bf16[8,7168]{1,0:T(8,128)(2,1)S(1)}, bf16[8,7168]{1,0:T(8,128)(2,1)S(1)}, u32[]{:S(2)}, u32[]{:S(2)}) collective-permute-start(bf16[8,7168]{1,0:T(8,128)(2,1)S(1)} %reshape.14.refs_0_), channel_id=1, source_target_pairs={{0,2},{1,3},{2,0},{3,1},{4,6},{5,7},{6,4},{7,5},{8,10},{9,11},{10,... | collective-permute-start | bytes 344072 | tf_op jit(solution)/shard_map/ppermute | solution.py:19
  8.2 5.3 %collective-permute-start.7 = (bf16[8,7168]{1,0:T(8,128)(2,1)S(1)}, bf16[8,7168]{1,0:T(8,128)(2,1)S(1)}, u32[]{:S(2)}, u32[]{:S(2)}) collective-permute-start(bf16[8,7168]{1,0:T(8,128)(2,1)S(1)} %reshape.14.refs_0_), channel_id=1, source_target_pairs={{0,1},{1,0},{2,3},{3,2},{4,5},{5,4},{6,7},{7,6},{8,9},{9,8},{10,11... | collective-permute-start | bytes 344072 | tf_op jit(solution)/shard_map/ppermute | solution.py:19
  10.8 4.9 %collective-permute-start.2 = (bf16[8,7168]{1,0:T(8,128)(2,1)S(1)}, bf16[8,7168]{1,0:T(8,128)(2,1)S(1)}, u32[]{:S(2)}, u32[]{:S(2)}) collective-permute-start(bf16[8,7168]{1,0:T(8,128)(2,1)S(1)} %pass_rows.1), channel_id=1, source_target_pairs={{0,4},{1,5},{2,6},{3,7},{4,0},{5,1},{6,2},{7,3},{8,12},{9,13},{10,... | collective-permute-start | bytes 344072 | tf_op jit(solution)/shard_map/ppermute | solution.py:19
  11.5 6.0 %collective-permute-start.5 = (bf16[8,7168]{1,0:T(8,128)(2,1)S(1)}, bf16[8,7168]{1,0:T(8,128)(2,1)S(1)}, u32[]{:S(2)}, u32[]{:S(2)}) collective-permute-start(bf16[8,7168]{1,0:T(8,128)(2,1)S(1)} %collective-permute-done.1.rows_ref.refs_2_), channel_id=1, source_target_pairs={{0,2},{1,3},{2,0},{3,1},{4,6},{5,7},{6,4},{7,5},{8,10},{9,11},{10,... | collective-permute-start | bytes 344072 | tf_op jit(solution)/shard_map/ppermute | solution.py:19
  13.0 6.9 %collective-permute-start.4 = (bf16[8,7168]{1,0:T(8,128)(2,1)S(1)}, bf16[8,7168]{1,0:T(8,128)(2,1)S(1)}, u32[]{:S(2)}, u32[]{:S(2)}) collective-permute-start(bf16[8,7168]{1,0:T(8,128)(2,1)S(1)} %collective-permute-done.refs_1_), channel_id=1, source_target_pairs={{0,2},{1,3},{2,0},{3,1},{4,6},{5,7},{6,4},{7,5},{8,10},{9,11},{10,... | collective-permute-start | bytes 344072 | tf_op jit(solution)/shard_map/ppermute | solution.py:19
  13.5 6.4 %collective-permute-start.9 = (bf16[8,7168]{1,0:T(8,128)(2,1)S(1)}, bf16[8,7168]{1,0:T(8,128)(2,1)S(1)}, u32[]{:S(2)}, u32[]{:S(2)}) collective-permute-start(bf16[8,7168]{1,0:T(8,128)(2,1)S(1)} %collective-permute-done.1.rows_ref.refs_2_), channel_id=1, source_target_pairs={{0,1},{1,0},{2,3},{3,2},{4,5},{5,4},{6,7},{7,6},{8,9},{9,8},{10,11... | collective-permute-start | bytes 344072 | tf_op jit(solution)/shard_map/ppermute | solution.py:19
  13.5 6.9 %collective-permute-start.8 = (bf16[8,7168]{1,0:T(8,128)(2,1)S(1)}, bf16[8,7168]{1,0:T(8,128)(2,1)S(1)}, u32[]{:S(2)}, u32[]{:S(2)}) collective-permute-start(bf16[8,7168]{1,0:T(8,128)(2,1)S(1)} %collective-permute-done.refs_1_), channel_id=1, source_target_pairs={{0,1},{1,0},{2,3},{3,2},{4,5},{5,4},{6,7},{7,6},{8,9},{9,8},{10,11... | collective-permute-start | bytes 344072 | tf_op jit(solution)/shard_map/ppermute | solution.py:19
  15.6 5.5 %collective-permute-start.6 = (bf16[8,7168]{1,0:T(8,128)(2,1)S(1)}, bf16[8,7168]{1,0:T(8,128)(2,1)S(1)}, u32[]{:S(2)}, u32[]{:S(2)}) collective-permute-start(bf16[8,7168]{1,0:T(8,128)(2,1)S(1)} %collective-permute-done.2.refs_3_), channel_id=1, source_target_pairs={{0,2},{1,3},{2,0},{3,1},{4,6},{5,7},{6,4},{7,5},{8,10},{9,11},{10,... | collective-permute-start | bytes 344072 | tf_op jit(solution)/shard_map/ppermute | solution.py:19
  17.5 3.7 %collective-permute-start.11 = (bf16[8,7168]{1,0:T(8,128)(2,1)S(1)}, bf16[8,7168]{1,0:T(8,128)(2,1)S(1)}, u32[]{:S(2)}, u32[]{:S(2)}) collective-permute-start(bf16[8,7168]{1,0:T(8,128)(2,1)S(1)} %collective-permute-done.3.refs_4_), channel_id=1, source_target_pairs={{0,1},{1,0},{2,3},{3,2},{4,5},{5,4},{6,7},{7,6},{8,9},{9,8},{10,11... | collective-permute-start | bytes 344072 | tf_op jit(solution)/shard_map/ppermute | solution.py:19
  19.9 1.3 %collective-permute-start.10 = (bf16[8,7168]{1,0:T(8,128)(2,1)S(1)}, bf16[8,7168]{1,0:T(8,128)(2,1)S(1)}, u32[]{:S(2)}, u32[]{:S(2)}) collective-permute-start(bf16[8,7168]{1,0:T(8,128)(2,1)S(1)} %collective-permute-done.2.refs_3_), channel_id=1, source_target_pairs={{0,1},{1,0},{2,3},{3,2},{4,5},{5,4},{6,7},{7,6},{8,9},{9,8},{10,11... | collective-permute-start | bytes 344072 | tf_op jit(solution)/shard_map/ppermute | solution.py:19
  19.9 1.5 %collective-permute-start.13 = (bf16[8,7168]{1,0:T(8,128)(2,1)S(1)}, bf16[8,7168]{1,0:T(8,128)(2,1)S(1)}, u32[]{:S(2)}, u32[]{:S(2)}) collective-permute-start(bf16[8,7168]{1,0:T(8,128)(2,1)S(1)} %collective-permute-done.5.refs_6_), channel_id=1, source_target_pairs={{0,1},{1,0},{2,3},{3,2},{4,5},{5,4},{6,7},{7,6},{8,9},{9,8},{10,11... | collective-permute-start | bytes 344072 | tf_op jit(solution)/shard_map/ppermute | solution.py:19
  20.5 1.3 %collective-permute-start.12 = (bf16[8,7168]{1,0:T(8,128)(2,1)S(1)}, bf16[8,7168]{1,0:T(8,128)(2,1)S(1)}, u32[]{:S(2)}, u32[]{:S(2)}) collective-permute-start(bf16[8,7168]{1,0:T(8,128)(2,1)S(1)} %collective-permute-done.4.refs_5_), channel_id=1, source_target_pairs={{0,1},{1,0},{2,3},{3,2},{4,5},{5,4},{6,7},{7,6},{8,9},{9,8},{10,11... | collective-permute-start | bytes 344072 | tf_op jit(solution)/shard_map/ppermute | solution.py:19
  21.2 1.3 %collective-permute-start.14 = (bf16[8,7168]{1,0:T(8,128)(2,1)S(1)}, bf16[8,7168]{1,0:T(8,128)(2,1)S(1)}, u32[]{:S(2)}, u32[]{:S(2)}) collective-permute-start(bf16[8,7168]{1,0:T(8,128)(2,1)S(1)} %collective-permute-done.6.refs_7_), channel_id=1, source_target_pairs={{0,1},{1,0},{2,3},{3,2},{4,5},{5,4},{6,7},{7,6},{8,9},{9,8},{10,11... | collective-permute-start | bytes 344072 | tf_op jit(solution)/shard_map/ppermute | solution.py:19
  26.4 2.5 %collective-permute-start.15 = (bf16[64,7168]{1,0:T(8,128)(2,1)S(1)}, bf16[64,7168]{1,0:T(8,128)(2,1)S(1)}, u32[]{:S(2)}, u32[]{:S(2)}) collective-permute-start(bf16[64,7168]{1,0:T(8,128)(2,1)S(1)} %get-tuple-element.8), channel_id=1, source_target_pairs={{0,1},{1,0},{2,3},{3,2},{4,5},{5,4},{6,7},{7,6},{8,9},{9,8},{10,11... | collective-permute-start | bytes 2752520 | tf_op jit(solution)/shard_map/ppermute | solution.py:19
  29.0 3.8 %copy-start.4 = (f32[2,4,2]{1,2,0:T(2,128)S(1)}, f32[2,4,2]{1,2,0:T(2,128)}, u32[]{:S(2)}) copy-start(f32[2,4,2]{1,2,0:T(2,128)} %param.8) | copy-start | bytes 196
  29.0 6.1 %collective-permute-start.21 = (bf16[8,7168]{1,0:T(8,128)(2,1)S(1)}, bf16[8,7168]{1,0:T(8,128)(2,1)S(1)}, u32[]{:S(2)}, u32[]{:S(2)}) collective-permute-start(bf16[8,7168]{1,0:T(8,128)(2,1)S(1)} %add_rows.14), channel_id=1, source_target_pairs={{0,2},{1,3},{2,0},{3,1},{4,6},{5,7},{6,4},{7,5},{8,10},{9,11},{10,... | collective-permute-start | bytes 344072 | tf_op jit(solution)/shard_map/ppermute | solution.py:19
  30.6 7.7 %collective-permute-start.19 = (bf16[8,7168]{1,0:T(8,128)(2,1)S(1)}, bf16[8,7168]{1,0:T(8,128)(2,1)S(1)}, u32[]{:S(2)}, u32[]{:S(2)}) collective-permute-start(bf16[8,7168]{1,0:T(8,128)(2,1)S(1)} %add_rows.12), channel_id=1, source_target_pairs={{0,2},{1,3},{2,0},{3,1},{4,6},{5,7},{6,4},{7,5},{8,10},{9,11},{10,... | collective-permute-start | bytes 344072 | tf_op jit(solution)/shard_map/ppermute | solution.py:19
  31.2 9.8 %collective-permute-start.17 = (bf16[8,7168]{1,0:T(8,128)(2,1)S(1)}, bf16[8,7168]{1,0:T(8,128)(2,1)S(1)}, u32[]{:S(2)}, u32[]{:S(2)}) collective-permute-start(bf16[8,7168]{1,0:T(8,128)(2,1)S(1)} %add_rows.10), channel_id=1, source_target_pairs={{0,2},{1,3},{2,0},{3,1},{4,6},{5,7},{6,4},{7,5},{8,10},{9,11},{10,... | collective-permute-start | bytes 344072 | tf_op jit(solution)/shard_map/ppermute | solution.py:19
  32.8 8.8 %collective-permute-start.16 = (bf16[8,7168]{1,0:T(8,128)(2,1)S(1)}, bf16[8,7168]{1,0:T(8,128)(2,1)S(1)}, u32[]{:S(2)}, u32[]{:S(2)}) collective-permute-start(bf16[8,7168]{1,0:T(8,128)(2,1)S(1)} %add_rows.8), channel_id=1, source_target_pairs={{0,2},{1,3},{2,0},{3,1},{4,6},{5,7},{6,4},{7,5},{8,10},{9,11},{10,... | collective-permute-start | bytes 344072 | tf_op jit(solution)/shard_map/ppermute | solution.py:19
  35.1 6.4 %copy-start.3 = (s32[2,4,2]{1,2,0:T(2,128)S(1)}, s32[2,4,2]{1,2,0:T(2,128)}, u32[]{:S(2)}) copy-start(s32[2,4,2]{1,2,0:T(2,128)} %param.7) | copy-start | bytes 196
  35.1 8.0 %collective-permute-start.22 = (bf16[8,7168]{1,0:T(8,128)(2,1)S(1)}, bf16[8,7168]{1,0:T(8,128)(2,1)S(1)}, u32[]{:S(2)}, u32[]{:S(2)}) collective-permute-start(bf16[8,7168]{1,0:T(8,128)(2,1)S(1)} %add_rows.15), channel_id=1, source_target_pairs={{0,12},{1,13},{2,14},{3,15},{4,8},{5,9},{6,10},{7,11},{8,4},{9,5},... | collective-permute-start | bytes 344072 | tf_op jit(solution)/shard_map/ppermute | solution.py:19
  38.4 9.5 %collective-permute-start.20 = (bf16[8,7168]{1,0:T(8,128)(2,1)S(1)}, bf16[8,7168]{1,0:T(8,128)(2,1)S(1)}, u32[]{:S(2)}, u32[]{:S(2)}) collective-permute-start(bf16[8,7168]{1,0:T(8,128)(2,1)S(1)} %add_rows.13), channel_id=1, source_target_pairs={{0,8},{1,9},{2,10},{3,11},{4,12},{5,13},{6,14},{7,15},{8,0},{9,1},... | collective-permute-start | bytes 344072 | tf_op jit(solution)/shard_map/ppermute | solution.py:19
  41.0 7.1 %collective-permute-start.18 = (bf16[8,7168]{1,0:T(8,128)(2,1)S(1)}, bf16[8,7168]{1,0:T(8,128)(2,1)S(1)}, u32[]{:S(2)}, u32[]{:S(2)}) collective-permute-start(bf16[8,7168]{1,0:T(8,128)(2,1)S(1)} %add_rows.11), channel_id=1, source_target_pairs={{0,4},{1,5},{2,6},{3,7},{4,0},{5,1},{6,2},{7,3},{8,12},{9,13},{10,... | collective-permute-start | bytes 344072 | tf_op jit(solution)/shard_map/ppermute | solution.py:19

commit v3 on v2

--- a/solution.py
+++ b/solution.py
@@ -23,6 +23,17 @@
     return max(c for c in range(128, most + 1, 128) if total % c == 0)
 
 
+def in_steps(total, depth, unrolled):
+    def run(body):
+        if unrolled:
+            for step in range(total // depth):
+                body(pl.ds(step * depth, depth))
+        else:
+            pl.loop(0, total // depth)(lambda step: body(pl.ds(pl.multiple_of(step * depth, depth), depth)))
+
+    return run
+
+
 def expert_kernel(count, *refs):
     blocks, (gate_ref, up_ref, down_ref, send_ref, keep_ref, both) = refs[:count], refs[count:]
     features, units = gate_ref.shape[-2:]
@@ -30,9 +41,8 @@
     half = send_ref.shape[0]
     both[...] = jnp.zeros_like(both)
 
-    @pl.loop(0, features // depth)
-    def _(step):
-        at = pl.ds(pl.multiple_of(step * depth, depth), depth)
+    @in_steps(features, depth, both.shape[1] <= 256)
+    def _(at):
         rows = jnp.concatenate([block[:, at] for block in blocks], axis=0)
         both[0] += jnp.dot(rows, gate_ref[at, :], preferred_element_type=jnp.float32)
         both[1] += jnp.dot(rows, up_ref[at, :], preferred_element_type=jnp.float32)
@@ -40,9 +50,8 @@
     gate_pre = both[0]
     slice_hidden = (gate_pre / (1 + jnp.exp(-gate_pre)) * both[1]).astype(jnp.bfloat16)
 
-    @pl.loop(0, features // depth)
-    def _(step):
-        at = pl.ds(pl.multiple_of(step * depth, depth), depth)
+    @in_steps(features, depth, both.shape[1] <= 256)
+    def _(at):
         out = jnp.dot(slice_hidden, down_ref[:, at], preferred_element_type=jnp.float32)
         keep_ref[:, at] = out[:half]
         send_ref[:, at] = out[half:].astype(jnp.bfloat16)
@@ -136,13 +145,13 @@
 
     own = hidden.reshape(row_count, features)
     blocks = {0: own}
-    mask = devices // 2
-    while mask:
-        for key, block in list(blocks.items()):
-            if key == devices // 2 and mask == devices // 4:
-                block = pass_rows(block, w_gate, w_up, w_down)
-            blocks[key + mask] = swap(block, mask, devices)
-        mask //= 2
+    for key in sorted(range(1, devices), key=lambda key: (key.bit_count(), -key)):
+        mask = splits if key == splits + 2 else key & -key
+        block = blocks[key - mask]
+        if key == devices // 2 + devices // 4:
+            block, blocks[splits] = lax.optimization_barrier((block, blocks[splits]))
+            block = pass_rows(block, w_gate, w_up, w_down)
+        blocks[key] = swap(block, mask, devices)
     order = [e * splits + y + c for c in (0, 1) for y in (0, 2) for e in range(experts)]
     send, keep = expert_slice([blocks[k] for k in order], w_gate[0], w_up[0], w_down[0])
 

time: 49.1 us -> 46.3 us (0.943)
  Pallas kernels: 4.96 us -> 2.82 us
  waiting for transfers between devices: 19.4 us -> 17.6 us
  starting transfers between devices: 23.4 us -> 24.5 us
    pallas_call x1, Pallas kernels: 3.89 us -> 1.74 us  [expert_slice(): pl.pallas_call(functools.partial(expert_kernel, len(blocks)), out_shape=(...]
    ppermute x23, waiting for transfers between devices: 19.4 us -> 17.6 us  [swap(): return lax.ppermute(value, 'ep', [(i, i ^ mask) for i in range(devices)])]
    ppermute x23, starting transfers between devices: 23.4 us -> 24.5 us  [swap(): return lax.ppermute(value, 'ep', [(i, i ^ mask) for i in range(devices)])]
  transfers between devices with their start and end apart: 23 -> 23, of which waited for: 15 -> 12; matrix products, arithmetic and copies ran while one was open for 0% -> 0% of each run, Pallas kernels for 0% -> 1%
where the time goes in v3:
time: 46.3 us; the launch traced here: 46.1 us
  starting transfers between devices  24.5 us (53%)
  waiting for transfers between devices  17.6 us (38%)
  Pallas kernels  2.82 us (6%)
  local copies, waits for them, and re-layouts  0.96 us (2%)
    ppermute x23, starting transfers between devices, swap(): return lax.ppermute(value, 'ep', [(i, i ^ mask) for i in range(devices)])  24.5 us
    ppermute x23, waiting for transfers between devices, swap(): return lax.ppermute(value, 'ep', [(i, i ^ mask) for i in range(devices)])  17.6 us
    pallas_call x1, Pallas kernels, expert_slice(): pl.pallas_call(functools.partial(expert_kernel, len(blocks)), out_shape=(...  1.74 us
    reshape x1, local copies, waits for them, and re-layouts, local(): own = hidden.reshape(row_count, features)  0.93 us
  transfers between devices with their start and end apart: 23, of which 12 were waited for; matrix products, arithmetic and copies ran while one was open for 0% of the time, Pallas kernels for 1%

profile of v3, /device:TPU:0, one launch (start us, length us, event | category | flops | bytes accessed | tf_op | source)
XLA Modules:
  0.0 46.1 jit_solution(3657313731750459779)
XLA Ops:
  0.0 0.9 %reshape.14.refs_0_ = bf16[8,7168]{1,0:T(8,128)(2,1)S(1)} reshape(bf16[2,4,7168]{2,1,0:T(4,128)(2,1)} %param.6) | data formatting | bytes 229376 | tf_op jit(solution)/shard_map/reshape | solution.py:146
  0.9 0.0 copy-start
  0.9 0.0 copy-start.1
  1.0 0.0 copy-start.2
  1.0 4.1 %collective-permute-start = (bf16[8,7168]{1,0:T(8,128)(2,1)S(1)}, bf16[8,7168]{1,0:T(8,128)(2,1)S(1)}, u32[]{:S(2)}, u32[]{:S(2)}) collective-permute-start(bf16[8,7168]{1,0:T(8,128)(2,1)S(1)} %reshape.14.refs_0_), channel_id=1, source_target_pairs={{0,8},{1,9},{2,10},{3,11},{4,12},{5,13},{6,14},{7,15},{8,0},{9,1},... | collective-permute-start | bytes 344072 | tf_op jit(solution)/shard_map/ppermute | solution.py:19
  5.1 1.6 %collective-permute-start.1 = (bf16[8,7168]{1,0:T(8,128)(2,1)S(1)}, bf16[8,7168]{1,0:T(8,128)(2,1)S(1)}, u32[]{:S(2)}, u32[]{:S(2)}) collective-permute-start(bf16[8,7168]{1,0:T(8,128)(2,1)S(1)} %reshape.14.refs_0_), channel_id=1, source_target_pairs={{0,4},{1,5},{2,6},{3,7},{4,0},{5,1},{6,2},{7,3},{8,12},{9,13},{10,... | collective-permute-start | bytes 344072 | tf_op jit(solution)/shard_map/ppermute | solution.py:19
  6.6 1.5 %collective-permute-start.3 = (bf16[8,7168]{1,0:T(8,128)(2,1)S(1)}, bf16[8,7168]{1,0:T(8,128)(2,1)S(1)}, u32[]{:S(2)}, u32[]{:S(2)}) collective-permute-start(bf16[8,7168]{1,0:T(8,128)(2,1)S(1)} %reshape.14.refs_0_), channel_id=1, source_target_pairs={{0,2},{1,3},{2,0},{3,1},{4,6},{5,7},{6,4},{7,5},{8,10},{9,11},{10,... | collective-permute-start | bytes 344072 | tf_op jit(solution)/shard_map/ppermute | solution.py:19
  8.2 0.0 collective-permute-start.7
  8.2 2.6 %collective-permute-done.rows_ref.refs_2_ = bf16[8,7168]{1,0:T(8,128)(2,1)S(1)} collective-permute-done((bf16[8,7168]{1,0:T(8,128)(2,1)S(1)}, bf16[8,7168]{1,0:T(8,128)(2,1)S(1)}, u32[]{:S(2)}, u32[]{:S(2)}) %collective-permute-start) | collective-permute-done | bytes 114720 | tf_op jit(solution)/shard_map/ppermute | solution.py:19
  10.8 0.2 collective-permute-done.1.refs_1_
  11.0 1.5 %collective-permute-start.2 = (bf16[8,7168]{1,0:T(8,128)(2,1)S(1)}, bf16[8,7168]{1,0:T(8,128)(2,1)S(1)}, u32[]{:S(2)}, u32[]{:S(2)}) collective-permute-start(bf16[8,7168]{1,0:T(8,128)(2,1)S(1)} %pass_rows.1), channel_id=1, source_target_pairs={{0,4},{1,5},{2,6},{3,7},{4,0},{5,1},{6,2},{7,3},{8,12},{9,13},{10,... | collective-permute-start | bytes 344072 | tf_op jit(solution)/shard_map/ppermute | solution.py:19
  12.5 0.0 collective-permute-start.8
  12.5 1.5 %collective-permute-start.5 = (bf16[8,7168]{1,0:T(8,128)(2,1)S(1)}, bf16[8,7168]{1,0:T(8,128)(2,1)S(1)}, u32[]{:S(2)}, u32[]{:S(2)}) collective-permute-start(bf16[8,7168]{1,0:T(8,128)(2,1)S(1)} %collective-permute-done.rows_ref.refs_2_), channel_id=1, source_target_pairs={{0,2},{1,3},{2,0},{3,1},{4,6},{5,7},{6,4},{7,5},{8,10},{9,11},{10,... | collective-permute-start | bytes 344072 | tf_op jit(solution)/shard_map/ppermute | solution.py:19
  14.0 0.0 collective-permute-done.3.refs_4_
  14.0 0.7 %collective-permute-start.4 = (bf16[8,7168]{1,0:T(8,128)(2,1)S(1)}, bf16[8,7168]{1,0:T(8,128)(2,1)S(1)}, u32[]{:S(2)}, u32[]{:S(2)}) collective-permute-start(bf16[8,7168]{1,0:T(8,128)(2,1)S(1)} %collective-permute-done.3.refs_4_), channel_id=1, source_target_pairs={{0,4},{1,5},{2,6},{3,7},{4,0},{5,1},{6,2},{7,3},{8,12},{9,13},{10,... | collective-permute-start | bytes 344072 | tf_op jit(solution)/shard_map/ppermute | solution.py:19
  14.7 0.0 collective-permute-done.7.refs_8_
  14.7 0.0 collective-permute-start.9
  14.7 1.2 %collective-permute-done.2.refs_3_ = bf16[8,7168]{1,0:T(8,128)(2,1)S(1)} collective-permute-done((bf16[8,7168]{1,0:T(8,128)(2,1)S(1)}, bf16[8,7168]{1,0:T(8,128)(2,1)S(1)}, u32[]{:S(2)}, u32[]{:S(2)}) %collective-permute-start.2) | collective-permute-done | bytes 114720 | tf_op jit(solution)/shard_map/ppermute | solution.py:19
  15.9 1.6 %collective-permute-start.6 = (bf16[8,7168]{1,0:T(8,128)(2,1)S(1)}, bf16[8,7168]{1,0:T(8,128)(2,1)S(1)}, u32[]{:S(2)}, u32[]{:S(2)}) collective-permute-start(bf16[8,7168]{1,0:T(8,128)(2,1)S(1)} %collective-permute-done.2.refs_3_), channel_id=1, source_target_pairs={{0,2},{1,3},{2,0},{3,1},{4,6},{5,7},{6,4},{7,5},{8,10},{9,11},{10,... | collective-permute-start | bytes 344072 | tf_op jit(solution)/shard_map/ppermute | solution.py:19
  17.5 0.0 collective-permute-done.8.refs_9_
  17.5 0.0 collective-permute-start.11
  17.5 0.7 %collective-permute-done.5.refs_6_ = bf16[8,7168]{1,0:T(8,128)(2,1)S(1)} collective-permute-done((bf16[8,7168]{1,0:T(8,128)(2,1)S(1)}, bf16[8,7168]{1,0:T(8,128)(2,1)S(1)}, u32[]{:S(2)}, u32[]{:S(2)}) %collective-permute-start.5) | collective-permute-done | bytes 114720 | tf_op jit(solution)/shard_map/ppermute | solution.py:19
  18.2 1.1 %collective-permute-done.4.refs_5_ = bf16[8,7168]{1,0:T(8,128)(2,1)S(1)} collective-permute-done((bf16[8,7168]{1,0:T(8,128)(2,1)S(1)}, bf16[8,7168]{1,0:T(8,128)(2,1)S(1)}, u32[]{:S(2)}, u32[]{:S(2)}) %collective-permute-start.4) | collective-permute-done | bytes 114720 | tf_op jit(solution)/shard_map/ppermute | solution.py:19
  19.3 0.5 %collective-permute-start.12 = (bf16[8,7168]{1,0:T(8,128)(2,1)S(1)}, bf16[8,7168]{1,0:T(8,128)(2,1)S(1)}, u32[]{:S(2)}, u32[]{:S(2)}) collective-permute-start(bf16[8,7168]{1,0:T(8,128)(2,1)S(1)} %collective-permute-done.4.refs_5_), channel_id=1, source_target_pairs={{0,1},{1,0},{2,3},{3,2},{4,5},{5,4},{6,7},{7,6},{8,9},{9,8},{10,11... | collective-permute-start | bytes 344072 | tf_op jit(solution)/shard_map/ppermute | solution.py:19
  19.8 0.9 %collective-permute-done.6.refs_7_ = bf16[8,7168]{1,0:T(8,128)(2,1)S(1)} collective-permute-done((bf16[8,7168]{1,0:T(8,128)(2,1)S(1)}, bf16[8,7168]{1,0:T(8,128)(2,1)S(1)}, u32[]{:S(2)}, u32[]{:S(2)}) %collective-permute-start.6) | collective-permute-done | bytes 114720 | tf_op jit(solution)/shard_map/ppermute | solution.py:19
  20.7 0.0 collective-permute-start.14
  20.7 0.0 collective-permute-done.11.refs_12_
  20.7 0.1 collective-permute-done.12.refs_13_
  20.8 1.2 %collective-permute-done.14.refs_15_ = bf16[8,7168]{1,0:T(8,128)(2,1)S(1)} collective-permute-done((bf16[8,7168]{1,0:T(8,128)(2,1)S(1)}, bf16[8,7168]{1,0:T(8,128)(2,1)S(1)}, u32[]{:S(2)}, u32[]{:S(2)}) %collective-permute-start.14) | collective-permute-done | bytes 114720 | tf_op jit(solution)/shard_map/ppermute | solution.py:19
  22.0 1.7 %expert_slice.1 = (bf16[64,7168]{1,0:T(8,128)(2,1)S(1)}, f32[64,7168]{1,0:T(8,128)S(1)}) custom-call(bf16[8,7168]{1,0:T(8,128)(2,1)S(1)} %reshape.14.refs_0_, bf16[8,7168]{1,0:T(8,128)(2,1)S(1)} %collective-permute-done.1.refs_1_, bf16[8,7168]{1,0:T(8,128)(2,1)S(1)} %collective-permute-done.rows_ref.refs_2_, ...), custom_call_target="tpu_custom_call" | custom-call | flops 1409286144 | bytes 11010048 | tf_op jit(solution)/shard_map/expert_slice/pallas_call | solution.py:64
  23.8 0.2 collective-permute-start.15
  24.0 2.3 %collective-permute-done.15.refs_0_ = bf16[64,7168]{1,0:T(8,128)(2,1)S(1)} collective-permute-done((bf16[64,7168]{1,0:T(8,128)(2,1)S(1)}, bf16[64,7168]{1,0:T(8,128)(2,1)S(1)}, u32[]{:S(2)}, u32[]{:S(2)}) %collective-permute-start.15) | collective-permute-done | bytes 917536 | tf_op jit(solution)/shard_map/ppermute | solution.py:19
  26.3 1.7 %collective-permute-start.21 = (bf16[8,7168]{1,0:T(8,128)(2,1)S(1)}, bf16[8,7168]{1,0:T(8,128)(2,1)S(1)}, u32[]{:S(2)}, u32[]{:S(2)}) collective-permute-start(bf16[8,7168]{1,0:T(8,128)(2,1)S(1)} %add_rows.14), channel_id=1, source_target_pairs={{0,2},{1,3},{2,0},{3,1},{4,6},{5,7},{6,4},{7,5},{8,10},{9,11},{10,... | collective-permute-start | bytes 344072 | tf_op jit(solution)/shard_map/ppermute | solution.py:19
  28.1 0.4 collective-permute-start.19
  28.5 1.7 %collective-permute-start.17 = (bf16[8,7168]{1,0:T(8,128)(2,1)S(1)}, bf16[8,7168]{1,0:T(8,128)(2,1)S(1)}, u32[]{:S(2)}, u32[]{:S(2)}) collective-permute-start(bf16[8,7168]{1,0:T(8,128)(2,1)S(1)} %add_rows.10), channel_id=1, source_target_pairs={{0,2},{1,3},{2,0},{3,1},{4,6},{5,7},{6,4},{7,5},{8,10},{9,11},{10,... | collective-permute-start | bytes 344072 | tf_op jit(solution)/shard_map/ppermute | solution.py:19
  30.3 0.4 collective-permute-start.16
  30.8 1.6 %collective-permute-done.21.refs_1_ = bf16[8,7168]{1,0:T(8,128)(2,1)S(1)} collective-permute-done((bf16[8,7168]{1,0:T(8,128)(2,1)S(1)}, bf16[8,7168]{1,0:T(8,128)(2,1)S(1)}, u32[]{:S(2)}, u32[]{:S(2)}) %collective-permute-start.21) | collective-permute-done | bytes 114720 | tf_op jit(solution)/shard_map/ppermute | solution.py:19
  32.4 0.0 copy-start.3
  32.4 4.0 %collective-permute-start.22 = (bf16[8,7168]{1,0:T(8,128)(2,1)S(1)}, bf16[8,7168]{1,0:T(8,128)(2,1)S(1)}, u32[]{:S(2)}, u32[]{:S(2)}) collective-permute-start(bf16[8,7168]{1,0:T(8,128)(2,1)S(1)} %add_rows.15), channel_id=1, source_target_pairs={{0,12},{1,13},{2,14},{3,15},{4,8},{5,9},{6,10},{7,11},{8,4},{9,5},... | collective-permute-start | bytes 344072 | tf_op jit(solution)/shard_map/ppermute | solution.py:19
  36.4 0.0 collective-permute-done.19.refs_1_
  36.4 0.8 %collective-permute-start.20 = (bf16[8,7168]{1,0:T(8,128)(2,1)S(1)}, bf16[8,7168]{1,0:T(8,128)(2,1)S(1)}, u32[]{:S(2)}, u32[]{:S(2)}) collective-permute-start(bf16[8,7168]{1,0:T(8,128)(2,1)S(1)} %add_rows.13), channel_id=1, source_target_pairs={{0,8},{1,9},{2,10},{3,11},{4,12},{5,13},{6,14},{7,15},{8,0},{9,1},... | collective-permute-start | bytes 344072 | tf_op jit(solution)/shard_map/ppermute | solution.py:19
  37.3 0.0 collective-permute-done.17.refs_1_
  37.3 2.2 %collective-permute-start.18 = (bf16[8,7168]{1,0:T(8,128)(2,1)S(1)}, bf16[8,7168]{1,0:T(8,128)(2,1)S(1)}, u32[]{:S(2)}, u32[]{:S(2)}) collective-permute-start(bf16[8,7168]{1,0:T(8,128)(2,1)S(1)} %add_rows.11), channel_id=1, source_target_pairs={{0,4},{1,5},{2,6},{3,7},{4,0},{5,1},{6,2},{7,3},{8,12},{9,13},{10,... | collective-permute-start | bytes 344072 | tf_op jit(solution)/shard_map/ppermute | solution.py:19
  39.5 0.1 select_reduce_fusion
  39.6 0.3 collective-permute-done.22.refs_3_
  40.0 5.3 %collective-permute-done.20.refs_2_ = bf16[8,7168]{1,0:T(8,128)(2,1)S(1)} collective-permute-done((bf16[8,7168]{1,0:T(8,128)(2,1)S(1)}, bf16[8,7168]{1,0:T(8,128)(2,1)S(1)}, u32[]{:S(2)}, u32[]{:S(2)}) %collective-permute-start.20) | collective-permute-done | bytes 114720 | tf_op jit(solution)/shard_map/ppermute | solution.py:19
  45.3 0.0 collective-permute-done.18.refs_1_
  45.3 0.8 %mix.1 = bf16[2,4,7168]{2,1,0:T(4,128)(2,1)} custom-call(f32[8,4]{1,0:T(8,128)S(1)} %bitcast.8, bf16[8,7168]{1,0:T(8,128)(2,1)S(1)} %add_rows.9.refs_0_, bf16[8,7168]{1,0:T(8,128)(2,1)S(1)} %collective-permute-done.18.refs_1_, bf16[8,7168]{1,0:T(8,128)(2,1)S(1)} %collective-permute-done.20.refs_2_, bf16[8,7168]{1,0:T(8,128)(2,1)S(1)} %collective-permute-done.22.refs_3_), custom_call_target="tpu_custom_call" | custom-call | tf_op jit(solution)/shard_map/mix/pallas_call | solution.py:127
  (23 shorter events, 0.3 us)
Async XLA Ops:
  0.9 21.1 %copy-start = (bf16[1,7168,256]{2,1,0:T(8,128)(2,1)S(1)}, bf16[1,7168,256]{2,1,0:T(8,128)(2,1)}, u32[]{:S(2)}) copy-start(bf16[1,7168,256]{2,1,0:T(8,128)(2,1)} %refs_0_.1) | copy-start | bytes 11010052
  0.9 21.1 %copy-start.1 = (bf16[1,7168,256]{2,1,0:T(8,128)(2,1)S(1)}, bf16[1,7168,256]{2,1,0:T(8,128)(2,1)}, u32[]{:S(2)}) copy-start(bf16[1,7168,256]{2,1,0:T(8,128)(2,1)} %refs_1_.1) | copy-start | bytes 11010052
  1.0 21.0 %copy-start.2 = (bf16[1,256,7168]{2,1,0:T(8,128)(2,1)S(1)}, bf16[1,256,7168]{2,1,0:T(8,128)(2,1)}, u32[]{:S(2)}) copy-start(bf16[1,256,7168]{2,1,0:T(8,128)(2,1)} %refs_2_.1) | copy-start | bytes 11010052
  1.0 9.8 %collective-permute-start = (bf16[8,7168]{1,0:T(8,128)(2,1)S(1)}, bf16[8,7168]{1,0:T(8,128)(2,1)S(1)}, u32[]{:S(2)}, u32[]{:S(2)}) collective-permute-start(bf16[8,7168]{1,0:T(8,128)(2,1)S(1)} %reshape.14.refs_0_), channel_id=1, source_target_pairs={{0,8},{1,9},{2,10},{3,11},{4,12},{5,13},{6,14},{7,15},{8,0},{9,1},... | collective-permute-start | bytes 344072 | tf_op jit(solution)/shard_map/ppermute | solution.py:19
  5.1 5.9 %collective-permute-start.1 = (bf16[8,7168]{1,0:T(8,128)(2,1)S(1)}, bf16[8,7168]{1,0:T(8,128)(2,1)S(1)}, u32[]{:S(2)}, u32[]{:S(2)}) collective-permute-start(bf16[8,7168]{1,0:T(8,128)(2,1)S(1)} %reshape.14.refs_0_), channel_id=1, source_target_pairs={{0,4},{1,5},{2,6},{3,7},{4,0},{5,1},{6,2},{7,3},{8,12},{9,13},{10,... | collective-permute-start | bytes 344072 | tf_op jit(solution)/shard_map/ppermute | solution.py:19
  6.6 7.4 %collective-permute-start.3 = (bf16[8,7168]{1,0:T(8,128)(2,1)S(1)}, bf16[8,7168]{1,0:T(8,128)(2,1)S(1)}, u32[]{:S(2)}, u32[]{:S(2)}) collective-permute-start(bf16[8,7168]{1,0:T(8,128)(2,1)S(1)} %reshape.14.refs_0_), channel_id=1, source_target_pairs={{0,2},{1,3},{2,0},{3,1},{4,6},{5,7},{6,4},{7,5},{8,10},{9,11},{10,... | collective-permute-start | bytes 344072 | tf_op jit(solution)/shard_map/ppermute | solution.py:19
  8.2 6.5 %collective-permute-start.7 = (bf16[8,7168]{1,0:T(8,128)(2,1)S(1)}, bf16[8,7168]{1,0:T(8,128)(2,1)S(1)}, u32[]{:S(2)}, u32[]{:S(2)}) collective-permute-start(bf16[8,7168]{1,0:T(8,128)(2,1)S(1)} %reshape.14.refs_0_), channel_id=1, source_target_pairs={{0,1},{1,0},{2,3},{3,2},{4,5},{5,4},{6,7},{7,6},{8,9},{9,8},{10,11... | collective-permute-start | bytes 344072 | tf_op jit(solution)/shard_map/ppermute | solution.py:19
  11.0 4.9 %collective-permute-start.2 = (bf16[8,7168]{1,0:T(8,128)(2,1)S(1)}, bf16[8,7168]{1,0:T(8,128)(2,1)S(1)}, u32[]{:S(2)}, u32[]{:S(2)}) collective-permute-start(bf16[8,7168]{1,0:T(8,128)(2,1)S(1)} %pass_rows.1), channel_id=1, source_target_pairs={{0,4},{1,5},{2,6},{3,7},{4,0},{5,1},{6,2},{7,3},{8,12},{9,13},{10,... | collective-permute-start | bytes 344072 | tf_op jit(solution)/shard_map/ppermute | solution.py:19
  12.5 5.0 %collective-permute-start.8 = (bf16[8,7168]{1,0:T(8,128)(2,1)S(1)}, bf16[8,7168]{1,0:T(8,128)(2,1)S(1)}, u32[]{:S(2)}, u32[]{:S(2)}) collective-permute-start(bf16[8,7168]{1,0:T(8,128)(2,1)S(1)} %collective-permute-done.1.refs_1_), channel_id=1, source_target_pairs={{0,1},{1,0},{2,3},{3,2},{4,5},{5,4},{6,7},{7,6},{8,9},{9,8},{10,11... | collective-permute-start | bytes 344072 | tf_op jit(solution)/shard_map/ppermute | solution.py:19
  12.5 5.7 %collective-permute-start.5 = (bf16[8,7168]{1,0:T(8,128)(2,1)S(1)}, bf16[8,7168]{1,0:T(8,128)(2,1)S(1)}, u32[]{:S(2)}, u32[]{:S(2)}) collective-permute-start(bf16[8,7168]{1,0:T(8,128)(2,1)S(1)} %collective-permute-done.rows_ref.refs_2_), channel_id=1, source_target_pairs={{0,2},{1,3},{2,0},{3,1},{4,6},{5,7},{6,4},{7,5},{8,10},{9,11},{10,... | collective-permute-start | bytes 344072 | tf_op jit(solution)/shard_map/ppermute | solution.py:19
  14.0 5.3 %collective-permute-start.4 = (bf16[8,7168]{1,0:T(8,128)(2,1)S(1)}, bf16[8,7168]{1,0:T(8,128)(2,1)S(1)}, u32[]{:S(2)}, u32[]{:S(2)}) collective-permute-start(bf16[8,7168]{1,0:T(8,128)(2,1)S(1)} %collective-permute-done.3.refs_4_), channel_id=1, source_target_pairs={{0,4},{1,5},{2,6},{3,7},{4,0},{5,1},{6,2},{7,3},{8,12},{9,13},{10,... | collective-permute-start | bytes 344072 | tf_op jit(solution)/shard_map/ppermute | solution.py:19
  14.7 4.6 %collective-permute-start.9 = (bf16[8,7168]{1,0:T(8,128)(2,1)S(1)}, bf16[8,7168]{1,0:T(8,128)(2,1)S(1)}, u32[]{:S(2)}, u32[]{:S(2)}) collective-permute-start(bf16[8,7168]{1,0:T(8,128)(2,1)S(1)} %collective-permute-done.rows_ref.refs_2_), channel_id=1, source_target_pairs={{0,1},{1,0},{2,3},{3,2},{4,5},{5,4},{6,7},{7,6},{8,9},{9,8},{10,11... | collective-permute-start | bytes 344072 | tf_op jit(solution)/shard_map/ppermute | solution.py:19
  15.9 4.8 %collective-permute-start.6 = (bf16[8,7168]{1,0:T(8,128)(2,1)S(1)}, bf16[8,7168]{1,0:T(8,128)(2,1)S(1)}, u32[]{:S(2)}, u32[]{:S(2)}) collective-permute-start(bf16[8,7168]{1,0:T(8,128)(2,1)S(1)} %collective-permute-done.2.refs_3_), channel_id=1, source_target_pairs={{0,2},{1,3},{2,0},{3,1},{4,6},{5,7},{6,4},{7,5},{8,10},{9,11},{10,... | collective-permute-start | bytes 344072 | tf_op jit(solution)/shard_map/ppermute | solution.py:19
  17.5 3.1 %collective-permute-start.11 = (bf16[8,7168]{1,0:T(8,128)(2,1)S(1)}, bf16[8,7168]{1,0:T(8,128)(2,1)S(1)}, u32[]{:S(2)}, u32[]{:S(2)}) collective-permute-start(bf16[8,7168]{1,0:T(8,128)(2,1)S(1)} %collective-permute-done.3.refs_4_), channel_id=1, source_target_pairs={{0,1},{1,0},{2,3},{3,2},{4,5},{5,4},{6,7},{7,6},{8,9},{9,8},{10,11... | collective-permute-start | bytes 344072 | tf_op jit(solution)/shard_map/ppermute | solution.py:19
  18.2 2.4 %collective-permute-start.10 = (bf16[8,7168]{1,0:T(8,128)(2,1)S(1)}, bf16[8,7168]{1,0:T(8,128)(2,1)S(1)}, u32[]{:S(2)}, u32[]{:S(2)}) collective-permute-start(bf16[8,7168]{1,0:T(8,128)(2,1)S(1)} %collective-permute-done.2.refs_3_), channel_id=1, source_target_pairs={{0,1},{1,0},{2,3},{3,2},{4,5},{5,4},{6,7},{7,6},{8,9},{9,8},{10,11... | collective-permute-start | bytes 344072 | tf_op jit(solution)/shard_map/ppermute | solution.py:19
  19.3 1.4 %collective-permute-start.13 = (bf16[8,7168]{1,0:T(8,128)(2,1)S(1)}, bf16[8,7168]{1,0:T(8,128)(2,1)S(1)}, u32[]{:S(2)}, u32[]{:S(2)}) collective-permute-start(bf16[8,7168]{1,0:T(8,128)(2,1)S(1)} %collective-permute-done.5.refs_6_), channel_id=1, source_target_pairs={{0,1},{1,0},{2,3},{3,2},{4,5},{5,4},{6,7},{7,6},{8,9},{9,8},{10,11... | collective-permute-start | bytes 344072 | tf_op jit(solution)/shard_map/ppermute | solution.py:19
  19.3 1.5 %collective-permute-start.12 = (bf16[8,7168]{1,0:T(8,128)(2,1)S(1)}, bf16[8,7168]{1,0:T(8,128)(2,1)S(1)}, u32[]{:S(2)}, u32[]{:S(2)}) collective-permute-start(bf16[8,7168]{1,0:T(8,128)(2,1)S(1)} %collective-permute-done.4.refs_5_), channel_id=1, source_target_pairs={{0,1},{1,0},{2,3},{3,2},{4,5},{5,4},{6,7},{7,6},{8,9},{9,8},{10,11... | collective-permute-start | bytes 344072 | tf_op jit(solution)/shard_map/ppermute | solution.py:19
  20.7 1.3 %collective-permute-start.14 = (bf16[8,7168]{1,0:T(8,128)(2,1)S(1)}, bf16[8,7168]{1,0:T(8,128)(2,1)S(1)}, u32[]{:S(2)}, u32[]{:S(2)}) collective-permute-start(bf16[8,7168]{1,0:T(8,128)(2,1)S(1)} %collective-permute-done.6.refs_7_), channel_id=1, source_target_pairs={{0,1},{1,0},{2,3},{3,2},{4,5},{5,4},{6,7},{7,6},{8,9},{9,8},{10,11... | collective-permute-start | bytes 344072 | tf_op jit(solution)/shard_map/ppermute | solution.py:19
  23.8 2.5 %collective-permute-start.15 = (bf16[64,7168]{1,0:T(8,128)(2,1)S(1)}, bf16[64,7168]{1,0:T(8,128)(2,1)S(1)}, u32[]{:S(2)}, u32[]{:S(2)}) collective-permute-start(bf16[64,7168]{1,0:T(8,128)(2,1)S(1)} %get-tuple-element.12), channel_id=1, source_target_pairs={{0,1},{1,0},{2,3},{3,2},{4,5},{5,4},{6,7},{7,6},{8,9},{9,8},{10,11... | collective-permute-start | bytes 2752520 | tf_op jit(solution)/shard_map/ppermute | solution.py:19
  26.3 3.9 %copy-start.4 = (f32[2,4,2]{1,2,0:T(2,128)S(1)}, f32[2,4,2]{1,2,0:T(2,128)}, u32[]{:S(2)}) copy-start(f32[2,4,2]{1,2,0:T(2,128)} %param.8) | copy-start | bytes 196
  26.3 6.1 %collective-permute-start.21 = (bf16[8,7168]{1,0:T(8,128)(2,1)S(1)}, bf16[8,7168]{1,0:T(8,128)(2,1)S(1)}, u32[]{:S(2)}, u32[]{:S(2)}) collective-permute-start(bf16[8,7168]{1,0:T(8,128)(2,1)S(1)} %add_rows.14), channel_id=1, source_target_pairs={{0,2},{1,3},{2,0},{3,1},{4,6},{5,7},{6,4},{7,5},{8,10},{9,11},{10,... | collective-permute-start | bytes 344072 | tf_op jit(solution)/shard_map/ppermute | solution.py:19
  28.1 8.3 %collective-permute-start.19 = (bf16[8,7168]{1,0:T(8,128)(2,1)S(1)}, bf16[8,7168]{1,0:T(8,128)(2,1)S(1)}, u32[]{:S(2)}, u32[]{:S(2)}) collective-permute-start(bf16[8,7168]{1,0:T(8,128)(2,1)S(1)} %add_rows.12), channel_id=1, source_target_pairs={{0,2},{1,3},{2,0},{3,1},{4,6},{5,7},{6,4},{7,5},{8,10},{9,11},{10,... | collective-permute-start | bytes 344072 | tf_op jit(solution)/shard_map/ppermute | solution.py:19
  28.5 8.8 %collective-permute-start.17 = (bf16[8,7168]{1,0:T(8,128)(2,1)S(1)}, bf16[8,7168]{1,0:T(8,128)(2,1)S(1)}, u32[]{:S(2)}, u32[]{:S(2)}) collective-permute-start(bf16[8,7168]{1,0:T(8,128)(2,1)S(1)} %add_rows.10), channel_id=1, source_target_pairs={{0,2},{1,3},{2,0},{3,1},{4,6},{5,7},{6,4},{7,5},{8,10},{9,11},{10,... | collective-permute-start | bytes 344072 | tf_op jit(solution)/shard_map/ppermute | solution.py:19
  30.3 9.3 %collective-permute-start.16 = (bf16[8,7168]{1,0:T(8,128)(2,1)S(1)}, bf16[8,7168]{1,0:T(8,128)(2,1)S(1)}, u32[]{:S(2)}, u32[]{:S(2)}) collective-permute-start(bf16[8,7168]{1,0:T(8,128)(2,1)S(1)} %add_rows.8), channel_id=1, source_target_pairs={{0,2},{1,3},{2,0},{3,1},{4,6},{5,7},{6,4},{7,5},{8,10},{9,11},{10,... | collective-permute-start | bytes 344072 | tf_op jit(solution)/shard_map/ppermute | solution.py:19
  32.4 7.1 %copy-start.3 = (s32[2,4,2]{1,2,0:T(2,128)S(1)}, s32[2,4,2]{1,2,0:T(2,128)}, u32[]{:S(2)}) copy-start(s32[2,4,2]{1,2,0:T(2,128)} %param.7) | copy-start | bytes 196
  32.4 7.6 %collective-permute-start.22 = (bf16[8,7168]{1,0:T(8,128)(2,1)S(1)}, bf16[8,7168]{1,0:T(8,128)(2,1)S(1)}, u32[]{:S(2)}, u32[]{:S(2)}) collective-permute-start(bf16[8,7168]{1,0:T(8,128)(2,1)S(1)} %add_rows.15), channel_id=1, source_target_pairs={{0,12},{1,13},{2,14},{3,15},{4,8},{5,9},{6,10},{7,11},{8,4},{9,5},... | collective-permute-start | bytes 344072 | tf_op jit(solution)/shard_map/ppermute | solution.py:19
  36.4 8.9 %collective-permute-start.20 = (bf16[8,7168]{1,0:T(8,128)(2,1)S(1)}, bf16[8,7168]{1,0:T(8,128)(2,1)S(1)}, u32[]{:S(2)}, u32[]{:S(2)}) collective-permute-start(bf16[8,7168]{1,0:T(8,128)(2,1)S(1)} %add_rows.13), channel_id=1, source_target_pairs={{0,8},{1,9},{2,10},{3,11},{4,12},{5,13},{6,14},{7,15},{8,0},{9,1},... | collective-permute-start | bytes 344072 | tf_op jit(solution)/shard_map/ppermute | solution.py:19
  37.3 8.0 %collective-permute-start.18 = (bf16[8,7168]{1,0:T(8,128)(2,1)S(1)}, bf16[8,7168]{1,0:T(8,128)(2,1)S(1)}, u32[]{:S(2)}, u32[]{:S(2)}) collective-permute-start(bf16[8,7168]{1,0:T(8,128)(2,1)S(1)} %add_rows.11), channel_id=1, source_target_pairs={{0,4},{1,5},{2,6},{3,7},{4,0},{5,1},{6,2},{7,3},{8,12},{9,13},{10,... | collective-permute-start | bytes 344072 | tf_op jit(solution)/shard_map/ppermute | solution.py:19

commit v4 on v3

--- a/solution.py
+++ b/solution.py
@@ -91,6 +91,24 @@
     )(rows, *[pltpu.with_memory_space_constraint(w, pltpu.HBM) for w in beside])
 
 
+def pack_kernel(*refs):
+    refs[-1][...] = jnp.concatenate([ref[step] for ref in refs[:-1] for step in range(ref.shape[0])], axis=0)
+
+
+def pack(blocks):
+    steps, tokens, features = blocks[0].shape
+    rows = len(blocks) * steps * tokens
+    return pl.pallas_call(
+        pack_kernel,
+        out_shape=jax.ShapeDtypeStruct((rows, features), blocks[0].dtype),
+        in_specs=[VMEM] * len(blocks),
+        out_specs=VMEM,
+        compiler_params=pltpu.CompilerParams(vmem_limit_bytes=16 * MIB),
+        cost_estimate=pl.CostEstimate(flops=0, bytes_accessed=4 * rows * features, transcendentals=0),
+        name="pack_rows",
+    )(*blocks)
+
+
 def add_kernel(size, places, keep_ref, *refs):
     terms, out_ref = refs[:-1], refs[-1]
     total = keep_ref[pl.ds(places[0] * size, size), :]
@@ -112,26 +130,24 @@
     )(keep, *terms)
 
 
-def mix_kernel(share_ref, *refs):
+def mix_kernel(fars, share_ref, *refs):
     backs, out_ref = refs[:-1], refs[-1]
     steps, tokens, _ = out_ref.shape
     share = share_ref[...]
-    total = share[:, 0:1] * backs[0][...].astype(jnp.float32)
-    for far in range(1, len(backs)):
-        total = total + share[:, far:far + 1] * backs[far][...].astype(jnp.float32)
+    total = sum(share[:, far:far + 1] * back[...].astype(jnp.float32) for far, back in zip(fars, backs))
     for step in range(steps):
         out_ref[step] = total[step * tokens:(step + 1) * tokens].astype(out_ref.dtype)
 
 
 def mix(share, backs, shape):
     return pl.pallas_call(
-        mix_kernel,
+        functools.partial(mix_kernel, tuple(backs)),
         out_shape=jax.ShapeDtypeStruct(shape, jnp.bfloat16),
         in_specs=[VMEM] * (1 + len(backs)),
         out_specs=VMEM,
         compiler_params=pltpu.CompilerParams(vmem_limit_bytes=16 * MIB),
         name="mix",
-    )(share, *backs)
+    )(share, *backs.values())
 
 
 def local(hidden, expert_ids, route_weight, w_gate, w_up, w_down):
@@ -143,31 +159,38 @@
     row_count = step_count * token_count
     own_expert = lax.axis_index("ep") // splits
 
-    own = hidden.reshape(row_count, features)
-    blocks = {0: own}
-    for key in sorted(range(1, devices), key=lambda key: (key.bit_count(), -key)):
+    blocks = {0: hidden}
+    for key in sorted(range(2, devices, 2), key=lambda key: (key.bit_count(), -key)):
         mask = splits if key == splits + 2 else key & -key
         block = blocks[key - mask]
         if key == devices // 2 + devices // 4:
             block, blocks[splits] = lax.optimization_barrier((block, blocks[splits]))
             block = pass_rows(block, w_gate, w_up, w_down)
         blocks[key] = swap(block, mask, devices)
-    order = [e * splits + y + c for c in (0, 1) for y in (0, 2) for e in range(experts)]
-    send, keep = expert_slice([blocks[k] for k in order], w_gate[0], w_up[0], w_down[0])
-
-    twin = swap(send, 1, devices)
-    across = {}
-    for far in reversed(range(experts)):
-        across[far] = swap(add_rows(row_count, (experts + far, experts + far), keep, twin), 2, devices)
+    last = devices - splits
+    batches = [
+        ([*range(0, last, splits), 2], range(splits + 2, last, splits)),
+        ([last, last + 2],),
+    ]
+
     backs = {}
-    for far in reversed(range(experts)):
-        rows = add_rows(row_count, (far, far, 0), keep, twin, across[far])
-        backs[far] = swap(rows, splits * far, devices) if far else rows
+    for batch in [[keys for batch in batches for keys in batch]]:
+        keep_rows = [pack([blocks[key] for key in keys]) for keys in batch]
+        send_rows = [swap(rows, 1, devices) for rows in keep_rows]
+        fars = [0, *range(3, experts), 1, 2]
+        send, keep = expert_slice(keep_rows + send_rows, w_gate[0], w_up[0], w_down[0])
+        twin = swap(send, 1, devices)
+        keys = [key for group in batch for key in group]
+        for far in reversed(fars):
+            theirs, mine = keys.index(far * splits + 2), keys.index(far * splits)
+            across = swap(add_rows(row_count, (theirs, theirs), keep, twin), 2, devices)
+            rows = add_rows(row_count, (mine, mine, 0), keep, twin, across)
+            backs[far] = swap(rows, splits * far, devices) if far else rows
 
     weights = route_scale * route_weight / jnp.sum(route_weight, axis=-1, keepdims=True)
     away = own_expert ^ jnp.arange(experts, dtype=jnp.int32)
     share = jnp.sum(jnp.where(expert_ids[..., None] == away, weights[..., None], 0.0), axis=-2)
-    return mix(share.reshape(row_count, experts), [backs[far] for far in range(experts)], hidden.shape)
+    return mix(share.reshape(row_count, experts), {far: backs[far] for far in fars}, hidden.shape)
 
 
 def solution(mesh):

time: 46.3 us -> 44.6 us (0.963)
  waiting for transfers between devices: 17.6 us -> 15.6 us
  local copies, waits for them, and re-layouts: 0.96 us -> 0.02 us
  starting transfers between devices: 24.5 us -> 25.4 us
    ppermute x23 -> x18, waiting for transfers between devices: 17.6 us -> 15.6 us  [swap(): return lax.ppermute(value, 'ep', [(i, i ^ mask) for i in range(devices)])]
    ppermute x23 -> x18, starting transfers between devices: 24.5 us -> 25.4 us  [swap(): return lax.ppermute(value, 'ep', [(i, i ^ mask) for i in range(devices)])]
    reshape x1 -> x0, local copies, waits for them, and re-layouts: 0.93 us -> none  [local(): own = hidden.reshape(row_count, features)]
    pallas_call x1 -> x4, Pallas kernels: 0.83 us -> 1.11 us  [the longest x1 0.83 us: mix(): pl.pallas_call(functools.partial(mix_kernel, tuple(backs)), out_shape=jax...]
  transfers between devices with their start and end apart: 23 -> 18, of which waited for: 12 -> 12; matrix products, arithmetic and copies ran while one was open for 0% -> 0% of each run, Pallas kernels for 1% -> 1%
where the time goes in v4:
time: 44.6 us; the launch traced here: 44.5 us
  starting transfers between devices  25.4 us (57%)
  waiting for transfers between devices  15.6 us (35%)
  Pallas kernels  3.1 us (7%)
    ppermute x18, starting transfers between devices, swap(): return lax.ppermute(value, 'ep', [(i, i ^ mask) for i in range(devices)])  25.4 us
    ppermute x18, waiting for transfers between devices, swap(): return lax.ppermute(value, 'ep', [(i, i ^ mask) for i in range(devices)])  15.6 us
    pallas_call x1, Pallas kernels, expert_slice(): pl.pallas_call(functools.partial(expert_kernel, len(blocks)), out_shape=(...  1.74 us
  transfers between devices with their start and end apart: 18, of which 12 were waited for; matrix products, arithmetic and copies ran while one was open for 0% of the time, Pallas kernels for 1%

profile of v4, /device:TPU:0, one launch (start us, length us, event | category | flops | bytes accessed | tf_op | source)
XLA Modules:
  0.0 44.5 jit_solution(8882126689862228383)
XLA Ops:
  0.0 4.0 %collective-permute-start = (bf16[2,4,7168]{2,1,0:T(4,128)(2,1)}, bf16[2,4,7168]{2,1,0:T(4,128)(2,1)S(1)}, u32[]{:S(2)}, u32[]{:S(2)}) collective-permute-start(bf16[2,4,7168]{2,1,0:T(4,128)(2,1)} %refs_0_.2), channel_id=1, source_target_pairs={{0,8},{1,9},{2,10},{3,11},{4,12},{5,13},{6,14},{7,15},{8,0},{9,1},... | collective-permute-start | bytes 344072 | tf_op jit(solution)/shard_map/ppermute | solution.py:19
  4.0 1.6 %collective-permute-start.1 = (bf16[2,4,7168]{2,1,0:T(4,128)(2,1)}, bf16[2,4,7168]{2,1,0:T(4,128)(2,1)S(1)}, u32[]{:S(2)}, u32[]{:S(2)}) collective-permute-start(bf16[2,4,7168]{2,1,0:T(4,128)(2,1)} %refs_0_.2), channel_id=1, source_target_pairs={{0,4},{1,5},{2,6},{3,7},{4,0},{5,1},{6,2},{7,3},{8,12},{9,13},{10,... | collective-permute-start | bytes 344072 | tf_op jit(solution)/shard_map/ppermute | solution.py:19
  5.6 1.5 %collective-permute-start.2 = (bf16[2,4,7168]{2,1,0:T(4,128)(2,1)}, bf16[2,4,7168]{2,1,0:T(4,128)(2,1)S(1)}, u32[]{:S(2)}, u32[]{:S(2)}) collective-permute-start(bf16[2,4,7168]{2,1,0:T(4,128)(2,1)} %refs_0_.2), channel_id=1, source_target_pairs={{0,2},{1,3},{2,0},{3,1},{4,6},{5,7},{6,4},{7,5},{8,10},{9,11},{10,... | collective-permute-start | bytes 344072 | tf_op jit(solution)/shard_map/ppermute | solution.py:19
  7.1 2.9 %collective-permute-done.refs_2_.rows_ref = bf16[2,4,7168]{2,1,0:T(4,128)(2,1)S(1)} collective-permute-done((bf16[2,4,7168]{2,1,0:T(4,128)(2,1)}, bf16[2,4,7168]{2,1,0:T(4,128)(2,1)S(1)}, u32[]{:S(2)}, u32[]{:S(2)}) %collective-permute-start) | collective-permute-done | bytes 114720 | tf_op jit(solution)/shard_map/ppermute | solution.py:19
  10.0 0.2 collective-permute-done.1.refs_1_
  10.3 1.4 %collective-permute-start.5 = (bf16[2,4,7168]{2,1,0:T(4,128)(2,1)S(1)}, bf16[2,4,7168]{2,1,0:T(4,128)(2,1)S(1)}, u32[]{:S(2)}, u32[]{:S(2)}) collective-permute-start(bf16[2,4,7168]{2,1,0:T(4,128)(2,1)S(1)} %pass_rows.1), channel_id=1, source_target_pairs={{0,4},{1,5},{2,6},{3,7},{4,0},{5,1},{6,2},{7,3},{8,12},{9,13},{10,... | collective-permute-start | bytes 344072 | tf_op jit(solution)/shard_map/ppermute | solution.py:19
  11.7 0.0 collective-permute-done.2.refs_3_
  11.7 0.0 copy-done.3
  11.7 0.1 pack_rows.3.refs_0_
  11.8 0.1 collective-permute-start.7
  11.9 1.6 %collective-permute-start.4 = (bf16[2,4,7168]{2,1,0:T(4,128)(2,1)S(1)}, bf16[2,4,7168]{2,1,0:T(4,128)(2,1)S(1)}, u32[]{:S(2)}, u32[]{:S(2)}) collective-permute-start(bf16[2,4,7168]{2,1,0:T(4,128)(2,1)S(1)} %collective-permute-done.refs_2_.rows_ref), channel_id=1, source_target_pairs={{0,2},{1,3},{2,0},{3,1},{4,6},{5,7},{6,4},{7,5},{8,10},{9,11},{10,... | collective-permute-start | bytes 344072 | tf_op jit(solution)/shard_map/ppermute | solution.py:19
  13.5 0.7 %collective-permute-start.3 = (bf16[2,4,7168]{2,1,0:T(4,128)(2,1)S(1)}, bf16[2,4,7168]{2,1,0:T(4,128)(2,1)S(1)}, u32[]{:S(2)}, u32[]{:S(2)}) collective-permute-start(bf16[2,4,7168]{2,1,0:T(4,128)(2,1)S(1)} %collective-permute-done.2.refs_3_), channel_id=1, source_target_pairs={{0,4},{1,5},{2,6},{3,7},{4,0},{5,1},{6,2},{7,3},{8,12},{9,13},{10,... | collective-permute-start | bytes 344072 | tf_op jit(solution)/shard_map/ppermute | solution.py:19
  14.2 0.9 %collective-permute-done.5.refs_0_ = bf16[2,4,7168]{2,1,0:T(4,128)(2,1)S(1)} collective-permute-done((bf16[2,4,7168]{2,1,0:T(4,128)(2,1)S(1)}, bf16[2,4,7168]{2,1,0:T(4,128)(2,1)S(1)}, u32[]{:S(2)}, u32[]{:S(2)}) %collective-permute-start.5) | collective-permute-done | bytes 114720 | tf_op jit(solution)/shard_map/ppermute | solution.py:19
  15.1 1.5 %collective-permute-start.6 = (bf16[2,4,7168]{2,1,0:T(4,128)(2,1)S(1)}, bf16[2,4,7168]{2,1,0:T(4,128)(2,1)S(1)}, u32[]{:S(2)}, u32[]{:S(2)}) collective-permute-start(bf16[2,4,7168]{2,1,0:T(4,128)(2,1)S(1)} %collective-permute-done.5.refs_0_), channel_id=1, source_target_pairs={{0,2},{1,3},{2,0},{3,1},{4,6},{5,7},{6,4},{7,5},{8,10},{9,11},{10,... | collective-permute-start | bytes 344072 | tf_op jit(solution)/shard_map/ppermute | solution.py:19
  16.6 1.3 %collective-permute-done.4.refs_1_ = bf16[2,4,7168]{2,1,0:T(4,128)(2,1)S(1)} collective-permute-done((bf16[2,4,7168]{2,1,0:T(4,128)(2,1)S(1)}, bf16[2,4,7168]{2,1,0:T(4,128)(2,1)S(1)}, u32[]{:S(2)}, u32[]{:S(2)}) %collective-permute-start.4) | collective-permute-done | bytes 114720 | tf_op jit(solution)/shard_map/ppermute | solution.py:19
  17.9 0.8 %collective-permute-done.3.refs_0_ = bf16[2,4,7168]{2,1,0:T(4,128)(2,1)S(1)} collective-permute-done((bf16[2,4,7168]{2,1,0:T(4,128)(2,1)S(1)}, bf16[2,4,7168]{2,1,0:T(4,128)(2,1)S(1)}, u32[]{:S(2)}, u32[]{:S(2)}) %collective-permute-start.3) | collective-permute-done | bytes 114720 | tf_op jit(solution)/shard_map/ppermute | solution.py:19
  18.7 0.1 pack_rows.4.refs_1_
  18.8 0.1 collective-permute-start.8
  18.9 1.1 %collective-permute-done.6.refs_1_ = bf16[2,4,7168]{2,1,0:T(4,128)(2,1)S(1)} collective-permute-done((bf16[2,4,7168]{2,1,0:T(4,128)(2,1)S(1)}, bf16[2,4,7168]{2,1,0:T(4,128)(2,1)S(1)}, u32[]{:S(2)}, u32[]{:S(2)}) %collective-permute-start.6) | collective-permute-done | bytes 114720 | tf_op jit(solution)/shard_map/ppermute | solution.py:19
  19.9 0.1 pack_rows.5.refs_2_
  20.0 0.1 collective-permute-start.9
  20.1 0.3 collective-permute-done.8.refs_4_
  20.3 1.2 %collective-permute-done.9.refs_5_ = bf16[16,7168]{1,0:T(8,128)(2,1)S(1)} collective-permute-done((bf16[16,7168]{1,0:T(8,128)(2,1)S(1)}, bf16[16,7168]{1,0:T(8,128)(2,1)S(1)}, u32[]{:S(2)}, u32[]{:S(2)}) %collective-permute-start.9) | collective-permute-done | bytes 229408 | tf_op jit(solution)/shard_map/ppermute | solution.py:19
  21.6 0.0 collective-permute-done.7.refs_3_
  21.6 0.0 copy-done
  21.6 0.0 copy-done.1
  21.6 0.0 copy-done.2
  21.6 1.7 %expert_slice.1 = (bf16[64,7168]{1,0:T(8,128)(2,1)S(1)}, f32[64,7168]{1,0:T(8,128)S(1)}) custom-call(bf16[32,7168]{1,0:T(8,128)(2,1)S(1)} %pack_rows.3.refs_0_, bf16[16,7168]{1,0:T(8,128)(2,1)S(1)} %pack_rows.4.refs_1_, bf16[16,7168]{1,0:T(8,128)(2,1)S(1)} %pack_rows.5.refs_2_, bf16[32,7168]{1,0:T(8,128)(2,1)S(1)} %collective-permute-done.7.refs_3_, ...), custom_call_target="tpu_custom_call" | custom-call | flops 1409286144 | bytes 11010048 | tf_op jit(solution)/shard_map/expert_slice/pallas_call | solution.py:64
  23.3 0.2 collective-permute-start.10
  23.5 2.3 %collective-permute-done.10.refs_0_ = bf16[64,7168]{1,0:T(8,128)(2,1)S(1)} collective-permute-done((bf16[64,7168]{1,0:T(8,128)(2,1)S(1)}, bf16[64,7168]{1,0:T(8,128)(2,1)S(1)}, u32[]{:S(2)}, u32[]{:S(2)}) %collective-permute-start.10) | collective-permute-done | bytes 917536 | tf_op jit(solution)/shard_map/ppermute | solution.py:19
  25.9 1.6 %collective-permute-start.16 = (bf16[8,7168]{1,0:T(8,128)(2,1)S(1)}, bf16[8,7168]{1,0:T(8,128)(2,1)S(1)}, u32[]{:S(2)}, u32[]{:S(2)}) collective-permute-start(bf16[8,7168]{1,0:T(8,128)(2,1)S(1)} %add_rows.14), channel_id=1, source_target_pairs={{0,2},{1,3},{2,0},{3,1},{4,6},{5,7},{6,4},{7,5},{8,10},{9,11},{10,... | collective-permute-start | bytes 344072 | tf_op jit(solution)/shard_map/ppermute | solution.py:19
  27.5 0.6 %collective-permute-start.14 = (bf16[8,7168]{1,0:T(8,128)(2,1)S(1)}, bf16[8,7168]{1,0:T(8,128)(2,1)S(1)}, u32[]{:S(2)}, u32[]{:S(2)}) collective-permute-start(bf16[8,7168]{1,0:T(8,128)(2,1)S(1)} %add_rows.12), channel_id=1, source_target_pairs={{0,2},{1,3},{2,0},{3,1},{4,6},{5,7},{6,4},{7,5},{8,10},{9,11},{10,... | collective-permute-start | bytes 344072 | tf_op jit(solution)/shard_map/ppermute | solution.py:19
  28.1 1.6 %collective-permute-start.12 = (bf16[8,7168]{1,0:T(8,128)(2,1)S(1)}, bf16[8,7168]{1,0:T(8,128)(2,1)S(1)}, u32[]{:S(2)}, u32[]{:S(2)}) collective-permute-start(bf16[8,7168]{1,0:T(8,128)(2,1)S(1)} %add_rows.10), channel_id=1, source_target_pairs={{0,2},{1,3},{2,0},{3,1},{4,6},{5,7},{6,4},{7,5},{8,10},{9,11},{10,... | collective-permute-start | bytes 344072 | tf_op jit(solution)/shard_map/ppermute | solution.py:19
  29.8 0.6 %collective-permute-start.11 = (bf16[8,7168]{1,0:T(8,128)(2,1)S(1)}, bf16[8,7168]{1,0:T(8,128)(2,1)S(1)}, u32[]{:S(2)}, u32[]{:S(2)}) collective-permute-start(bf16[8,7168]{1,0:T(8,128)(2,1)S(1)} %add_rows.8), channel_id=1, source_target_pairs={{0,2},{1,3},{2,0},{3,1},{4,6},{5,7},{6,4},{7,5},{8,10},{9,11},{10,... | collective-permute-start | bytes 344072 | tf_op jit(solution)/shard_map/ppermute | solution.py:19
  30.3 1.6 %collective-permute-done.16.refs_1_ = bf16[8,7168]{1,0:T(8,128)(2,1)S(1)} collective-permute-done((bf16[8,7168]{1,0:T(8,128)(2,1)S(1)}, bf16[8,7168]{1,0:T(8,128)(2,1)S(1)}, u32[]{:S(2)}, u32[]{:S(2)}) %collective-permute-start.16) | collective-permute-done | bytes 114720 | tf_op jit(solution)/shard_map/ppermute | solution.py:19
  32.0 0.0 copy-start.4
  32.0 2.4 %collective-permute-start.17 = (bf16[8,7168]{1,0:T(8,128)(2,1)S(1)}, bf16[8,7168]{1,0:T(8,128)(2,1)S(1)}, u32[]{:S(2)}, u32[]{:S(2)}) collective-permute-start(bf16[8,7168]{1,0:T(8,128)(2,1)S(1)} %add_rows.15), channel_id=1, source_target_pairs={{0,8},{1,9},{2,10},{3,11},{4,12},{5,13},{6,14},{7,15},{8,0},{9,1},... | collective-permute-start | bytes 344072 | tf_op jit(solution)/shard_map/ppermute | solution.py:19
  34.4 0.0 collective-permute-done.14.refs_1_
  34.5 2.1 %collective-permute-start.15 = (bf16[8,7168]{1,0:T(8,128)(2,1)S(1)}, bf16[8,7168]{1,0:T(8,128)(2,1)S(1)}, u32[]{:S(2)}, u32[]{:S(2)}) collective-permute-start(bf16[8,7168]{1,0:T(8,128)(2,1)S(1)} %add_rows.13), channel_id=1, source_target_pairs={{0,4},{1,5},{2,6},{3,7},{4,0},{5,1},{6,2},{7,3},{8,12},{9,13},{10,... | collective-permute-start | bytes 344072 | tf_op jit(solution)/shard_map/ppermute | solution.py:19
  36.6 0.3 collective-permute-done.12.refs_1_
  36.9 3.9 %collective-permute-start.13 = (bf16[8,7168]{1,0:T(8,128)(2,1)S(1)}, bf16[8,7168]{1,0:T(8,128)(2,1)S(1)}, u32[]{:S(2)}, u32[]{:S(2)}) collective-permute-start(bf16[8,7168]{1,0:T(8,128)(2,1)S(1)} %add_rows.11), channel_id=1, source_target_pairs={{0,12},{1,13},{2,14},{3,15},{4,8},{5,9},{6,10},{7,11},{8,4},{9,5},... | collective-permute-start | bytes 344072 | tf_op jit(solution)/shard_map/ppermute | solution.py:19
  40.8 0.0 copy-done.4
  40.8 0.1 select_reduce_fusion
  40.9 0.0 collective-permute-done.11.refs_1_
  40.9 0.0 collective-permute-done.17.refs_3_
  40.9 0.0 collective-permute-done.15.refs_2_
  40.9 2.7 %collective-permute-done.13.refs_1_ = bf16[8,7168]{1,0:T(8,128)(2,1)S(1)} collective-permute-done((bf16[8,7168]{1,0:T(8,128)(2,1)S(1)}, bf16[8,7168]{1,0:T(8,128)(2,1)S(1)}, u32[]{:S(2)}, u32[]{:S(2)}) %collective-permute-start.13) | collective-permute-done | bytes 114720 | tf_op jit(solution)/shard_map/ppermute | solution.py:19
  43.6 0.8 %mix.1 = bf16[2,4,7168]{2,1,0:T(4,128)(2,1)} custom-call(f32[8,4]{1,0:T(8,128)S(1)} %bitcast.8, bf16[8,7168]{1,0:T(8,128)(2,1)S(1)} %add_rows.9.refs_0_, bf16[8,7168]{1,0:T(8,128)(2,1)S(1)} %collective-permute-done.13.refs_1_, bf16[8,7168]{1,0:T(8,128)(2,1)S(1)} %collective-permute-done.15.refs_2_, bf16[8,7168]{1,0:T(8,128)(2,1)S(1)} %collective-permute-done.17.refs_3_), custom_call_target="tpu_custom_call" | custom-call | tf_op jit(solution)/shard_map/mix/pallas_call | solution.py:143
  (17 shorter events, 0.3 us)
Async XLA Ops:
  0.0 11.7 %copy-start.3 = (bf16[2,4,7168]{2,1,0:T(4,128)(2,1)S(1)}, bf16[2,4,7168]{2,1,0:T(4,128)(2,1)}, u32[]{:S(2)}) copy-start(bf16[2,4,7168]{2,1,0:T(4,128)(2,1)} %refs_0_.2) | copy-start | bytes 344068
  0.0 10.0 %collective-permute-start = (bf16[2,4,7168]{2,1,0:T(4,128)(2,1)}, bf16[2,4,7168]{2,1,0:T(4,128)(2,1)S(1)}, u32[]{:S(2)}, u32[]{:S(2)}) collective-permute-start(bf16[2,4,7168]{2,1,0:T(4,128)(2,1)} %refs_0_.2), channel_id=1, source_target_pairs={{0,8},{1,9},{2,10},{3,11},{4,12},{5,13},{6,14},{7,15},{8,0},{9,1},... | collective-permute-start | bytes 344072 | tf_op jit(solution)/shard_map/ppermute | solution.py:19
  4.0 6.2 %collective-permute-start.1 = (bf16[2,4,7168]{2,1,0:T(4,128)(2,1)}, bf16[2,4,7168]{2,1,0:T(4,128)(2,1)S(1)}, u32[]{:S(2)}, u32[]{:S(2)}) collective-permute-start(bf16[2,4,7168]{2,1,0:T(4,128)(2,1)} %refs_0_.2), channel_id=1, source_target_pairs={{0,4},{1,5},{2,6},{3,7},{4,0},{5,1},{6,2},{7,3},{8,12},{9,13},{10,... | collective-permute-start | bytes 344072 | tf_op jit(solution)/shard_map/ppermute | solution.py:19
  5.6 6.1 %collective-permute-start.2 = (bf16[2,4,7168]{2,1,0:T(4,128)(2,1)}, bf16[2,4,7168]{2,1,0:T(4,128)(2,1)S(1)}, u32[]{:S(2)}, u32[]{:S(2)}) collective-permute-start(bf16[2,4,7168]{2,1,0:T(4,128)(2,1)} %refs_0_.2), channel_id=1, source_target_pairs={{0,2},{1,3},{2,0},{3,1},{4,6},{5,7},{6,4},{7,5},{8,10},{9,11},{10,... | collective-permute-start | bytes 344072 | tf_op jit(solution)/shard_map/ppermute | solution.py:19
  10.3 11.3 %copy-start = (bf16[1,7168,256]{2,1,0:T(8,128)(2,1)S(1)}, bf16[1,7168,256]{2,1,0:T(8,128)(2,1)}, u32[]{:S(2)}) copy-start(bf16[1,7168,256]{2,1,0:T(8,128)(2,1)} %refs_0_.3) | copy-start | bytes 11010052
  10.3 11.3 %copy-start.1 = (bf16[1,7168,256]{2,1,0:T(8,128)(2,1)S(1)}, bf16[1,7168,256]{2,1,0:T(8,128)(2,1)}, u32[]{:S(2)}) copy-start(bf16[1,7168,256]{2,1,0:T(8,128)(2,1)} %refs_1_.1) | copy-start | bytes 11010052
  10.3 11.3 %copy-start.2 = (bf16[1,256,7168]{2,1,0:T(8,128)(2,1)S(1)}, bf16[1,256,7168]{2,1,0:T(8,128)(2,1)}, u32[]{:S(2)}) copy-start(bf16[1,256,7168]{2,1,0:T(8,128)(2,1)} %refs_2_.1) | copy-start | bytes 11010052
  10.3 4.9 %collective-permute-start.5 = (bf16[2,4,7168]{2,1,0:T(4,128)(2,1)S(1)}, bf16[2,4,7168]{2,1,0:T(4,128)(2,1)S(1)}, u32[]{:S(2)}, u32[]{:S(2)}) collective-permute-start(bf16[2,4,7168]{2,1,0:T(4,128)(2,1)S(1)} %pass_rows.1), channel_id=1, source_target_pairs={{0,4},{1,5},{2,6},{3,7},{4,0},{5,1},{6,2},{7,3},{8,12},{9,13},{10,... | collective-permute-start | bytes 344072 | tf_op jit(solution)/shard_map/ppermute | solution.py:19
  11.8 9.7 %collective-permute-start.7 = (bf16[32,7168]{1,0:T(8,128)(2,1)S(1)}, bf16[32,7168]{1,0:T(8,128)(2,1)S(1)}, u32[]{:S(2)}, u32[]{:S(2)}) collective-permute-start(bf16[32,7168]{1,0:T(8,128)(2,1)S(1)} %pack_rows.3.refs_0_), channel_id=1, source_target_pairs={{0,1},{1,0},{2,3},{3,2},{4,5},{5,4},{6,7},{7,6},{8,9},{9,8},{10,11... | collective-permute-start | bytes 1376264 | tf_op jit(solution)/shard_map/ppermute | solution.py:19
  11.9 6.0 %collective-permute-start.4 = (bf16[2,4,7168]{2,1,0:T(4,128)(2,1)S(1)}, bf16[2,4,7168]{2,1,0:T(4,128)(2,1)S(1)}, u32[]{:S(2)}, u32[]{:S(2)}) collective-permute-start(bf16[2,4,7168]{2,1,0:T(4,128)(2,1)S(1)} %collective-permute-done.refs_2_.rows_ref), channel_id=1, source_target_pairs={{0,2},{1,3},{2,0},{3,1},{4,6},{5,7},{6,4},{7,5},{8,10},{9,11},{10,... | collective-permute-start | bytes 344072 | tf_op jit(solution)/shard_map/ppermute | solution.py:19
  13.5 5.2 %collective-permute-start.3 = (bf16[2,4,7168]{2,1,0:T(4,128)(2,1)S(1)}, bf16[2,4,7168]{2,1,0:T(4,128)(2,1)S(1)}, u32[]{:S(2)}, u32[]{:S(2)}) collective-permute-start(bf16[2,4,7168]{2,1,0:T(4,128)(2,1)S(1)} %collective-permute-done.2.refs_3_), channel_id=1, source_target_pairs={{0,4},{1,5},{2,6},{3,7},{4,0},{5,1},{6,2},{7,3},{8,12},{9,13},{10,... | collective-permute-start | bytes 344072 | tf_op jit(solution)/shard_map/ppermute | solution.py:19
  15.1 4.8 %collective-permute-start.6 = (bf16[2,4,7168]{2,1,0:T(4,128)(2,1)S(1)}, bf16[2,4,7168]{2,1,0:T(4,128)(2,1)S(1)}, u32[]{:S(2)}, u32[]{:S(2)}) collective-permute-start(bf16[2,4,7168]{2,1,0:T(4,128)(2,1)S(1)} %collective-permute-done.5.refs_0_), channel_id=1, source_target_pairs={{0,2},{1,3},{2,0},{3,1},{4,6},{5,7},{6,4},{7,5},{8,10},{9,11},{10,... | collective-permute-start | bytes 344072 | tf_op jit(solution)/shard_map/ppermute | solution.py:19
  18.8 1.6 %collective-permute-start.8 = (bf16[16,7168]{1,0:T(8,128)(2,1)S(1)}, bf16[16,7168]{1,0:T(8,128)(2,1)S(1)}, u32[]{:S(2)}, u32[]{:S(2)}) collective-permute-start(bf16[16,7168]{1,0:T(8,128)(2,1)S(1)} %pack_rows.4.refs_1_), channel_id=1, source_target_pairs={{0,1},{1,0},{2,3},{3,2},{4,5},{5,4},{6,7},{7,6},{8,9},{9,8},{10,11... | collective-permute-start | bytes 688136 | tf_op jit(solution)/shard_map/ppermute | solution.py:19
  20.0 1.6 %collective-permute-start.9 = (bf16[16,7168]{1,0:T(8,128)(2,1)S(1)}, bf16[16,7168]{1,0:T(8,128)(2,1)S(1)}, u32[]{:S(2)}, u32[]{:S(2)}) collective-permute-start(bf16[16,7168]{1,0:T(8,128)(2,1)S(1)} %pack_rows.5.refs_2_), channel_id=1, source_target_pairs={{0,1},{1,0},{2,3},{3,2},{4,5},{5,4},{6,7},{7,6},{8,9},{9,8},{10,11... | collective-permute-start | bytes 688136 | tf_op jit(solution)/shard_map/ppermute | solution.py:19
  23.3 2.5 %collective-permute-start.10 = (bf16[64,7168]{1,0:T(8,128)(2,1)S(1)}, bf16[64,7168]{1,0:T(8,128)(2,1)S(1)}, u32[]{:S(2)}, u32[]{:S(2)}) collective-permute-start(bf16[64,7168]{1,0:T(8,128)(2,1)S(1)} %get-tuple-element.12), channel_id=1, source_target_pairs={{0,1},{1,0},{2,3},{3,2},{4,5},{5,4},{6,7},{7,6},{8,9},{9,8},{10,11... | collective-permute-start | bytes 2752520 | tf_op jit(solution)/shard_map/ppermute | solution.py:19
  25.9 3.8 %copy-start.5 = (f32[2,4,2]{1,2,0:T(2,128)S(1)}, f32[2,4,2]{1,2,0:T(2,128)}, u32[]{:S(2)}) copy-start(f32[2,4,2]{1,2,0:T(2,128)} %param.8) | copy-start | bytes 196
  25.9 6.1 %collective-permute-start.16 = (bf16[8,7168]{1,0:T(8,128)(2,1)S(1)}, bf16[8,7168]{1,0:T(8,128)(2,1)S(1)}, u32[]{:S(2)}, u32[]{:S(2)}) collective-permute-start(bf16[8,7168]{1,0:T(8,128)(2,1)S(1)} %add_rows.14), channel_id=1, source_target_pairs={{0,2},{1,3},{2,0},{3,1},{4,6},{5,7},{6,4},{7,5},{8,10},{9,11},{10,... | collective-permute-start | bytes 344072 | tf_op jit(solution)/shard_map/ppermute | solution.py:19
  27.5 6.9 %collective-permute-start.14 = (bf16[8,7168]{1,0:T(8,128)(2,1)S(1)}, bf16[8,7168]{1,0:T(8,128)(2,1)S(1)}, u32[]{:S(2)}, u32[]{:S(2)}) collective-permute-start(bf16[8,7168]{1,0:T(8,128)(2,1)S(1)} %add_rows.12), channel_id=1, source_target_pairs={{0,2},{1,3},{2,0},{3,1},{4,6},{5,7},{6,4},{7,5},{8,10},{9,11},{10,... | collective-permute-start | bytes 344072 | tf_op jit(solution)/shard_map/ppermute | solution.py:19
  28.1 8.8 %collective-permute-start.12 = (bf16[8,7168]{1,0:T(8,128)(2,1)S(1)}, bf16[8,7168]{1,0:T(8,128)(2,1)S(1)}, u32[]{:S(2)}, u32[]{:S(2)}) collective-permute-start(bf16[8,7168]{1,0:T(8,128)(2,1)S(1)} %add_rows.10), channel_id=1, source_target_pairs={{0,2},{1,3},{2,0},{3,1},{4,6},{5,7},{6,4},{7,5},{8,10},{9,11},{10,... | collective-permute-start | bytes 344072 | tf_op jit(solution)/shard_map/ppermute | solution.py:19
  29.8 11.1 %collective-permute-start.11 = (bf16[8,7168]{1,0:T(8,128)(2,1)S(1)}, bf16[8,7168]{1,0:T(8,128)(2,1)S(1)}, u32[]{:S(2)}, u32[]{:S(2)}) collective-permute-start(bf16[8,7168]{1,0:T(8,128)(2,1)S(1)} %add_rows.8), channel_id=1, source_target_pairs={{0,2},{1,3},{2,0},{3,1},{4,6},{5,7},{6,4},{7,5},{8,10},{9,11},{10,... | collective-permute-start | bytes 344072 | tf_op jit(solution)/shard_map/ppermute | solution.py:19
  32.0 8.8 %copy-start.4 = (s32[2,4,2]{1,2,0:T(2,128)S(1)}, s32[2,4,2]{1,2,0:T(2,128)}, u32[]{:S(2)}) copy-start(s32[2,4,2]{1,2,0:T(2,128)} %param.7) | copy-start | bytes 196
  32.0 8.9 %collective-permute-start.17 = (bf16[8,7168]{1,0:T(8,128)(2,1)S(1)}, bf16[8,7168]{1,0:T(8,128)(2,1)S(1)}, u32[]{:S(2)}, u32[]{:S(2)}) collective-permute-start(bf16[8,7168]{1,0:T(8,128)(2,1)S(1)} %add_rows.15), channel_id=1, source_target_pairs={{0,8},{1,9},{2,10},{3,11},{4,12},{5,13},{6,14},{7,15},{8,0},{9,1},... | collective-permute-start | bytes 344072 | tf_op jit(solution)/shard_map/ppermute | solution.py:19
  34.5 6.4 %collective-permute-start.15 = (bf16[8,7168]{1,0:T(8,128)(2,1)S(1)}, bf16[8,7168]{1,0:T(8,128)(2,1)S(1)}, u32[]{:S(2)}, u32[]{:S(2)}) collective-permute-start(bf16[8,7168]{1,0:T(8,128)(2,1)S(1)} %add_rows.13), channel_id=1, source_target_pairs={{0,4},{1,5},{2,6},{3,7},{4,0},{5,1},{6,2},{7,3},{8,12},{9,13},{10,... | collective-permute-start | bytes 344072 | tf_op jit(solution)/shard_map/ppermute | solution.py:19
  36.9 6.7 %collective-permute-start.13 = (bf16[8,7168]{1,0:T(8,128)(2,1)S(1)}, bf16[8,7168]{1,0:T(8,128)(2,1)S(1)}, u32[]{:S(2)}, u32[]{:S(2)}) collective-permute-start(bf16[8,7168]{1,0:T(8,128)(2,1)S(1)} %add_rows.11), channel_id=1, source_target_pairs={{0,12},{1,13},{2,14},{3,15},{4,8},{5,9},{6,10},{7,11},{8,4},{9,5},... | collective-permute-start | bytes 344072 | tf_op jit(solution)/shard_map/ppermute | solution.py:19

commit v5 on v4

--- a/solution.py
+++ b/solution.py
@@ -159,33 +159,33 @@
     row_count = step_count * token_count
     own_expert = lax.axis_index("ep") // splits
 
+    last = devices - splits
+    near, half = splits + 2, devices // 2
+    direct = [key for key in range(devices - 1, 0, -1) if key & (key - 1) == 0 and key > 1] + [last + 2, near]
     blocks = {0: hidden}
+    for key in direct:
+        blocks[key] = swap(hidden, key, devices)
+    blocks[half], blocks[splits] = lax.optimization_barrier((blocks[half], blocks[splits]))
+    sources = dict(blocks)
+    sources[half] = pass_rows(blocks[half], w_gate, w_up, w_down)
     for key in sorted(range(2, devices, 2), key=lambda key: (key.bit_count(), -key)):
-        mask = splits if key == splits + 2 else key & -key
-        block = blocks[key - mask]
-        if key == devices // 2 + devices // 4:
-            block, blocks[splits] = lax.optimization_barrier((block, blocks[splits]))
-            block = pass_rows(block, w_gate, w_up, w_down)
-        blocks[key] = swap(block, mask, devices)
-    last = devices - splits
-    batches = [
-        ([*range(0, last, splits), 2], range(splits + 2, last, splits)),
-        ([last, last + 2],),
-    ]
+        if key not in blocks:
+            blocks[key] = sources[key] = swap(sources[key & (key - 1)], key & -key, devices)
+    batches = [[*range(0, last, splits)], [2, near, last + 2]]
+    batches.append([key for key in range(2, devices, 2) if key not in batches[0] + batches[1]])
+    keep_rows = [pack([blocks[key] for key in keys]) for keys in batches]
+    send_rows = [swap(rows, 1, devices) for rows in keep_rows]
 
     backs = {}
-    for batch in [[keys for batch in batches for keys in batch]]:
-        keep_rows = [pack([blocks[key] for key in keys]) for keys in batch]
-        send_rows = [swap(rows, 1, devices) for rows in keep_rows]
-        fars = [0, *range(3, experts), 1, 2]
-        send, keep = expert_slice(keep_rows + send_rows, w_gate[0], w_up[0], w_down[0])
-        twin = swap(send, 1, devices)
-        keys = [key for group in batch for key in group]
-        for far in reversed(fars):
-            theirs, mine = keys.index(far * splits + 2), keys.index(far * splits)
-            across = swap(add_rows(row_count, (theirs, theirs), keep, twin), 2, devices)
-            rows = add_rows(row_count, (mine, mine, 0), keep, twin, across)
-            backs[far] = swap(rows, splits * far, devices) if far else rows
+    fars = [0, *range(3, experts), 1, 2]
+    keys = [key for batch in batches for key in batch]
+    send, keep = expert_slice(keep_rows + send_rows, w_gate[0], w_up[0], w_down[0])
+    twin = swap(send, 1, devices)
+    for far in reversed(fars):
+        theirs, mine = keys.index(far * splits + 2), keys.index(far * splits)
+        across = swap(add_rows(row_count, (theirs, theirs), keep, twin), 2, devices)
+        rows = add_rows(row_count, (mine, mine, 0), keep, twin, across)
+        backs[far] = swap(rows, splits * far, devices) if far else rows
 
     weights = route_scale * route_weight / jnp.sum(route_weight, axis=-1, keepdims=True)
     away = own_expert ^ jnp.arange(experts, dtype=jnp.int32)

time: 44.6 us -> 43.2 us (0.969)
  starting transfers between devices: 25.4 us -> 23.2 us
  waiting for transfers between devices: 15.6 us -> 16.5 us
    ppermute x18, starting transfers between devices: 25.4 us -> 23.2 us  [swap(): return lax.ppermute(value, 'ep', [(i, i ^ mask) for i in range(devices)])]
    ppermute x18, waiting for transfers between devices: 15.6 us -> 16.5 us  [swap(): return lax.ppermute(value, 'ep', [(i, i ^ mask) for i in range(devices)])]
where the time goes in v5:
time: 43.2 us; the launch traced here: 43 us
  starting transfers between devices  23.2 us (54%)
  waiting for transfers between devices  16.5 us (38%)
  Pallas kernels  3.1 us (7%)
    ppermute x18, starting transfers between devices, swap(): return lax.ppermute(value, 'ep', [(i, i ^ mask) for i in range(devices)])  23.2 us
    ppermute x18, waiting for transfers between devices, swap(): return lax.ppermute(value, 'ep', [(i, i ^ mask) for i in range(devices)])  16.5 us
    pallas_call x1, Pallas kernels, expert_slice(): pl.pallas_call(functools.partial(expert_kernel, len(blocks)), out_shape=(...  1.74 us
  transfers between devices with their start and end apart: 18, of which 12 were waited for; matrix products, arithmetic and copies ran while one was open for 0% of the time, Pallas kernels for 1%

profile of v5, /device:TPU:0, one launch (start us, length us, event | category | flops | bytes accessed | tf_op | source)
XLA Modules:
  0.0 43.0 jit_solution(7633314637634996313)
XLA Ops:
  0.0 4.0 %collective-permute-start = (bf16[2,4,7168]{2,1,0:T(4,128)(2,1)}, bf16[2,4,7168]{2,1,0:T(4,128)(2,1)S(1)}, u32[]{:S(2)}, u32[]{:S(2)}) collective-permute-start(bf16[2,4,7168]{2,1,0:T(4,128)(2,1)} %refs_0_.2), channel_id=1, source_target_pairs={{0,8},{1,9},{2,10},{3,11},{4,12},{5,13},{6,14},{7,15},{8,0},{9,1},... | collective-permute-start | bytes 344072 | tf_op jit(solution)/shard_map/ppermute | solution.py:19
  4.0 1.6 %collective-permute-start.1 = (bf16[2,4,7168]{2,1,0:T(4,128)(2,1)}, bf16[2,4,7168]{2,1,0:T(4,128)(2,1)S(1)}, u32[]{:S(2)}, u32[]{:S(2)}) collective-permute-start(bf16[2,4,7168]{2,1,0:T(4,128)(2,1)} %refs_0_.2), channel_id=1, source_target_pairs={{0,4},{1,5},{2,6},{3,7},{4,0},{5,1},{6,2},{7,3},{8,12},{9,13},{10,... | collective-permute-start | bytes 344072 | tf_op jit(solution)/shard_map/ppermute | solution.py:19
  5.6 1.5 %collective-permute-start.2 = (bf16[2,4,7168]{2,1,0:T(4,128)(2,1)}, bf16[2,4,7168]{2,1,0:T(4,128)(2,1)S(1)}, u32[]{:S(2)}, u32[]{:S(2)}) collective-permute-start(bf16[2,4,7168]{2,1,0:T(4,128)(2,1)} %refs_0_.2), channel_id=1, source_target_pairs={{0,2},{1,3},{2,0},{3,1},{4,6},{5,7},{6,4},{7,5},{8,10},{9,11},{10,... | collective-permute-start | bytes 344072 | tf_op jit(solution)/shard_map/ppermute | solution.py:19
  7.1 0.4 collective-permute-start.3
  7.5 2.3 %collective-permute-start.4 = (bf16[2,4,7168]{2,1,0:T(4,128)(2,1)}, bf16[2,4,7168]{2,1,0:T(4,128)(2,1)S(1)}, u32[]{:S(2)}, u32[]{:S(2)}) collective-permute-start(bf16[2,4,7168]{2,1,0:T(4,128)(2,1)} %refs_0_.2), channel_id=1, source_target_pairs={{0,14},{1,15},{2,12},{3,13},{4,10},{5,11},{6,8},{7,9},{8,6},{9,7},... | collective-permute-start | bytes 344072 | tf_op jit(solution)/shard_map/ppermute | solution.py:19
  9.8 0.2 collective-permute-done.refs_2_.rows_ref
  10.0 0.9 %collective-permute-done.1.refs_1_ = bf16[2,4,7168]{2,1,0:T(4,128)(2,1)S(1)} collective-permute-done((bf16[2,4,7168]{2,1,0:T(4,128)(2,1)}, bf16[2,4,7168]{2,1,0:T(4,128)(2,1)S(1)}, u32[]{:S(2)}, u32[]{:S(2)}) %collective-permute-start.1) | collective-permute-done | bytes 114720 | tf_op jit(solution)/shard_map/ppermute | solution.py:19
  11.0 1.6 %collective-permute-start.5 = (bf16[2,4,7168]{2,1,0:T(4,128)(2,1)S(1)}, bf16[2,4,7168]{2,1,0:T(4,128)(2,1)S(1)}, u32[]{:S(2)}, u32[]{:S(2)}) collective-permute-start(bf16[2,4,7168]{2,1,0:T(4,128)(2,1)S(1)} %pass_rows.1), channel_id=1, source_target_pairs={{0,2},{1,3},{2,0},{3,1},{4,6},{5,7},{6,4},{7,5},{8,10},{9,11},{10,... | collective-permute-start | bytes 344072 | tf_op jit(solution)/shard_map/ppermute | solution.py:19
  12.5 1.8 %collective-permute-start.6 = (bf16[2,4,7168]{2,1,0:T(4,128)(2,1)S(1)}, bf16[2,4,7168]{2,1,0:T(4,128)(2,1)S(1)}, u32[]{:S(2)}, u32[]{:S(2)}) collective-permute-start(bf16[2,4,7168]{2,1,0:T(4,128)(2,1)S(1)} %pass_rows.1), channel_id=1, source_target_pairs={{0,4},{1,5},{2,6},{3,7},{4,0},{5,1},{6,2},{7,3},{8,12},{9,13},{10,... | collective-permute-start | bytes 344072 | tf_op jit(solution)/shard_map/ppermute | solution.py:19
  14.3 0.0 copy-done.3
  14.3 0.1 pack_rows.3.refs_0_
  14.5 0.0 collective-permute-done.2.refs_0_
  14.5 0.1 collective-permute-start.7
  14.5 0.9 %collective-permute-done.3.refs_1_ = bf16[2,4,7168]{2,1,0:T(4,128)(2,1)S(1)} collective-permute-done((bf16[2,4,7168]{2,1,0:T(4,128)(2,1)}, bf16[2,4,7168]{2,1,0:T(4,128)(2,1)S(1)}, u32[]{:S(2)}, u32[]{:S(2)}) %collective-permute-start.3) | collective-permute-done | bytes 114720 | tf_op jit(solution)/shard_map/ppermute | solution.py:19
  15.5 2.5 %collective-permute-done.4.refs_2_ = bf16[2,4,7168]{2,1,0:T(4,128)(2,1)S(1)} collective-permute-done((bf16[2,4,7168]{2,1,0:T(4,128)(2,1)}, bf16[2,4,7168]{2,1,0:T(4,128)(2,1)S(1)}, u32[]{:S(2)}, u32[]{:S(2)}) %collective-permute-start.4) | collective-permute-done | bytes 114720 | tf_op jit(solution)/shard_map/ppermute | solution.py:19
  17.9 0.1 pack_rows.4.refs_1_
  18.0 0.1 collective-permute-start.8
  18.1 0.2 collective-permute-done.5.refs_0_
  18.3 0.0 collective-permute-done.6.refs_1_
  18.3 0.1 pack_rows.5.refs_2_
  18.4 0.4 collective-permute-start.9
  18.8 1.3 %collective-permute-done.9.refs_5_ = bf16[16,7168]{1,0:T(8,128)(2,1)S(1)} collective-permute-done((bf16[16,7168]{1,0:T(8,128)(2,1)S(1)}, bf16[16,7168]{1,0:T(8,128)(2,1)S(1)}, u32[]{:S(2)}, u32[]{:S(2)}) %collective-permute-start.9) | collective-permute-done | bytes 229408 | tf_op jit(solution)/shard_map/ppermute | solution.py:19
  20.1 0.0 collective-permute-done.7.refs_3_
  20.1 0.0 collective-permute-done.8.refs_4_
  20.1 0.0 copy-done
  20.1 0.0 copy-done.1
  20.1 0.0 copy-done.2
  20.1 1.7 %expert_slice.1 = (bf16[64,7168]{1,0:T(8,128)(2,1)S(1)}, f32[64,7168]{1,0:T(8,128)S(1)}) custom-call(bf16[24,7168]{1,0:T(8,128)(2,1)S(1)} %pack_rows.3.refs_0_, bf16[24,7168]{1,0:T(8,128)(2,1)S(1)} %pack_rows.4.refs_1_, bf16[16,7168]{1,0:T(8,128)(2,1)S(1)} %pack_rows.5.refs_2_, bf16[24,7168]{1,0:T(8,128)(2,1)S(1)} %collective-permute-done.7.refs_3_, ...), custom_call_target="tpu_custom_call" | custom-call | flops 1409286144 | bytes 11010048 | tf_op jit(solution)/shard_map/expert_slice/pallas_call | solution.py:64
  21.9 0.2 collective-permute-start.10
  22.1 2.3 %collective-permute-done.10.refs_0_ = bf16[64,7168]{1,0:T(8,128)(2,1)S(1)} collective-permute-done((bf16[64,7168]{1,0:T(8,128)(2,1)S(1)}, bf16[64,7168]{1,0:T(8,128)(2,1)S(1)}, u32[]{:S(2)}, u32[]{:S(2)}) %collective-permute-start.10) | collective-permute-done | bytes 917536 | tf_op jit(solution)/shard_map/ppermute | solution.py:19
  24.4 1.0 %collective-permute-start.16 = (bf16[8,7168]{1,0:T(8,128)(2,1)S(1)}, bf16[8,7168]{1,0:T(8,128)(2,1)S(1)}, u32[]{:S(2)}, u32[]{:S(2)}) collective-permute-start(bf16[8,7168]{1,0:T(8,128)(2,1)S(1)} %add_rows.14), channel_id=1, source_target_pairs={{0,2},{1,3},{2,0},{3,1},{4,6},{5,7},{6,4},{7,5},{8,10},{9,11},{10,... | collective-permute-start | bytes 344072 | tf_op jit(solution)/shard_map/ppermute | solution.py:19
  25.4 1.2 %collective-permute-start.14 = (bf16[8,7168]{1,0:T(8,128)(2,1)S(1)}, bf16[8,7168]{1,0:T(8,128)(2,1)S(1)}, u32[]{:S(2)}, u32[]{:S(2)}) collective-permute-start(bf16[8,7168]{1,0:T(8,128)(2,1)S(1)} %add_rows.12), channel_id=1, source_target_pairs={{0,2},{1,3},{2,0},{3,1},{4,6},{5,7},{6,4},{7,5},{8,10},{9,11},{10,... | collective-permute-start | bytes 344072 | tf_op jit(solution)/shard_map/ppermute | solution.py:19
  26.6 1.0 %collective-permute-start.12 = (bf16[8,7168]{1,0:T(8,128)(2,1)S(1)}, bf16[8,7168]{1,0:T(8,128)(2,1)S(1)}, u32[]{:S(2)}, u32[]{:S(2)}) collective-permute-start(bf16[8,7168]{1,0:T(8,128)(2,1)S(1)} %add_rows.10), channel_id=1, source_target_pairs={{0,2},{1,3},{2,0},{3,1},{4,6},{5,7},{6,4},{7,5},{8,10},{9,11},{10,... | collective-permute-start | bytes 344072 | tf_op jit(solution)/shard_map/ppermute | solution.py:19
  27.6 0.0 copy-done.5
  27.7 1.2 %collective-permute-start.11 = (bf16[8,7168]{1,0:T(8,128)(2,1)S(1)}, bf16[8,7168]{1,0:T(8,128)(2,1)S(1)}, u32[]{:S(2)}, u32[]{:S(2)}) collective-permute-start(bf16[8,7168]{1,0:T(8,128)(2,1)S(1)} %add_rows.8), channel_id=1, source_target_pairs={{0,2},{1,3},{2,0},{3,1},{4,6},{5,7},{6,4},{7,5},{8,10},{9,11},{10,... | collective-permute-start | bytes 344072 | tf_op jit(solution)/shard_map/ppermute | solution.py:19
  28.9 1.6 %collective-permute-done.16.refs_1_ = bf16[8,7168]{1,0:T(8,128)(2,1)S(1)} collective-permute-done((bf16[8,7168]{1,0:T(8,128)(2,1)S(1)}, bf16[8,7168]{1,0:T(8,128)(2,1)S(1)}, u32[]{:S(2)}, u32[]{:S(2)}) %collective-permute-start.16) | collective-permute-done | bytes 114720 | tf_op jit(solution)/shard_map/ppermute | solution.py:19
  30.5 0.0 copy-start.4
  30.5 1.3 %collective-permute-start.17 = (bf16[8,7168]{1,0:T(8,128)(2,1)S(1)}, bf16[8,7168]{1,0:T(8,128)(2,1)S(1)}, u32[]{:S(2)}, u32[]{:S(2)}) collective-permute-start(bf16[8,7168]{1,0:T(8,128)(2,1)S(1)} %add_rows.15), channel_id=1, source_target_pairs={{0,8},{1,9},{2,10},{3,11},{4,12},{5,13},{6,14},{7,15},{8,0},{9,1},... | collective-permute-start | bytes 344072 | tf_op jit(solution)/shard_map/ppermute | solution.py:19
  31.9 1.1 %collective-permute-done.14.refs_1_ = bf16[8,7168]{1,0:T(8,128)(2,1)S(1)} collective-permute-done((bf16[8,7168]{1,0:T(8,128)(2,1)S(1)}, bf16[8,7168]{1,0:T(8,128)(2,1)S(1)}, u32[]{:S(2)}, u32[]{:S(2)}) %collective-permute-start.14) | collective-permute-done | bytes 114720 | tf_op jit(solution)/shard_map/ppermute | solution.py:19
  33.0 0.9 %collective-permute-start.15 = (bf16[8,7168]{1,0:T(8,128)(2,1)S(1)}, bf16[8,7168]{1,0:T(8,128)(2,1)S(1)}, u32[]{:S(2)}, u32[]{:S(2)}) collective-permute-start(bf16[8,7168]{1,0:T(8,128)(2,1)S(1)} %add_rows.13), channel_id=1, source_target_pairs={{0,4},{1,5},{2,6},{3,7},{4,0},{5,1},{6,2},{7,3},{8,12},{9,13},{10,... | collective-permute-start | bytes 344072 | tf_op jit(solution)/shard_map/ppermute | solution.py:19
  33.9 1.5 %collective-permute-done.12.refs_1_ = bf16[8,7168]{1,0:T(8,128)(2,1)S(1)} collective-permute-done((bf16[8,7168]{1,0:T(8,128)(2,1)S(1)}, bf16[8,7168]{1,0:T(8,128)(2,1)S(1)}, u32[]{:S(2)}, u32[]{:S(2)}) %collective-permute-start.12) | collective-permute-done | bytes 114720 | tf_op jit(solution)/shard_map/ppermute | solution.py:19
  35.4 2.7 %collective-permute-start.13 = (bf16[8,7168]{1,0:T(8,128)(2,1)S(1)}, bf16[8,7168]{1,0:T(8,128)(2,1)S(1)}, u32[]{:S(2)}, u32[]{:S(2)}) collective-permute-start(bf16[8,7168]{1,0:T(8,128)(2,1)S(1)} %add_rows.11), channel_id=1, source_target_pairs={{0,12},{1,13},{2,14},{3,15},{4,8},{5,9},{6,10},{7,11},{8,4},{9,5},... | collective-permute-start | bytes 344072 | tf_op jit(solution)/shard_map/ppermute | solution.py:19
  38.1 0.1 select_reduce_fusion
  38.2 0.0 collective-permute-done.11.refs_1_
  38.3 0.0 collective-permute-done.17.refs_3_
  38.3 0.7 %collective-permute-done.15.refs_2_ = bf16[8,7168]{1,0:T(8,128)(2,1)S(1)} collective-permute-done((bf16[8,7168]{1,0:T(8,128)(2,1)S(1)}, bf16[8,7168]{1,0:T(8,128)(2,1)S(1)}, u32[]{:S(2)}, u32[]{:S(2)}) %collective-permute-start.15) | collective-permute-done | bytes 114720 | tf_op jit(solution)/shard_map/ppermute | solution.py:19
  39.0 3.2 %collective-permute-done.13.refs_1_ = bf16[8,7168]{1,0:T(8,128)(2,1)S(1)} collective-permute-done((bf16[8,7168]{1,0:T(8,128)(2,1)S(1)}, bf16[8,7168]{1,0:T(8,128)(2,1)S(1)}, u32[]{:S(2)}, u32[]{:S(2)}) %collective-permute-start.13) | collective-permute-done | bytes 114720 | tf_op jit(solution)/shard_map/ppermute | solution.py:19
  42.2 0.8 %mix.1 = bf16[2,4,7168]{2,1,0:T(4,128)(2,1)} custom-call(f32[8,4]{1,0:T(8,128)S(1)} %bitcast.8, bf16[8,7168]{1,0:T(8,128)(2,1)S(1)} %add_rows.9.refs_0_, bf16[8,7168]{1,0:T(8,128)(2,1)S(1)} %collective-permute-done.13.refs_1_, bf16[8,7168]{1,0:T(8,128)(2,1)S(1)} %collective-permute-done.15.refs_2_, bf16[8,7168]{1,0:T(8,128)(2,1)S(1)} %collective-permute-done.17.refs_3_), custom_call_target="tpu_custom_call" | custom-call | tf_op jit(solution)/shard_map/mix/pallas_call | solution.py:143
  (17 shorter events, 0.3 us)
Async XLA Ops:
  0.0 14.3 %copy-start.3 = (bf16[2,4,7168]{2,1,0:T(4,128)(2,1)S(1)}, bf16[2,4,7168]{2,1,0:T(4,128)(2,1)}, u32[]{:S(2)}) copy-start(bf16[2,4,7168]{2,1,0:T(4,128)(2,1)} %refs_0_.2) | copy-start | bytes 344068
  0.0 10.0 %collective-permute-start = (bf16[2,4,7168]{2,1,0:T(4,128)(2,1)}, bf16[2,4,7168]{2,1,0:T(4,128)(2,1)S(1)}, u32[]{:S(2)}, u32[]{:S(2)}) collective-permute-start(bf16[2,4,7168]{2,1,0:T(4,128)(2,1)} %refs_0_.2), channel_id=1, source_target_pairs={{0,8},{1,9},{2,10},{3,11},{4,12},{5,13},{6,14},{7,15},{8,0},{9,1},... | collective-permute-start | bytes 344072 | tf_op jit(solution)/shard_map/ppermute | solution.py:19
  4.0 6.9 %collective-permute-start.1 = (bf16[2,4,7168]{2,1,0:T(4,128)(2,1)}, bf16[2,4,7168]{2,1,0:T(4,128)(2,1)S(1)}, u32[]{:S(2)}, u32[]{:S(2)}) collective-permute-start(bf16[2,4,7168]{2,1,0:T(4,128)(2,1)} %refs_0_.2), channel_id=1, source_target_pairs={{0,4},{1,5},{2,6},{3,7},{4,0},{5,1},{6,2},{7,3},{8,12},{9,13},{10,... | collective-permute-start | bytes 344072 | tf_op jit(solution)/shard_map/ppermute | solution.py:19
  5.6 8.8 %collective-permute-start.2 = (bf16[2,4,7168]{2,1,0:T(4,128)(2,1)}, bf16[2,4,7168]{2,1,0:T(4,128)(2,1)S(1)}, u32[]{:S(2)}, u32[]{:S(2)}) collective-permute-start(bf16[2,4,7168]{2,1,0:T(4,128)(2,1)} %refs_0_.2), channel_id=1, source_target_pairs={{0,2},{1,3},{2,0},{3,1},{4,6},{5,7},{6,4},{7,5},{8,10},{9,11},{10,... | collective-permute-start | bytes 344072 | tf_op jit(solution)/shard_map/ppermute | solution.py:19
  7.1 8.3 %collective-permute-start.3 = (bf16[2,4,7168]{2,1,0:T(4,128)(2,1)}, bf16[2,4,7168]{2,1,0:T(4,128)(2,1)S(1)}, u32[]{:S(2)}, u32[]{:S(2)}) collective-permute-start(bf16[2,4,7168]{2,1,0:T(4,128)(2,1)} %refs_0_.2), channel_id=1, source_target_pairs={{0,6},{1,7},{2,4},{3,5},{4,2},{5,3},{6,0},{7,1},{8,14},{9,15},{10,... | collective-permute-start | bytes 344072 | tf_op jit(solution)/shard_map/ppermute | solution.py:19
  7.5 10.4 %collective-permute-start.4 = (bf16[2,4,7168]{2,1,0:T(4,128)(2,1)}, bf16[2,4,7168]{2,1,0:T(4,128)(2,1)S(1)}, u32[]{:S(2)}, u32[]{:S(2)}) collective-permute-start(bf16[2,4,7168]{2,1,0:T(4,128)(2,1)} %refs_0_.2), channel_id=1, source_target_pairs={{0,14},{1,15},{2,12},{3,13},{4,10},{5,11},{6,8},{7,9},{8,6},{9,7},... | collective-permute-start | bytes 344072 | tf_op jit(solution)/shard_map/ppermute | solution.py:19
  10.9 9.2 %copy-start = (bf16[1,7168,256]{2,1,0:T(8,128)(2,1)S(1)}, bf16[1,7168,256]{2,1,0:T(8,128)(2,1)}, u32[]{:S(2)}) copy-start(bf16[1,7168,256]{2,1,0:T(8,128)(2,1)} %refs_0_.3) | copy-start | bytes 11010052
  10.9 9.2 %copy-start.1 = (bf16[1,7168,256]{2,1,0:T(8,128)(2,1)S(1)}, bf16[1,7168,256]{2,1,0:T(8,128)(2,1)}, u32[]{:S(2)}) copy-start(bf16[1,7168,256]{2,1,0:T(8,128)(2,1)} %refs_1_.1) | copy-start | bytes 11010052
  10.9 9.2 %copy-start.2 = (bf16[1,256,7168]{2,1,0:T(8,128)(2,1)S(1)}, bf16[1,256,7168]{2,1,0:T(8,128)(2,1)}, u32[]{:S(2)}) copy-start(bf16[1,256,7168]{2,1,0:T(8,128)(2,1)} %refs_2_.1) | copy-start | bytes 11010052
  11.0 7.4 %collective-permute-start.5 = (bf16[2,4,7168]{2,1,0:T(4,128)(2,1)S(1)}, bf16[2,4,7168]{2,1,0:T(4,128)(2,1)S(1)}, u32[]{:S(2)}, u32[]{:S(2)}) collective-permute-start(bf16[2,4,7168]{2,1,0:T(4,128)(2,1)S(1)} %pass_rows.1), channel_id=1, source_target_pairs={{0,2},{1,3},{2,0},{3,1},{4,6},{5,7},{6,4},{7,5},{8,10},{9,11},{10,... | collective-permute-start | bytes 344072 | tf_op jit(solution)/shard_map/ppermute | solution.py:19
  12.5 5.8 %collective-permute-start.6 = (bf16[2,4,7168]{2,1,0:T(4,128)(2,1)S(1)}, bf16[2,4,7168]{2,1,0:T(4,128)(2,1)S(1)}, u32[]{:S(2)}, u32[]{:S(2)}) collective-permute-start(bf16[2,4,7168]{2,1,0:T(4,128)(2,1)S(1)} %pass_rows.1), channel_id=1, source_target_pairs={{0,4},{1,5},{2,6},{3,7},{4,0},{5,1},{6,2},{7,3},{8,12},{9,13},{10,... | collective-permute-start | bytes 344072 | tf_op jit(solution)/shard_map/ppermute | solution.py:19
  14.5 5.6 %collective-permute-start.7 = (bf16[24,7168]{1,0:T(8,128)(2,1)S(1)}, bf16[24,7168]{1,0:T(8,128)(2,1)S(1)}, u32[]{:S(2)}, u32[]{:S(2)}) collective-permute-start(bf16[24,7168]{1,0:T(8,128)(2,1)S(1)} %pack_rows.3.refs_0_), channel_id=1, source_target_pairs={{0,1},{1,0},{2,3},{3,2},{4,5},{5,4},{6,7},{7,6},{8,9},{9,8},{10,11... | collective-permute-start | bytes 1032200 | tf_op jit(solution)/shard_map/ppermute | solution.py:19
  18.0 2.1 %collective-permute-start.8 = (bf16[24,7168]{1,0:T(8,128)(2,1)S(1)}, bf16[24,7168]{1,0:T(8,128)(2,1)S(1)}, u32[]{:S(2)}, u32[]{:S(2)}) collective-permute-start(bf16[24,7168]{1,0:T(8,128)(2,1)S(1)} %pack_rows.4.refs_1_), channel_id=1, source_target_pairs={{0,1},{1,0},{2,3},{3,2},{4,5},{5,4},{6,7},{7,6},{8,9},{9,8},{10,11... | collective-permute-start | bytes 1032200 | tf_op jit(solution)/shard_map/ppermute | solution.py:19
  18.4 1.7 %collective-permute-start.9 = (bf16[16,7168]{1,0:T(8,128)(2,1)S(1)}, bf16[16,7168]{1,0:T(8,128)(2,1)S(1)}, u32[]{:S(2)}, u32[]{:S(2)}) collective-permute-start(bf16[16,7168]{1,0:T(8,128)(2,1)S(1)} %pack_rows.5.refs_2_), channel_id=1, source_target_pairs={{0,1},{1,0},{2,3},{3,2},{4,5},{5,4},{6,7},{7,6},{8,9},{9,8},{10,11... | collective-permute-start | bytes 688136 | tf_op jit(solution)/shard_map/ppermute | solution.py:19
  21.9 2.5 %collective-permute-start.10 = (bf16[64,7168]{1,0:T(8,128)(2,1)S(1)}, bf16[64,7168]{1,0:T(8,128)(2,1)S(1)}, u32[]{:S(2)}, u32[]{:S(2)}) collective-permute-start(bf16[64,7168]{1,0:T(8,128)(2,1)S(1)} %get-tuple-element.12), channel_id=1, source_target_pairs={{0,1},{1,0},{2,3},{3,2},{4,5},{5,4},{6,7},{7,6},{8,9},{9,8},{10,11... | collective-permute-start | bytes 2752520 | tf_op jit(solution)/shard_map/ppermute | solution.py:19
  24.4 3.2 %copy-start.5 = (f32[2,4,2]{1,2,0:T(2,128)S(1)}, f32[2,4,2]{1,2,0:T(2,128)}, u32[]{:S(2)}) copy-start(f32[2,4,2]{1,2,0:T(2,128)} %param.8) | copy-start | bytes 196
  24.4 6.1 %collective-permute-start.16 = (bf16[8,7168]{1,0:T(8,128)(2,1)S(1)}, bf16[8,7168]{1,0:T(8,128)(2,1)S(1)}, u32[]{:S(2)}, u32[]{:S(2)}) collective-permute-start(bf16[8,7168]{1,0:T(8,128)(2,1)S(1)} %add_rows.14), channel_id=1, source_target_pairs={{0,2},{1,3},{2,0},{3,1},{4,6},{5,7},{6,4},{7,5},{8,10},{9,11},{10,... | collective-permute-start | bytes 344072 | tf_op jit(solution)/shard_map/ppermute | solution.py:19
  25.4 7.5 %collective-permute-start.14 = (bf16[8,7168]{1,0:T(8,128)(2,1)S(1)}, bf16[8,7168]{1,0:T(8,128)(2,1)S(1)}, u32[]{:S(2)}, u32[]{:S(2)}) collective-permute-start(bf16[8,7168]{1,0:T(8,128)(2,1)S(1)} %add_rows.12), channel_id=1, source_target_pairs={{0,2},{1,3},{2,0},{3,1},{4,6},{5,7},{6,4},{7,5},{8,10},{9,11},{10,... | collective-permute-start | bytes 344072 | tf_op jit(solution)/shard_map/ppermute | solution.py:19
  26.6 8.8 %collective-permute-start.12 = (bf16[8,7168]{1,0:T(8,128)(2,1)S(1)}, bf16[8,7168]{1,0:T(8,128)(2,1)S(1)}, u32[]{:S(2)}, u32[]{:S(2)}) collective-permute-start(bf16[8,7168]{1,0:T(8,128)(2,1)S(1)} %add_rows.10), channel_id=1, source_target_pairs={{0,2},{1,3},{2,0},{3,1},{4,6},{5,7},{6,4},{7,5},{8,10},{9,11},{10,... | collective-permute-start | bytes 344072 | tf_op jit(solution)/shard_map/ppermute | solution.py:19
  27.7 10.5 %collective-permute-start.11 = (bf16[8,7168]{1,0:T(8,128)(2,1)S(1)}, bf16[8,7168]{1,0:T(8,128)(2,1)S(1)}, u32[]{:S(2)}, u32[]{:S(2)}) collective-permute-start(bf16[8,7168]{1,0:T(8,128)(2,1)S(1)} %add_rows.8), channel_id=1, source_target_pairs={{0,2},{1,3},{2,0},{3,1},{4,6},{5,7},{6,4},{7,5},{8,10},{9,11},{10,... | collective-permute-start | bytes 344072 | tf_op jit(solution)/shard_map/ppermute | solution.py:19
  30.5 7.6 %copy-start.4 = (s32[2,4,2]{1,2,0:T(2,128)S(1)}, s32[2,4,2]{1,2,0:T(2,128)}, u32[]{:S(2)}) copy-start(s32[2,4,2]{1,2,0:T(2,128)} %param.7) | copy-start | bytes 196
  30.5 7.7 %collective-permute-start.17 = (bf16[8,7168]{1,0:T(8,128)(2,1)S(1)}, bf16[8,7168]{1,0:T(8,128)(2,1)S(1)}, u32[]{:S(2)}, u32[]{:S(2)}) collective-permute-start(bf16[8,7168]{1,0:T(8,128)(2,1)S(1)} %add_rows.15), channel_id=1, source_target_pairs={{0,8},{1,9},{2,10},{3,11},{4,12},{5,13},{6,14},{7,15},{8,0},{9,1},... | collective-permute-start | bytes 344072 | tf_op jit(solution)/shard_map/ppermute | solution.py:19
  33.0 6.0 %collective-permute-start.15 = (bf16[8,7168]{1,0:T(8,128)(2,1)S(1)}, bf16[8,7168]{1,0:T(8,128)(2,1)S(1)}, u32[]{:S(2)}, u32[]{:S(2)}) collective-permute-start(bf16[8,7168]{1,0:T(8,128)(2,1)S(1)} %add_rows.13), channel_id=1, source_target_pairs={{0,4},{1,5},{2,6},{3,7},{4,0},{5,1},{6,2},{7,3},{8,12},{9,13},{10,... | collective-permute-start | bytes 344072 | tf_op jit(solution)/shard_map/ppermute | solution.py:19
  35.4 6.8 %collective-permute-start.13 = (bf16[8,7168]{1,0:T(8,128)(2,1)S(1)}, bf16[8,7168]{1,0:T(8,128)(2,1)S(1)}, u32[]{:S(2)}, u32[]{:S(2)}) collective-permute-start(bf16[8,7168]{1,0:T(8,128)(2,1)S(1)} %add_rows.11), channel_id=1, source_target_pairs={{0,12},{1,13},{2,14},{3,15},{4,8},{5,9},{6,10},{7,11},{8,4},{9,5},... | collective-permute-start | bytes 344072 | tf_op jit(solution)/shard_map/ppermute | solution.py:19

commit v6 on v5

--- a/solution.py
+++ b/solution.py
@@ -34,11 +34,13 @@
     return run
 
 
-def expert_kernel(count, *refs):
-    blocks, (gate_ref, up_ref, down_ref, send_ref, keep_ref, both) = refs[:count], refs[count:]
+def expert_kernel(count, size, first, *refs):
+    blocks, (gate_ref, up_ref, down_ref, first_ref, rest_ref, keep_ref, both) = refs[:count], refs[count:]
     features, units = gate_ref.shape[-2:]
     depth = largest_chunk(features, 1024)
-    half = send_ref.shape[0]
+    half = keep_ref.shape[0]
+    pieces = range(half // size)
+    chosen = [(first_ref, first), (rest_ref, [piece for piece in pieces if piece not in first])]
     both[...] = jnp.zeros_like(both)
 
     @in_steps(features, depth, both.shape[1] <= 256)
@@ -54,21 +56,24 @@
     def _(at):
         out = jnp.dot(slice_hidden, down_ref[:, at], preferred_element_type=jnp.float32)
         keep_ref[:, at] = out[:half]
-        send_ref[:, at] = out[half:].astype(jnp.bfloat16)
-
-
-def expert_slice(blocks, gate_w, up_w, down_w):
+        for ref, places in chosen:
+            rows = [out[half + place * size:half + (place + 1) * size] for place in places]
+            ref[:, at] = jnp.concatenate(rows, axis=0).astype(jnp.bfloat16)
+
+
+def expert_slice(blocks, size, first, gate_w, up_w, down_w):
     features, units = gate_w.shape
     rows = sum(block.shape[0] for block in blocks)
     half = rows // 2
     return pl.pallas_call(
-        functools.partial(expert_kernel, len(blocks)),
+        functools.partial(expert_kernel, len(blocks), size, first),
         out_shape=(
-            jax.ShapeDtypeStruct((half, features), jnp.bfloat16),
+            jax.ShapeDtypeStruct((len(first) * size, features), jnp.bfloat16),
+            jax.ShapeDtypeStruct((half - len(first) * size, features), jnp.bfloat16),
             jax.ShapeDtypeStruct((half, features), jnp.float32),
         ),
         in_specs=[VMEM] * (len(blocks) + 3),
-        out_specs=(VMEM, VMEM),
+        out_specs=(VMEM, VMEM, VMEM),
         scratch_shapes=[pltpu.VMEM((2, rows, units), jnp.float32)],
         compiler_params=pltpu.CompilerParams(vmem_limit_bytes=28 * MIB),
         cost_estimate=pl.CostEstimate(flops=6 * rows * units * features, bytes_accessed=6 * units * features, transcendentals=0),
@@ -176,15 +181,20 @@
     keep_rows = [pack([blocks[key] for key in keys]) for keys in batches]
     send_rows = [swap(rows, 1, devices) for rows in keep_rows]
 
-    backs = {}
     fars = [0, *range(3, experts), 1, 2]
     keys = [key for batch in batches for key in batch]
-    send, keep = expert_slice(keep_rows + send_rows, w_gate[0], w_up[0], w_down[0])
-    twin = swap(send, 1, devices)
+    first = [keys.index(fars[-1] * splits), keys.index(fars[-1] * splits + 2)]
+    rest = [place for place in range(len(keys)) if place not in first]
+    *sends, keep = expert_slice(keep_rows + send_rows, row_count, first, w_gate[0], w_up[0], w_down[0])
+    twins = [swap(sends[0], 1, devices)]
+    twins[0], sends[1] = lax.optimization_barrier((twins[0], sends[1]))
+    twins.append(swap(sends[1], 1, devices))
+    backs = {}
     for far in reversed(fars):
-        theirs, mine = keys.index(far * splits + 2), keys.index(far * splits)
-        across = swap(add_rows(row_count, (theirs, theirs), keep, twin), 2, devices)
-        rows = add_rows(row_count, (mine, mine, 0), keep, twin, across)
+        mine, theirs = keys.index(far * splits), keys.index(far * splits + 2)
+        twin, there = (twins[0], first) if mine in first else (twins[1], rest)
+        across = swap(add_rows(row_count, (theirs, there.index(theirs)), keep, twin), 2, devices)
+        rows = add_rows(row_count, (mine, there.index(mine), 0), keep, twin, across)
         backs[far] = swap(rows, splits * far, devices) if far else rows
 
     weights = route_scale * route_weight / jnp.sum(route_weight, axis=-1, keepdims=True)

time: 43.2 us -> 42.3 us (0.979)
  waiting for transfers between devices: 16.5 us -> 14.9 us
  starting transfers between devices: 23.2 us -> 23.9 us
    ppermute x18 -> x19, waiting for transfers between devices: 16.5 us -> 14.9 us  [swap(): return lax.ppermute(value, 'ep', [(i, i ^ mask) for i in range(devices)])]
    ppermute x18 -> x19, starting transfers between devices: 23.2 us -> 23.9 us  [swap(): return lax.ppermute(value, 'ep', [(i, i ^ mask) for i in range(devices)])]
  transfers between devices with their start and end apart: 18 -> 19, of which waited for: 12 -> 14; matrix products, arithmetic and copies ran while one was open for 0% -> 0% of each run, Pallas kernels for 1% -> 1%
where the time goes in v6:
time: 42.3 us; the launch traced here: 42.2 us
  starting transfers between devices  23.9 us (57%)
  waiting for transfers between devices  14.9 us (35%)
  Pallas kernels  3.1 us (7%)
    ppermute x19, starting transfers between devices, swap(): return lax.ppermute(value, 'ep', [(i, i ^ mask) for i in range(devices)])  23.9 us
    ppermute x19, waiting for transfers between devices, swap(): return lax.ppermute(value, 'ep', [(i, i ^ mask) for i in range(devices)])  14.9 us
    pallas_call x1, Pallas kernels, expert_slice(): pl.pallas_call(functools.partial(expert_kernel, len(blocks), size, first)...  1.74 us
  transfers between devices with their start and end apart: 19, of which 14 were waited for; matrix products, arithmetic and copies ran while one was open for 0% of the time, Pallas kernels for 1%

profile of v6, /device:TPU:0, one launch (start us, length us, event | category | flops | bytes accessed | tf_op | source)
XLA Modules:
  0.0 42.2 jit_solution(1683229152382425032)
XLA Ops:
  0.0 4.0 %collective-permute-start = (bf16[2,4,7168]{2,1,0:T(4,128)(2,1)}, bf16[2,4,7168]{2,1,0:T(4,128)(2,1)S(1)}, u32[]{:S(2)}, u32[]{:S(2)}) collective-permute-start(bf16[2,4,7168]{2,1,0:T(4,128)(2,1)} %refs_0_.2), channel_id=1, source_target_pairs={{0,8},{1,9},{2,10},{3,11},{4,12},{5,13},{6,14},{7,15},{8,0},{9,1},... | collective-permute-start | bytes 344072 | tf_op jit(solution)/shard_map/ppermute | solution.py:19
  4.0 1.6 %collective-permute-start.1 = (bf16[2,4,7168]{2,1,0:T(4,128)(2,1)}, bf16[2,4,7168]{2,1,0:T(4,128)(2,1)S(1)}, u32[]{:S(2)}, u32[]{:S(2)}) collective-permute-start(bf16[2,4,7168]{2,1,0:T(4,128)(2,1)} %refs_0_.2), channel_id=1, source_target_pairs={{0,4},{1,5},{2,6},{3,7},{4,0},{5,1},{6,2},{7,3},{8,12},{9,13},{10,... | collective-permute-start | bytes 344072 | tf_op jit(solution)/shard_map/ppermute | solution.py:19
  5.6 1.5 %collective-permute-start.2 = (bf16[2,4,7168]{2,1,0:T(4,128)(2,1)}, bf16[2,4,7168]{2,1,0:T(4,128)(2,1)S(1)}, u32[]{:S(2)}, u32[]{:S(2)}) collective-permute-start(bf16[2,4,7168]{2,1,0:T(4,128)(2,1)} %refs_0_.2), channel_id=1, source_target_pairs={{0,2},{1,3},{2,0},{3,1},{4,6},{5,7},{6,4},{7,5},{8,10},{9,11},{10,... | collective-permute-start | bytes 344072 | tf_op jit(solution)/shard_map/ppermute | solution.py:19
  7.1 0.4 collective-permute-start.3
  7.5 2.3 %collective-permute-start.4 = (bf16[2,4,7168]{2,1,0:T(4,128)(2,1)}, bf16[2,4,7168]{2,1,0:T(4,128)(2,1)S(1)}, u32[]{:S(2)}, u32[]{:S(2)}) collective-permute-start(bf16[2,4,7168]{2,1,0:T(4,128)(2,1)} %refs_0_.2), channel_id=1, source_target_pairs={{0,14},{1,15},{2,12},{3,13},{4,10},{5,11},{6,8},{7,9},{8,6},{9,7},... | collective-permute-start | bytes 344072 | tf_op jit(solution)/shard_map/ppermute | solution.py:19
  9.8 0.2 collective-permute-done.refs_2_.rows_ref
  10.0 0.9 %collective-permute-done.1.refs_1_ = bf16[2,4,7168]{2,1,0:T(4,128)(2,1)S(1)} collective-permute-done((bf16[2,4,7168]{2,1,0:T(4,128)(2,1)}, bf16[2,4,7168]{2,1,0:T(4,128)(2,1)S(1)}, u32[]{:S(2)}, u32[]{:S(2)}) %collective-permute-start.1) | collective-permute-done | bytes 114720 | tf_op jit(solution)/shard_map/ppermute | solution.py:19
  11.0 1.6 %collective-permute-start.5 = (bf16[2,4,7168]{2,1,0:T(4,128)(2,1)S(1)}, bf16[2,4,7168]{2,1,0:T(4,128)(2,1)S(1)}, u32[]{:S(2)}, u32[]{:S(2)}) collective-permute-start(bf16[2,4,7168]{2,1,0:T(4,128)(2,1)S(1)} %pass_rows.1), channel_id=1, source_target_pairs={{0,2},{1,3},{2,0},{3,1},{4,6},{5,7},{6,4},{7,5},{8,10},{9,11},{10,... | collective-permute-start | bytes 344072 | tf_op jit(solution)/shard_map/ppermute | solution.py:19
  12.5 1.8 %collective-permute-start.6 = (bf16[2,4,7168]{2,1,0:T(4,128)(2,1)S(1)}, bf16[2,4,7168]{2,1,0:T(4,128)(2,1)S(1)}, u32[]{:S(2)}, u32[]{:S(2)}) collective-permute-start(bf16[2,4,7168]{2,1,0:T(4,128)(2,1)S(1)} %pass_rows.1), channel_id=1, source_target_pairs={{0,4},{1,5},{2,6},{3,7},{4,0},{5,1},{6,2},{7,3},{8,12},{9,13},{10,... | collective-permute-start | bytes 344072 | tf_op jit(solution)/shard_map/ppermute | solution.py:19
  14.3 0.0 copy-done.3
  14.3 0.1 pack_rows.3.refs_0_
  14.5 0.0 collective-permute-done.2.refs_0_
  14.5 0.1 collective-permute-start.7
  14.5 0.9 %collective-permute-done.3.refs_1_ = bf16[2,4,7168]{2,1,0:T(4,128)(2,1)S(1)} collective-permute-done((bf16[2,4,7168]{2,1,0:T(4,128)(2,1)}, bf16[2,4,7168]{2,1,0:T(4,128)(2,1)S(1)}, u32[]{:S(2)}, u32[]{:S(2)}) %collective-permute-start.3) | collective-permute-done | bytes 114720 | tf_op jit(solution)/shard_map/ppermute | solution.py:19
  15.5 2.5 %collective-permute-done.4.refs_2_ = bf16[2,4,7168]{2,1,0:T(4,128)(2,1)S(1)} collective-permute-done((bf16[2,4,7168]{2,1,0:T(4,128)(2,1)}, bf16[2,4,7168]{2,1,0:T(4,128)(2,1)S(1)}, u32[]{:S(2)}, u32[]{:S(2)}) %collective-permute-start.4) | collective-permute-done | bytes 114720 | tf_op jit(solution)/shard_map/ppermute | solution.py:19
  17.9 0.1 pack_rows.4.refs_1_
  18.0 0.1 collective-permute-start.8
  18.1 0.2 collective-permute-done.5.refs_0_
  18.3 0.0 collective-permute-done.6.refs_1_
  18.3 0.1 pack_rows.5.refs_2_
  18.4 0.4 collective-permute-start.9
  18.8 1.3 %collective-permute-done.9.refs_5_ = bf16[16,7168]{1,0:T(8,128)(2,1)S(1)} collective-permute-done((bf16[16,7168]{1,0:T(8,128)(2,1)S(1)}, bf16[16,7168]{1,0:T(8,128)(2,1)S(1)}, u32[]{:S(2)}, u32[]{:S(2)}) %collective-permute-start.9) | collective-permute-done | bytes 229408 | tf_op jit(solution)/shard_map/ppermute | solution.py:19
  20.1 0.0 collective-permute-done.7.refs_3_
  20.1 0.0 collective-permute-done.8.refs_4_
  20.1 0.0 copy-done
  20.1 1.7 %expert_slice.1 = (bf16[16,7168]{1,0:T(8,128)(2,1)S(1)}, bf16[48,7168]{1,0:T(8,128)(2,1)S(1)}, f32[64,7168]{1,0:T(8,128)S(1)}) custom-call(bf16[24,7168]{1,0:T(8,128)(2,1)S(1)} %pack_rows.3.refs_0_, bf16[24,7168]{1,0:T(8,128)(2,1)S(1)} %pack_rows.4.refs_1_, bf16[16,7168]{1,0:T(8,128)(2,1)S(1)} %pack_rows.5.refs_2_, ...), custom_call_target="tpu_custom_call" | custom-call | flops 1409286144 | bytes 11010048 | tf_op jit(solution)/shard_map/expert_slice/pallas_call | solution.py:68
  21.9 0.2 collective-permute-start.10
  22.1 1.3 %collective-permute-done.10.refs_0_ = bf16[16,7168]{1,0:T(8,128)(2,1)S(1)} collective-permute-done((bf16[16,7168]{1,0:T(8,128)(2,1)S(1)}, bf16[16,7168]{1,0:T(8,128)(2,1)S(1)}, u32[]{:S(2)}, u32[]{:S(2)}) %collective-permute-start.10) | collective-permute-done | bytes 229408 | tf_op jit(solution)/shard_map/ppermute | solution.py:19
  23.4 0.2 collective-permute-start.11
  23.6 1.0 %collective-permute-start.17 = (bf16[8,7168]{1,0:T(8,128)(2,1)S(1)}, bf16[8,7168]{1,0:T(8,128)(2,1)S(1)}, u32[]{:S(2)}, u32[]{:S(2)}) collective-permute-start(bf16[8,7168]{1,0:T(8,128)(2,1)S(1)} %add_rows.14), channel_id=1, source_target_pairs={{0,2},{1,3},{2,0},{3,1},{4,6},{5,7},{6,4},{7,5},{8,10},{9,11},{10,... | collective-permute-start | bytes 344072 | tf_op jit(solution)/shard_map/ppermute | solution.py:19
  24.6 1.0 %collective-permute-done.11.refs_0_ = bf16[48,7168]{1,0:T(8,128)(2,1)S(1)} collective-permute-done((bf16[48,7168]{1,0:T(8,128)(2,1)S(1)}, bf16[48,7168]{1,0:T(8,128)(2,1)S(1)}, u32[]{:S(2)}, u32[]{:S(2)}) %collective-permute-start.11) | collective-permute-done | bytes 688160 | tf_op jit(solution)/shard_map/ppermute | solution.py:19
  25.6 1.0 %collective-permute-start.15 = (bf16[8,7168]{1,0:T(8,128)(2,1)S(1)}, bf16[8,7168]{1,0:T(8,128)(2,1)S(1)}, u32[]{:S(2)}, u32[]{:S(2)}) collective-permute-start(bf16[8,7168]{1,0:T(8,128)(2,1)S(1)} %add_rows.12), channel_id=1, source_target_pairs={{0,2},{1,3},{2,0},{3,1},{4,6},{5,7},{6,4},{7,5},{8,10},{9,11},{10,... | collective-permute-start | bytes 344072 | tf_op jit(solution)/shard_map/ppermute | solution.py:19
  26.6 1.2 %collective-permute-start.13 = (bf16[8,7168]{1,0:T(8,128)(2,1)S(1)}, bf16[8,7168]{1,0:T(8,128)(2,1)S(1)}, u32[]{:S(2)}, u32[]{:S(2)}) collective-permute-start(bf16[8,7168]{1,0:T(8,128)(2,1)S(1)} %add_rows.10), channel_id=1, source_target_pairs={{0,2},{1,3},{2,0},{3,1},{4,6},{5,7},{6,4},{7,5},{8,10},{9,11},{10,... | collective-permute-start | bytes 344072 | tf_op jit(solution)/shard_map/ppermute | solution.py:19
  27.8 0.0 copy-done.5
  27.8 1.8 %collective-permute-done.17.refs_1_ = bf16[8,7168]{1,0:T(8,128)(2,1)S(1)} collective-permute-done((bf16[8,7168]{1,0:T(8,128)(2,1)S(1)}, bf16[8,7168]{1,0:T(8,128)(2,1)S(1)}, u32[]{:S(2)}, u32[]{:S(2)}) %collective-permute-start.17) | collective-permute-done | bytes 114720 | tf_op jit(solution)/shard_map/ppermute | solution.py:19
  29.7 0.0 copy-start.4
  29.7 1.3 %collective-permute-start.18 = (bf16[8,7168]{1,0:T(8,128)(2,1)S(1)}, bf16[8,7168]{1,0:T(8,128)(2,1)S(1)}, u32[]{:S(2)}, u32[]{:S(2)}) collective-permute-start(bf16[8,7168]{1,0:T(8,128)(2,1)S(1)} %add_rows.15), channel_id=1, source_target_pairs={{0,8},{1,9},{2,10},{3,11},{4,12},{5,13},{6,14},{7,15},{8,0},{9,1},... | collective-permute-start | bytes 344072 | tf_op jit(solution)/shard_map/ppermute | solution.py:19
  31.0 0.8 %collective-permute-start.12 = (bf16[8,7168]{1,0:T(8,128)(2,1)S(1)}, bf16[8,7168]{1,0:T(8,128)(2,1)S(1)}, u32[]{:S(2)}, u32[]{:S(2)}) collective-permute-start(bf16[8,7168]{1,0:T(8,128)(2,1)S(1)} %add_rows.8), channel_id=1, source_target_pairs={{0,2},{1,3},{2,0},{3,1},{4,6},{5,7},{6,4},{7,5},{8,10},{9,11},{10,... | collective-permute-start | bytes 344072 | tf_op jit(solution)/shard_map/ppermute | solution.py:19
  31.8 0.3 collective-permute-done.15.refs_1_
  32.1 1.9 %collective-permute-start.16 = (bf16[8,7168]{1,0:T(8,128)(2,1)S(1)}, bf16[8,7168]{1,0:T(8,128)(2,1)S(1)}, u32[]{:S(2)}, u32[]{:S(2)}) collective-permute-start(bf16[8,7168]{1,0:T(8,128)(2,1)S(1)} %add_rows.13), channel_id=1, source_target_pairs={{0,4},{1,5},{2,6},{3,7},{4,0},{5,1},{6,2},{7,3},{8,12},{9,13},{10,... | collective-permute-start | bytes 344072 | tf_op jit(solution)/shard_map/ppermute | solution.py:19
  34.0 0.5 %collective-permute-done.13.refs_1_ = bf16[8,7168]{1,0:T(8,128)(2,1)S(1)} collective-permute-done((bf16[8,7168]{1,0:T(8,128)(2,1)S(1)}, bf16[8,7168]{1,0:T(8,128)(2,1)S(1)}, u32[]{:S(2)}, u32[]{:S(2)}) %collective-permute-start.13) | collective-permute-done | bytes 114720 | tf_op jit(solution)/shard_map/ppermute | solution.py:19
  34.6 2.7 %collective-permute-start.14 = (bf16[8,7168]{1,0:T(8,128)(2,1)S(1)}, bf16[8,7168]{1,0:T(8,128)(2,1)S(1)}, u32[]{:S(2)}, u32[]{:S(2)}) collective-permute-start(bf16[8,7168]{1,0:T(8,128)(2,1)S(1)} %add_rows.11), channel_id=1, source_target_pairs={{0,12},{1,13},{2,14},{3,15},{4,8},{5,9},{6,10},{7,11},{8,4},{9,5},... | collective-permute-start | bytes 344072 | tf_op jit(solution)/shard_map/ppermute | solution.py:19
  37.3 0.1 select_reduce_fusion
  37.4 0.0 collective-permute-done.12.refs_1_
  37.4 0.4 %collective-permute-done.18.refs_3_ = bf16[8,7168]{1,0:T(8,128)(2,1)S(1)} collective-permute-done((bf16[8,7168]{1,0:T(8,128)(2,1)S(1)}, bf16[8,7168]{1,0:T(8,128)(2,1)S(1)}, u32[]{:S(2)}, u32[]{:S(2)}) %collective-permute-start.18) | collective-permute-done | bytes 114720 | tf_op jit(solution)/shard_map/ppermute | solution.py:19
  37.8 1.8 %collective-permute-done.16.refs_2_ = bf16[8,7168]{1,0:T(8,128)(2,1)S(1)} collective-permute-done((bf16[8,7168]{1,0:T(8,128)(2,1)S(1)}, bf16[8,7168]{1,0:T(8,128)(2,1)S(1)}, u32[]{:S(2)}, u32[]{:S(2)}) %collective-permute-start.16) | collective-permute-done | bytes 114720 | tf_op jit(solution)/shard_map/ppermute | solution.py:19
  39.6 1.8 %collective-permute-done.14.refs_1_ = bf16[8,7168]{1,0:T(8,128)(2,1)S(1)} collective-permute-done((bf16[8,7168]{1,0:T(8,128)(2,1)S(1)}, bf16[8,7168]{1,0:T(8,128)(2,1)S(1)}, u32[]{:S(2)}, u32[]{:S(2)}) %collective-permute-start.14) | collective-permute-done | bytes 114720 | tf_op jit(solution)/shard_map/ppermute | solution.py:19
  41.4 0.8 %mix.1 = bf16[2,4,7168]{2,1,0:T(4,128)(2,1)} custom-call(f32[8,4]{1,0:T(8,128)S(1)} %bitcast.8, bf16[8,7168]{1,0:T(8,128)(2,1)S(1)} %add_rows.9.refs_0_, bf16[8,7168]{1,0:T(8,128)(2,1)S(1)} %collective-permute-done.14.refs_1_, bf16[8,7168]{1,0:T(8,128)(2,1)S(1)} %collective-permute-done.16.refs_2_, bf16[8,7168]{1,0:T(8,128)(2,1)S(1)} %collective-permute-done.18.refs_3_), custom_call_target="tpu_custom_call" | custom-call | tf_op jit(solution)/shard_map/mix/pallas_call | solution.py:148
  (19 shorter events, 0.3 us)
Async XLA Ops:
  0.0 14.3 %copy-start.3 = (bf16[2,4,7168]{2,1,0:T(4,128)(2,1)S(1)}, bf16[2,4,7168]{2,1,0:T(4,128)(2,1)}, u32[]{:S(2)}) copy-start(bf16[2,4,7168]{2,1,0:T(4,128)(2,1)} %refs_0_.2) | copy-start | bytes 344068
  0.0 10.0 %collective-permute-start = (bf16[2,4,7168]{2,1,0:T(4,128)(2,1)}, bf16[2,4,7168]{2,1,0:T(4,128)(2,1)S(1)}, u32[]{:S(2)}, u32[]{:S(2)}) collective-permute-start(bf16[2,4,7168]{2,1,0:T(4,128)(2,1)} %refs_0_.2), channel_id=1, source_target_pairs={{0,8},{1,9},{2,10},{3,11},{4,12},{5,13},{6,14},{7,15},{8,0},{9,1},... | collective-permute-start | bytes 344072 | tf_op jit(solution)/shard_map/ppermute | solution.py:19
  4.0 6.9 %collective-permute-start.1 = (bf16[2,4,7168]{2,1,0:T(4,128)(2,1)}, bf16[2,4,7168]{2,1,0:T(4,128)(2,1)S(1)}, u32[]{:S(2)}, u32[]{:S(2)}) collective-permute-start(bf16[2,4,7168]{2,1,0:T(4,128)(2,1)} %refs_0_.2), channel_id=1, source_target_pairs={{0,4},{1,5},{2,6},{3,7},{4,0},{5,1},{6,2},{7,3},{8,12},{9,13},{10,... | collective-permute-start | bytes 344072 | tf_op jit(solution)/shard_map/ppermute | solution.py:19
  5.6 8.8 %collective-permute-start.2 = (bf16[2,4,7168]{2,1,0:T(4,128)(2,1)}, bf16[2,4,7168]{2,1,0:T(4,128)(2,1)S(1)}, u32[]{:S(2)}, u32[]{:S(2)}) collective-permute-start(bf16[2,4,7168]{2,1,0:T(4,128)(2,1)} %refs_0_.2), channel_id=1, source_target_pairs={{0,2},{1,3},{2,0},{3,1},{4,6},{5,7},{6,4},{7,5},{8,10},{9,11},{10,... | collective-permute-start | bytes 344072 | tf_op jit(solution)/shard_map/ppermute | solution.py:19
  7.1 8.3 %collective-permute-start.3 = (bf16[2,4,7168]{2,1,0:T(4,128)(2,1)}, bf16[2,4,7168]{2,1,0:T(4,128)(2,1)S(1)}, u32[]{:S(2)}, u32[]{:S(2)}) collective-permute-start(bf16[2,4,7168]{2,1,0:T(4,128)(2,1)} %refs_0_.2), channel_id=1, source_target_pairs={{0,6},{1,7},{2,4},{3,5},{4,2},{5,3},{6,0},{7,1},{8,14},{9,15},{10,... | collective-permute-start | bytes 344072 | tf_op jit(solution)/shard_map/ppermute | solution.py:19
  7.5 10.4 %collective-permute-start.4 = (bf16[2,4,7168]{2,1,0:T(4,128)(2,1)}, bf16[2,4,7168]{2,1,0:T(4,128)(2,1)S(1)}, u32[]{:S(2)}, u32[]{:S(2)}) collective-permute-start(bf16[2,4,7168]{2,1,0:T(4,128)(2,1)} %refs_0_.2), channel_id=1, source_target_pairs={{0,14},{1,15},{2,12},{3,13},{4,10},{5,11},{6,8},{7,9},{8,6},{9,7},... | collective-permute-start | bytes 344072 | tf_op jit(solution)/shard_map/ppermute | solution.py:19
  10.9 9.2 %copy-start = (bf16[1,7168,256]{2,1,0:T(8,128)(2,1)S(1)}, bf16[1,7168,256]{2,1,0:T(8,128)(2,1)}, u32[]{:S(2)}) copy-start(bf16[1,7168,256]{2,1,0:T(8,128)(2,1)} %refs_0_.3) | copy-start | bytes 11010052
  10.9 9.2 %copy-start.1 = (bf16[1,7168,256]{2,1,0:T(8,128)(2,1)S(1)}, bf16[1,7168,256]{2,1,0:T(8,128)(2,1)}, u32[]{:S(2)}) copy-start(bf16[1,7168,256]{2,1,0:T(8,128)(2,1)} %refs_1_.1) | copy-start | bytes 11010052
  10.9 9.2 %copy-start.2 = (bf16[1,256,7168]{2,1,0:T(8,128)(2,1)S(1)}, bf16[1,256,7168]{2,1,0:T(8,128)(2,1)}, u32[]{:S(2)}) copy-start(bf16[1,256,7168]{2,1,0:T(8,128)(2,1)} %refs_2_.1) | copy-start | bytes 11010052
  11.0 7.4 %collective-permute-start.5 = (bf16[2,4,7168]{2,1,0:T(4,128)(2,1)S(1)}, bf16[2,4,7168]{2,1,0:T(4,128)(2,1)S(1)}, u32[]{:S(2)}, u32[]{:S(2)}) collective-permute-start(bf16[2,4,7168]{2,1,0:T(4,128)(2,1)S(1)} %pass_rows.1), channel_id=1, source_target_pairs={{0,2},{1,3},{2,0},{3,1},{4,6},{5,7},{6,4},{7,5},{8,10},{9,11},{10,... | collective-permute-start | bytes 344072 | tf_op jit(solution)/shard_map/ppermute | solution.py:19
  12.5 5.8 %collective-permute-start.6 = (bf16[2,4,7168]{2,1,0:T(4,128)(2,1)S(1)}, bf16[2,4,7168]{2,1,0:T(4,128)(2,1)S(1)}, u32[]{:S(2)}, u32[]{:S(2)}) collective-permute-start(bf16[2,4,7168]{2,1,0:T(4,128)(2,1)S(1)} %pass_rows.1), channel_id=1, source_target_pairs={{0,4},{1,5},{2,6},{3,7},{4,0},{5,1},{6,2},{7,3},{8,12},{9,13},{10,... | collective-permute-start | bytes 344072 | tf_op jit(solution)/shard_map/ppermute | solution.py:19
  14.5 5.6 %collective-permute-start.7 = (bf16[24,7168]{1,0:T(8,128)(2,1)S(1)}, bf16[24,7168]{1,0:T(8,128)(2,1)S(1)}, u32[]{:S(2)}, u32[]{:S(2)}) collective-permute-start(bf16[24,7168]{1,0:T(8,128)(2,1)S(1)} %pack_rows.3.refs_0_), channel_id=1, source_target_pairs={{0,1},{1,0},{2,3},{3,2},{4,5},{5,4},{6,7},{7,6},{8,9},{9,8},{10,11... | collective-permute-start | bytes 1032200 | tf_op jit(solution)/shard_map/ppermute | solution.py:19
  18.0 2.1 %collective-permute-start.8 = (bf16[24,7168]{1,0:T(8,128)(2,1)S(1)}, bf16[24,7168]{1,0:T(8,128)(2,1)S(1)}, u32[]{:S(2)}, u32[]{:S(2)}) collective-permute-start(bf16[24,7168]{1,0:T(8,128)(2,1)S(1)} %pack_rows.4.refs_1_), channel_id=1, source_target_pairs={{0,1},{1,0},{2,3},{3,2},{4,5},{5,4},{6,7},{7,6},{8,9},{9,8},{10,11... | collective-permute-start | bytes 1032200 | tf_op jit(solution)/shard_map/ppermute | solution.py:19
  18.4 1.7 %collective-permute-start.9 = (bf16[16,7168]{1,0:T(8,128)(2,1)S(1)}, bf16[16,7168]{1,0:T(8,128)(2,1)S(1)}, u32[]{:S(2)}, u32[]{:S(2)}) collective-permute-start(bf16[16,7168]{1,0:T(8,128)(2,1)S(1)} %pack_rows.5.refs_2_), channel_id=1, source_target_pairs={{0,1},{1,0},{2,3},{3,2},{4,5},{5,4},{6,7},{7,6},{8,9},{9,8},{10,11... | collective-permute-start | bytes 688136 | tf_op jit(solution)/shard_map/ppermute | solution.py:19
  21.9 1.6 %collective-permute-start.10 = (bf16[16,7168]{1,0:T(8,128)(2,1)S(1)}, bf16[16,7168]{1,0:T(8,128)(2,1)S(1)}, u32[]{:S(2)}, u32[]{:S(2)}) collective-permute-start(bf16[16,7168]{1,0:T(8,128)(2,1)S(1)} %get-tuple-element.15), channel_id=1, source_target_pairs={{0,1},{1,0},{2,3},{3,2},{4,5},{5,4},{6,7},{7,6},{8,9},{9,8},{10,11... | collective-permute-start | bytes 688136 | tf_op jit(solution)/shard_map/ppermute | solution.py:19
  23.4 2.1 %collective-permute-start.11 = (bf16[48,7168]{1,0:T(8,128)(2,1)S(1)}, bf16[48,7168]{1,0:T(8,128)(2,1)S(1)}, u32[]{:S(2)}, u32[]{:S(2)}) collective-permute-start(bf16[48,7168]{1,0:T(8,128)(2,1)S(1)} %get-tuple-element.17), channel_id=1, source_target_pairs={{0,1},{1,0},{2,3},{3,2},{4,5},{5,4},{6,7},{7,6},{8,9},{9,8},{10,11... | collective-permute-start | bytes 2064392 | tf_op jit(solution)/shard_map/ppermute | solution.py:19
  23.6 4.2 %copy-start.5 = (f32[2,4,2]{1,2,0:T(2,128)S(1)}, f32[2,4,2]{1,2,0:T(2,128)}, u32[]{:S(2)}) copy-start(f32[2,4,2]{1,2,0:T(2,128)} %param.8) | copy-start | bytes 196
  23.6 6.0 %collective-permute-start.17 = (bf16[8,7168]{1,0:T(8,128)(2,1)S(1)}, bf16[8,7168]{1,0:T(8,128)(2,1)S(1)}, u32[]{:S(2)}, u32[]{:S(2)}) collective-permute-start(bf16[8,7168]{1,0:T(8,128)(2,1)S(1)} %add_rows.14), channel_id=1, source_target_pairs={{0,2},{1,3},{2,0},{3,1},{4,6},{5,7},{6,4},{7,5},{8,10},{9,11},{10,... | collective-permute-start | bytes 344072 | tf_op jit(solution)/shard_map/ppermute | solution.py:19
  25.6 6.5 %collective-permute-start.15 = (bf16[8,7168]{1,0:T(8,128)(2,1)S(1)}, bf16[8,7168]{1,0:T(8,128)(2,1)S(1)}, u32[]{:S(2)}, u32[]{:S(2)}) collective-permute-start(bf16[8,7168]{1,0:T(8,128)(2,1)S(1)} %add_rows.12), channel_id=1, source_target_pairs={{0,2},{1,3},{2,0},{3,1},{4,6},{5,7},{6,4},{7,5},{8,10},{9,11},{10,... | collective-permute-start | bytes 344072 | tf_op jit(solution)/shard_map/ppermute | solution.py:19
  26.6 8.0 %collective-permute-start.13 = (bf16[8,7168]{1,0:T(8,128)(2,1)S(1)}, bf16[8,7168]{1,0:T(8,128)(2,1)S(1)}, u32[]{:S(2)}, u32[]{:S(2)}) collective-permute-start(bf16[8,7168]{1,0:T(8,128)(2,1)S(1)} %add_rows.10), channel_id=1, source_target_pairs={{0,2},{1,3},{2,0},{3,1},{4,6},{5,7},{6,4},{7,5},{8,10},{9,11},{10,... | collective-permute-start | bytes 344072 | tf_op jit(solution)/shard_map/ppermute | solution.py:19
  29.7 7.6 %copy-start.4 = (s32[2,4,2]{1,2,0:T(2,128)S(1)}, s32[2,4,2]{1,2,0:T(2,128)}, u32[]{:S(2)}) copy-start(s32[2,4,2]{1,2,0:T(2,128)} %param.7) | copy-start | bytes 196
  29.7 8.1 %collective-permute-start.18 = (bf16[8,7168]{1,0:T(8,128)(2,1)S(1)}, bf16[8,7168]{1,0:T(8,128)(2,1)S(1)}, u32[]{:S(2)}, u32[]{:S(2)}) collective-permute-start(bf16[8,7168]{1,0:T(8,128)(2,1)S(1)} %add_rows.15), channel_id=1, source_target_pairs={{0,8},{1,9},{2,10},{3,11},{4,12},{5,13},{6,14},{7,15},{8,0},{9,1},... | collective-permute-start | bytes 344072 | tf_op jit(solution)/shard_map/ppermute | solution.py:19
  31.0 6.3 %collective-permute-start.12 = (bf16[8,7168]{1,0:T(8,128)(2,1)S(1)}, bf16[8,7168]{1,0:T(8,128)(2,1)S(1)}, u32[]{:S(2)}, u32[]{:S(2)}) collective-permute-start(bf16[8,7168]{1,0:T(8,128)(2,1)S(1)} %add_rows.8), channel_id=1, source_target_pairs={{0,2},{1,3},{2,0},{3,1},{4,6},{5,7},{6,4},{7,5},{8,10},{9,11},{10,... | collective-permute-start | bytes 344072 | tf_op jit(solution)/shard_map/ppermute | solution.py:19
  32.1 7.5 %collective-permute-start.16 = (bf16[8,7168]{1,0:T(8,128)(2,1)S(1)}, bf16[8,7168]{1,0:T(8,128)(2,1)S(1)}, u32[]{:S(2)}, u32[]{:S(2)}) collective-permute-start(bf16[8,7168]{1,0:T(8,128)(2,1)S(1)} %add_rows.13), channel_id=1, source_target_pairs={{0,4},{1,5},{2,6},{3,7},{4,0},{5,1},{6,2},{7,3},{8,12},{9,13},{10,... | collective-permute-start | bytes 344072 | tf_op jit(solution)/shard_map/ppermute | solution.py:19
  34.6 6.8 %collective-permute-start.14 = (bf16[8,7168]{1,0:T(8,128)(2,1)S(1)}, bf16[8,7168]{1,0:T(8,128)(2,1)S(1)}, u32[]{:S(2)}, u32[]{:S(2)}) collective-permute-start(bf16[8,7168]{1,0:T(8,128)(2,1)S(1)} %add_rows.11), channel_id=1, source_target_pairs={{0,12},{1,13},{2,14},{3,15},{4,8},{5,9},{6,10},{7,11},{8,4},{9,5},... | collective-permute-start | bytes 344072 | tf_op jit(solution)/shard_map/ppermute | solution.py:19
